TPU v7x, 128 devices: a whole 4x4x4 slice. The times are simulated.
128 devices in a mesh: dx: 8 (over z, core), dy: 16 (over y, x).
Axes of the slice: x: 4, y: 4, z: 4, core: 2. Of those that a mesh axis runs over, the one named last changes fastest.
Arguments:
- orbitals: bfloat16 [128, 64, 4096], P(('dx', 'dy')), may hold values from -6 to 6
- offsets: int32 [128, 3], replicated, may hold values from 0 to 31
- pair_list: int32 [1024, 2], P(('dx', 'dy')), may hold values from 0 to 127, as said below
- pair_mask: int32 [1024], P(('dx', 'dy')), may hold values from 0 to 1, as said below
Outputs:
- exchange: float32 [128, 64, 4096], P(('dx', 'dy'))
Inputs may be any that keep to these rules, and one draw needn't show every extreme that they name: `pair_list`: in each spatial domain's block of 8 slots (domain index dx * 16 + dy owns orbitals 1 * that index onward), the first orbital belongs to that domain and the second to it or to one of the eight domains whose x and y domain indices differ by at most one, wrapping around. `pair_mask`: every domain uses at least one slot; in every draw some domain uses all 8.
All inputs are finite; a program needn't handle non-finite values.
Results may differ from a plain program's by a relative error of at most 0.0003.
Values may be sent and summed in bfloat16 or wider, within the bound.
No kernel may reach another device: no remote copies, remote signals or barrier semaphores. Data moves between devices by JAX's collectives and lax.ppermute only.
A program may use at most 64 MiB of HBM per device.

v0:
```python
import math

import jax
import jax.numpy as jnp
from jax import lax
from jax.sharding import PartitionSpec as P


def extended(value, sides, width):
    for axis, dim in sides:
        size, length = (lax.axis_size(axis), value.shape[dim])
        up = [(i, (i + 1) % size) for i in range(size)]
        down = [(j, i) for i, j in up]
        last = lax.slice_in_dim(value, length - width, length, axis=dim)
        leading = lax.slice_in_dim(value, 0, width, axis=dim)
        before = lax.ppermute(last, axis, up)
        after = lax.ppermute(leading, axis, down)
        value = jnp.concatenate([before, value, after], axis=dim)
    return value


def shifted(value, axis, steps):
    count = lax.axis_size(axis)
    pairs = [(source, (source + steps) % count) for source in range(count)]
    return lax.ppermute(value, axis, pairs)


def shift_box(field, sx, sy, sz):
    box = field.shape[0]
    flat = field.shape[1]
    padded = jnp.pad(field, ((box, box), (0, 0)))
    field = lax.dynamic_slice_in_dim(padded, box + sx, box, 0)
    padded = jnp.pad(field, ((0, 0), (flat, flat)))
    field = lax.dynamic_slice_in_dim(padded, flat + sy * box, flat, 1)
    padded = jnp.pad(field, ((0, 0), (box, box)))
    field = lax.dynamic_slice_in_dim(padded, box + sz, flat, 1)
    column = jnp.arange(flat, dtype=jnp.int32) % box + sz
    keep = (column >= 0) & (column < box)
    return jnp.where(keep[None, :], field, jnp.zeros_like(field))


def kernel_tiled(box):
    freq = jnp.arange(box, dtype=jnp.int32)
    freq = freq - box * (freq >= box // 2).astype(jnp.int32)
    wave = 2.0 * math.pi / box * freq.astype(jnp.float32)
    square = wave * wave
    inner = jnp.concatenate([square, square])
    total = square[:, None, None] + square[None, :, None] + inner[None, None, :]
    return 1.0 / (total + (8.0 * math.pi / box) ** 2)


def dft_tables(box):
    index = jnp.arange(box, dtype=jnp.int32)
    angle = 2.0 * math.pi / box * (index[:, None] * index[None, :] % box).astype(jnp.float32)
    return (jnp.cos(angle), jnp.sin(angle))


def swap_parts(block, box):
    return jnp.concatenate([block[..., box:], -block[..., :box]], axis=-1)


def poisson_solve(density, cosine, sine, kernel):
    box = density.shape[0]
    high = lax.Precision.HIGHEST
    forward_z = jnp.concatenate([cosine, -sine], axis=1)
    wave = jnp.dot(density.reshape(box * box, box), forward_z, precision=high).reshape(
        box, box, 2 * box
    )
    along = jnp.einsum("ky,xyw->xkw", cosine, wave, precision=high)
    across = jnp.einsum("ky,xyw->xkw", sine, wave, precision=high)
    wave = along + swap_parts(across, box)
    along = jnp.einsum("kx,xyw->kyw", cosine, wave, precision=high)
    across = jnp.einsum("kx,xyw->kyw", sine, wave, precision=high)
    wave = (along + swap_parts(across, box)) * kernel
    along = jnp.einsum("kx,xyw->kyw", cosine, wave, precision=high)
    across = jnp.einsum("kx,xyw->kyw", sine, wave, precision=high)
    wave = along - swap_parts(across, box)
    along = jnp.einsum("ky,xyw->xkw", cosine, wave, precision=high)
    across = jnp.einsum("ky,xyw->xkw", sine, wave, precision=high)
    wave = along - swap_parts(across, box)
    back_z = jnp.concatenate([cosine, -sine], axis=0)
    field = jnp.dot(wave.reshape(box * box, 2 * box), back_z, precision=high) / float(box**3)
    return field.reshape(box, box * box)


def body(orbitals, offsets, pair_list, pair_mask):
    orb_dev, box, flat = orbitals.shape
    count_x = lax.axis_size("dx")
    count_y = lax.axis_size("dy")
    place_x = lax.axis_index("dx")
    place_y = lax.axis_index("dy")
    base = (place_x * count_y + place_y) * orb_dev
    nearby = extended(orbitals[None, None], (("dx", 0), ("dy", 1)), 1)
    nearby = nearby.reshape(9 * orb_dev, box, flat)
    cosine, sine = dft_tables(box)
    kernel = kernel_tiled(box)

    def visit(slot, carry):
        own_total, outgoing = carry
        first = pair_list[slot, 0]
        second = pair_list[slot, 1]
        valid = pair_mask[slot].astype(jnp.float32)
        owner = second // orb_dev
        rel_x = (owner // count_y - place_x + 1) % count_x
        rel_y = (owner % count_y - place_y + 1) % count_y
        target = (rel_x * 3 + rel_y) * orb_dev + second % orb_dev
        local = first - base
        phi_first = lax.dynamic_index_in_dim(orbitals, local, 0, keepdims=False).astype(jnp.float32)
        phi_second = lax.dynamic_index_in_dim(nearby, target, 0, keepdims=False).astype(jnp.float32)
        move = offsets[first] - offsets[second]
        partner = shift_box(phi_second, move[0], move[1], move[2])
        density = phi_first * partner * valid
        potential = poisson_solve(density, cosine, sine, kernel)
        own_total = own_total.at[local].add(potential * partner)
        outgoing = outgoing.at[target].add(
            shift_box(potential * phi_first, -move[0], -move[1], -move[2])
        )
        return (own_total, outgoing)

    own_total = jnp.zeros((orb_dev, box, flat), jnp.float32)
    outgoing = jnp.zeros((9 * orb_dev, box, flat), jnp.float32)
    own_total, outgoing = lax.fori_loop(0, pair_list.shape[0], visit, (own_total, outgoing))
    outgoing = outgoing.reshape(3, 3, orb_dev, box, flat)
    arrived = outgoing[1, 1]
    for step, source in ((1, 2), (-1, 0)):
        arrived = arrived + shifted(outgoing[source, 1], "dx", step)
    for step, source in ((1, 2), (-1, 0)):
        arrived = arrived + shifted(outgoing[1, source], "dy", step)
    for step, source in ((1, 2), (-1, 0)):
        corners = shifted(outgoing[source, 0::2], "dx", step)
        for which, turn in ((0, -1), (1, 1)):
            arrived = arrived + shifted(corners[which], "dy", turn)
    return own_total + arrived


def solution(mesh):
    placed = (P(("dx", "dy"), None, None), P(), P(("dx", "dy"), None), P(("dx", "dy")))
    return jax.shard_map(
        body, mesh=mesh, in_specs=placed, out_specs=P(("dx", "dy"), None, None), check_vma=False
    )
```

profile of v0, /device:TPU:0, one launch (start us, length us, event | category | flops | bytes accessed | tf_op | source)
XLA Modules:
  0.0 711.9 jit_solution(12569094905583328268)
XLA Ops:
  0.0 3.6 collective-permute-start.1
  3.6 7.0 collective-permute-done.1
  10.6 3.0 collective-permute-done
  15.9 5.2 collective-permute-start.3
  21.6 29.6 %collective-permute-done.3 = bf16[3,1,1,64,4096]{4,3,2,1,0:T(8,128)(2,1)S(1)} collective-permute-done((bf16[3,1,1,64,4096]{4,3,2,1,0:T(8,128)(2,1)}, bf16[3,1,1,64,4096]{4,3,2,1,0:T(8,128)(2,1)S(1)}, u32[]{:S(2)}, u32[]{:S(2)}) %collective-permute-start.3) | collective-permute-done | bytes 1572896 | tf_op jit(solution)/shard_map/ppermute | solution.py:17
  51.2 5.5 collective-permute-done.2
  56.7 3.7 pad_maximum_fusion
  60.4 4.8 broadcast_in_dim.70
  65.2 554.2 %while.22 = (s32[]{:T(128)}, f32[1,64,4096]{2,1,0:T(8,128)}, f32[9,64,4096]{2,1,0:T(8,128)}, s32[8,2]{0,1:T(2,128)S(1)}, s32[]{:T(128)}, /*index=5*/bf16[1,64,40...) while((s32[]{:T(128)}, f32[1,64,4096]{2,1,0:T(8,128)}, ...), condition=%wide.region_3.4_spmd.clone.clone, body=%wide.region_0.3_spmd.clone.clone.sunk | while | flops 4038606848 | bytes 101293488 | solution.py:122
  115.3 2.6 maximum_add_fusion.3
  117.9 3.3 fusion.194
  122.1 3.9 fusion.196
  131.7 3.3 fusion.198
  135.9 3.8 maximum_subtract_fusion.5
  148.6 4.7 add_select_fusion.6
  184.0 3.3 fusion.194
  188.2 3.9 fusion.196
  197.8 3.3 fusion.198
  202.0 3.8 maximum_subtract_fusion.5
  214.7 4.6 add_select_fusion.6
  249.9 3.3 fusion.194
  254.1 3.9 fusion.196
  263.7 3.3 fusion.198
  267.9 3.8 maximum_subtract_fusion.5
  280.6 4.6 add_select_fusion.6
  315.9 3.3 fusion.194
  320.0 3.9 fusion.196
  327.0 2.6 maximum_subtract_fusion.4
  329.7 3.3 fusion.198
  333.9 3.8 maximum_subtract_fusion.5
  346.5 4.6 add_select_fusion.6
  381.8 3.3 fusion.194
  386.0 3.9 fusion.196
  392.9 2.6 maximum_subtract_fusion.4
  395.6 3.3 fusion.198
  399.8 3.8 maximum_subtract_fusion.5
  412.5 4.6 add_select_fusion.6
  447.7 3.3 fusion.194
  451.9 3.9 fusion.196
  458.9 2.6 maximum_subtract_fusion.4
  461.5 3.3 fusion.198
  465.7 3.8 maximum_subtract_fusion.5
  478.4 4.7 add_select_fusion.6
  513.8 3.3 fusion.194
  518.0 3.9 fusion.196
  524.9 2.6 maximum_subtract_fusion.4
  527.6 3.3 fusion.198
  531.8 3.8 maximum_subtract_fusion.5
  544.5 4.6 add_select_fusion.6
  579.7 3.3 fusion.194
  583.9 3.9 fusion.196
  590.9 2.6 maximum_subtract_fusion.4
  593.5 3.3 fusion.198
  597.7 3.8 maximum_subtract_fusion.5
  610.4 4.6 add_select_fusion.6
  622.0 4.0 collective-permute-start.11
  630.6 19.1 %collective-permute-done.8 = f32[2,1,64,4096]{3,2,1,0:T(8,128)S(1)} collective-permute-done((f32[2,1,64,4096]{3,2,1,0:T(8,128)S(1)}, f32[2,1,64,4096]{3,2,1,0:T(8,128)S(1)}, u32[]{:S(2)}, u32[]{:S(2)}) %collective-permute-start.8) | collective-permute-done | bytes 2097184 | tf_op jit(solution)/shard_map/ppermute | solution.py:25
  650.3 10.6 %collective-permute-done.4 = f32[1,64,4096]{2,1,0:T(8,128)S(1)} collective-permute-done((f32[1,64,4096]{2,1,0:T(8,128)S(1)}, f32[1,64,4096]{2,1,0:T(8,128)S(1)}, u32[]{:S(2)}, u32[]{:S(2)}) %collective-permute-start.4) | collective-permute-done | bytes 1048608 | tf_op jit(solution)/shard_map/ppermute | solution.py:25
  660.9 5.3 collective-permute-start.12
  666.3 9.6 %collective-permute-done.9 = f32[1,64,4096]{2,1,0:T(8,128)S(1)} collective-permute-done((f32[1,64,4096]{2,1,0:T(8,128)S(1)}, f32[1,64,4096]{2,1,0:T(8,128)S(1)}, u32[]{:S(2)}, u32[]{:S(2)}) %collective-permute-start.9) | collective-permute-done | bytes 1048608 | tf_op jit(solution)/shard_map/ppermute | solution.py:25
  675.9 14.4 %collective-permute-done.10 = f32[1,64,4096]{2,1,0:T(8,128)S(1)} collective-permute-done((f32[1,64,4096]{2,1,0:T(8,128)S(1)}, f32[1,64,4096]{2,1,0:T(8,128)S(1)}, u32[]{:S(2)}, u32[]{:S(2)}) %collective-permute-start.10) | collective-permute-done | bytes 1048608 | tf_op jit(solution)/shard_map/ppermute | solution.py:25
  690.4 7.6 %collective-permute-done.12 = f32[1,64,4096]{2,1,0:T(8,128)S(1)} collective-permute-done((f32[1,64,4096]{2,1,0:T(8,128)S(1)}, f32[1,64,4096]{2,1,0:T(8,128)S(1)}, u32[]{:S(2)}, u32[]{:S(2)}) %collective-permute-start.12) | collective-permute-done | bytes 1048608 | tf_op jit(solution)/shard_map/ppermute | solution.py:25
  698.0 10.8 %collective-permute-done.13 = f32[1,64,4096]{2,1,0:T(8,128)S(1)} collective-permute-done((f32[1,64,4096]{2,1,0:T(8,128)S(1)}, f32[1,64,4096]{2,1,0:T(8,128)S(1)}, u32[]{:S(2)}, u32[]{:S(2)}) %collective-permute-start.13) | collective-permute-done | bytes 1048608 | tf_op jit(solution)/shard_map/ppermute | solution.py:25
  708.8 2.9 fusion.109
  (286 shorter events, 271.6 us)
Async XLA Ops:
  0.0 10.6 %collective-permute-start.1 = (bf16[1,1,1,64,4096]{4,3,2,1,0:T(8,128)(2,1)}, bf16[1,1,1,64,4096]{4,3,2,1,0:T(8,128)(2,1)S(1)}, u32[]{:S(2)}, u32[]{:S(2)}) collective-permute-start(bf16[1,1,1,64,4096]{4,3,2,1,0:T(8,128)(2,1)} %bitcast), channel_id=1, source_target_pairs={{16,0},{32,16},{48,32},{64,48},{80,64},{96,80},{112,96},{0,112},{1... | collective-permute-start | bytes 1572872 | tf_op jit(solution)/shard_map/ppermute | solution.py:17
  3.6 10.0 %collective-permute-start = (bf16[1,1,1,64,4096]{4,3,2,1,0:T(8,128)(2,1)}, bf16[1,1,1,64,4096]{4,3,2,1,0:T(8,128)(2,1)S(1)}, u32[]{:S(2)}, u32[]{:S(2)}) collective-permute-start(bf16[1,1,1,64,4096]{4,3,2,1,0:T(8,128)(2,1)} %bitcast), channel_id=1, source_target_pairs={{0,16},{16,32},{32,48},{48,64},{64,80},{80,96},{96,112},{112,0},{1... | collective-permute-start | bytes 1572872 | tf_op jit(solution)/shard_map/ppermute | solution.py:16
  15.9 35.2 %collective-permute-start.3 = (bf16[3,1,1,64,4096]{4,3,2,1,0:T(8,128)(2,1)}, bf16[3,1,1,64,4096]{4,3,2,1,0:T(8,128)(2,1)S(1)}, u32[]{:S(2)}, u32[]{:S(2)}) collective-permute-start(bf16[3,1,1,64,4096]{4,3,2,1,0:T(8,128)(2,1)} %pad_maximum_fusion.1), channel_id=1, source_target_pairs={{1,0},{2,1},{3,2},{4,3},{5,4},{6,5},{7,6},{8,7},{9,8},{10,9},{11,1... | collective-permute-start | bytes 4718600 | tf_op jit(solution)/shard_map/ppermute | solution.py:17
  21.2 35.6 %collective-permute-start.2 = (bf16[3,1,1,64,4096]{4,3,2,1,0:T(8,128)(2,1)}, bf16[3,1,1,64,4096]{4,3,2,1,0:T(8,128)(2,1)}, u32[]{:S(2)}, u32[]{:S(2)}) collective-permute-start(bf16[3,1,1,64,4096]{4,3,2,1,0:T(8,128)(2,1)} %pad_maximum_fusion.1), channel_id=1, source_target_pairs={{0,1},{1,2},{2,3},{3,4},{4,5},{5,6},{6,7},{7,8},{8,9},{9,10},{10,1... | collective-permute-start | bytes 4718600 | tf_op jit(solution)/shard_map/ppermute | solution.py:16
  60.4 4.9 copy-start.3
  60.4 4.9 copy-start.4
  60.4 4.9 copy-start.5
  60.4 4.9 copy-start.6
  147.4 1.2 copy-start
  153.3 1.0 copy-start.1
  213.4 1.2 copy-start
  219.2 1.0 copy-start.1
  279.4 1.2 copy-start
  285.2 1.0 copy-start.1
  345.3 1.2 copy-start
  351.1 1.0 copy-start.1
  411.3 1.2 copy-start
  417.1 1.0 copy-start.1
  477.2 1.2 copy-start
  483.1 1.0 copy-start.1
  543.2 1.2 copy-start
  549.1 1.0 copy-start.1
  609.2 1.2 copy-start
  615.0 1.0 copy-start.1
  621.9 27.8 %collective-permute-start.8 = (f32[2,1,64,4096]{3,2,1,0:T(8,128)S(1)}, f32[2,1,64,4096]{3,2,1,0:T(8,128)S(1)}, u32[]{:S(2)}, u32[]{:S(2)}) collective-permute-start(f32[2,1,64,4096]{3,2,1,0:T(8,128)S(1)} %get-tuple-element.650), channel_id=1, source_target_pairs={{0,16},{16,32},{32,48},{48,64},{64,80},{80,96},{96,112},{112,0},{1... | collective-permute-start | bytes 6291464 | tf_op jit(solution)/shard_map/ppermute | solution.py:25
  622.0 27.9 %collective-permute-start.11 = (f32[2,1,64,4096]{3,2,1,0:T(8,128)S(1)}, f32[2,1,64,4096]{3,2,1,0:T(8,128)S(1)}, u32[]{:S(2)}, u32[]{:S(2)}) collective-permute-start(f32[2,1,64,4096]{3,2,1,0:T(8,128)S(1)} %get-tuple-element.651), channel_id=1, source_target_pairs={{0,112},{16,0},{32,16},{48,32},{64,48},{80,64},{96,80},{112,96},{1... | collective-permute-start | bytes 6291464 | tf_op jit(solution)/shard_map/ppermute | solution.py:25
  628.5 32.5 %collective-permute-start.4 = (f32[1,64,4096]{2,1,0:T(8,128)S(1)}, f32[1,64,4096]{2,1,0:T(8,128)S(1)}, u32[]{:S(2)}, u32[]{:S(2)}) collective-permute-start(f32[1,64,4096]{2,1,0:T(8,128)S(1)} %get-tuple-element.646), channel_id=1, source_target_pairs={{0,16},{16,32},{32,48},{48,64},{64,80},{80,96},{96,112},{112,0},{1... | collective-permute-start | bytes 3145736 | tf_op jit(solution)/shard_map/ppermute | solution.py:25
  628.5 32.4 %collective-permute-start.7 = (f32[1,64,4096]{2,1,0:T(8,128)S(1)}, f32[1,64,4096]{2,1,0:T(8,128)S(1)}, u32[]{:S(2)}, u32[]{:S(2)}) collective-permute-start(f32[1,64,4096]{2,1,0:T(8,128)S(1)} %get-tuple-element.647), channel_id=1, source_target_pairs={{0,15},{1,0},{2,1},{3,2},{4,3},{5,4},{6,5},{7,6},{8,7},{9,8},{10,9... | collective-permute-start | bytes 3145736 | tf_op jit(solution)/shard_map/ppermute | solution.py:25
  628.8 37.5 %collective-permute-start.6 = (f32[1,64,4096]{2,1,0:T(8,128)S(1)}, f32[1,64,4096]{2,1,0:T(8,128)S(1)}, u32[]{:S(2)}, u32[]{:S(2)}) collective-permute-start(f32[1,64,4096]{2,1,0:T(8,128)S(1)} %get-tuple-element.648), channel_id=1, source_target_pairs={{0,1},{1,2},{2,3},{3,4},{4,5},{5,6},{6,7},{7,8},{8,9},{9,10},{10,1... | collective-permute-start | bytes 3145736 | tf_op jit(solution)/shard_map/ppermute | solution.py:25
  649.7 16.6 %collective-permute-start.5 = (f32[1,64,4096]{2,1,0:T(8,128)S(1)}, f32[1,64,4096]{2,1,0:T(8,128)S(1)}, u32[]{:S(2)}, u32[]{:S(2)}) collective-permute-start(f32[1,64,4096]{2,1,0:T(8,128)S(1)} %get-tuple-element.649), channel_id=1, source_target_pairs={{0,112},{16,0},{32,16},{48,32},{64,48},{80,64},{96,80},{112,96},{1... | collective-permute-start | bytes 3145736 | tf_op jit(solution)/shard_map/ppermute | solution.py:25
  649.9 58.9 %copy-start.2 = (f32[1,64,4096]{2,1,0:T(8,128)S(1)}, f32[1,64,4096]{2,1,0:T(8,128)}, u32[]{:S(2)}) copy-start(f32[1,64,4096]{2,1,0:T(8,128)} %get-tuple-element.500) | copy-start | bytes 3145732
  649.9 26.0 %collective-permute-start.9 = (f32[1,64,4096]{2,1,0:T(8,128)S(1)}, f32[1,64,4096]{2,1,0:T(8,128)S(1)}, u32[]{:S(2)}, u32[]{:S(2)}) collective-permute-start(f32[1,64,4096]{2,1,0:T(8,128)S(1)} %get-tuple-element.652), channel_id=1, source_target_pairs={{0,15},{1,0},{2,1},{3,2},{4,3},{5,4},{6,5},{7,6},{8,7},{9,8},{10,9... | collective-permute-start | bytes 3145736 | tf_op jit(solution)/shard_map/ppermute | solution.py:25
  660.9 29.4 %collective-permute-start.10 = (f32[1,64,4096]{2,1,0:T(8,128)S(1)}, f32[1,64,4096]{2,1,0:T(8,128)S(1)}, u32[]{:S(2)}, u32[]{:S(2)}) collective-permute-start(f32[1,64,4096]{2,1,0:T(8,128)S(1)} %get-tuple-element.653), channel_id=1, source_target_pairs={{0,1},{1,2},{2,3},{3,4},{4,5},{5,6},{6,7},{7,8},{8,9},{9,10},{10,1... | collective-permute-start | bytes 3145736 | tf_op jit(solution)/shard_map/ppermute | solution.py:25
  660.9 37.1 %collective-permute-start.12 = (f32[1,64,4096]{2,1,0:T(8,128)S(1)}, f32[1,64,4096]{2,1,0:T(8,128)S(1)}, u32[]{:S(2)}, u32[]{:S(2)}) collective-permute-start(f32[1,64,4096]{2,1,0:T(8,128)S(1)} %get-tuple-element.654), channel_id=1, source_target_pairs={{0,15},{1,0},{2,1},{3,2},{4,3},{5,4},{6,5},{7,6},{8,7},{9,8},{10,9... | collective-permute-start | bytes 3145736 | tf_op jit(solution)/shard_map/ppermute | solution.py:25
  666.3 42.5 %collective-permute-start.13 = (f32[1,64,4096]{2,1,0:T(8,128)S(1)}, f32[1,64,4096]{2,1,0:T(8,128)S(1)}, u32[]{:S(2)}, u32[]{:S(2)}) collective-permute-start(f32[1,64,4096]{2,1,0:T(8,128)S(1)} %get-tuple-element.655), channel_id=1, source_target_pairs={{0,1},{1,2},{2,3},{3,4},{4,5},{5,6},{6,7},{7,8},{8,9},{9,10},{10,1... | collective-permute-start | bytes 3145736 | tf_op jit(solution)/shard_map/ppermute | solution.py:25
where the time goes:
time: 719 us; the launch traced here: 712 us
  matrix products  225 us (31%)
  loops' own time  125 us (17%)
  other arithmetic  121 us (17%)
  waiting for transfers between devices  117 us (16%)
  local copies, waits for them, and re-layouts  102 us (14%)
  starting transfers between devices  20.6 us (3%)
    another operation x1, loops' own time, body(): lax.fori_loop(0, pair_list.shape[0], visit, (own_total, outgoing))  125 us
    ppermute x10, waiting for transfers between devices, shifted(): return lax.ppermute(value, axis, pairs)  72.2 us
    dot_general x16, matrix products, poisson_solve(): along = jnp.einsum('kx,xyw->kyw', cosine, wave, precision=high)  52.7 us
    dot_general x16, matrix products, poisson_solve(): along = jnp.einsum('ky,xyw->xkw', cosine, wave, precision=high)  51.5 us
    dot_general x16, matrix products, poisson_solve(): across = jnp.einsum('ky,xyw->xkw', sine, wave, precision=high)  43.6 us
    dot_general x16, matrix products, poisson_solve(): across = jnp.einsum('kx,xyw->kyw', sine, wave, precision=high)  43.6 us
    scatter-add x8, other arithmetic, visit(): own_total = own_total.at[local].add(potential * partner)  36.9 us
    ppermute x2, waiting for transfers between devices, extended(): after = lax.ppermute(leading, axis, down)  36.6 us
  transfers between devices with their start and end apart: 14, of which 10 were waited for; matrix products, arithmetic and copies ran while one was open for 0% of the time, Pallas kernels for 0%

commit v1 on v0

v1 whole, which is shorter than its diff:
```python
import functools
import math

import jax
import jax.numpy as jnp
import numpy as np
import ml_dtypes
from jax import lax
from jax.experimental import pallas as pl
from jax.experimental.pallas import tpu as pltpu
from jax.sharding import PartitionSpec as P

BOX = 64
ROW = 96
GROUP = 8
F32 = jnp.float32
BF16 = jnp.bfloat16


def tables():
    n = np.arange(BOX)
    basis = np.zeros((BOX, BOX))
    basis[0] = 1.0
    for m in range(1, BOX // 2):
        basis[2 * m - 1] = math.sqrt(2.0) * np.cos(2.0 * np.pi * m * n / BOX)
        basis[2 * m] = math.sqrt(2.0) * np.sin(2.0 * np.pi * m * n / BOX)
    basis[BOX - 1] = (-1.0) ** n
    basis /= math.sqrt(BOX)

    def cut(value):
        high = value.astype(ml_dtypes.bfloat16)
        low = (value - high.astype(np.float64)).astype(ml_dtypes.bfloat16)
        return high, low

    def right(matrix):
        both = np.kron(np.eye(2), matrix)
        high, low = cut(both)
        half = np.concatenate([high, low], 1)
        return np.concatenate([half, half], 0)

    def left(matrix):
        high, low = cut(matrix)
        return np.concatenate([high, high, low], 1)

    square = (2.0 * np.pi / BOX * ((n + 1) // 2)) ** 2
    some = (2.0 * np.pi / BOX * np.arange(BOX // 2 + 1)) ** 2
    total = some[:, None, None] + square[None, :, None] + np.concatenate([square, square])[None, None, :]
    green = (1.0 / (total + (8.0 * np.pi / BOX) ** 2)).astype(np.float32)
    return right(basis.T), right(basis), left(basis), left(basis.T), green


def split(value):
    high = value.astype(BF16)
    return high, (value - high.astype(F32)).astype(BF16)


def dot(a, b):
    return jnp.dot(a, b, preferred_element_type=F32)


def stacked(first, second):
    return jnp.concatenate([first, second], axis=1)


def kernel(pairs, shift_ref, weight_ref, own_ref, *refs):
    near = refs[: 2 * pairs]
    wz, wzi, rf, ri, green, acc_in, out, held, own, mid = refs[2 * pairs :]
    lanes = 2 * BOX
    low = lax.broadcasted_iota(jnp.int32, (BOX, lanes), 1) < BOX

    row = lax.broadcasted_iota(jnp.int32, (4 * BOX, 4 * BOX), 0)
    col = lax.broadcasted_iota(jnp.int32, (4 * BOX, 4 * BOX), 1)
    row_half, col_half = row // lanes, (col // BOX) % 2
    same = (row_half == col_half) & ((row // BOX) % 2 == col // lanes)
    away = row % BOX - col % BOX

    for y in range(BOX + 1):
        held[pl.ds(y * ROW, ROW - BOX), :] = jnp.zeros((ROW - BOX, lanes), F32)
    held[pl.ds(BOX * ROW, ROW + 32), :] = jnp.zeros((ROW + 32, lanes), F32)

    def own_step(t, _):
        v = own_ref[:, pl.ds(pl.multiple_of(t * lanes, lanes), lanes)].astype(F32)
        r = pltpu.roll(v, BOX, 1)
        base = pl.multiple_of(t * lanes, lanes)
        own[pl.ds(base, BOX), :] = jnp.where(low, v, r)
        own[pl.ds(base + BOX, BOX), :] = jnp.where(low, r, v)
        return 0

    lax.fori_loop(0, BOX // 2, own_step, 0, unroll=4)

    for p in range(pairs):
        a_ref, b_ref = near[2 * p], near[2 * p + 1]
        sx = [shift_ref[3 * (2 * p + h)] for h in range(2)]
        sy = [shift_ref[3 * (2 * p + h) + 1] for h in range(2)]
        sz = [shift_ref[3 * (2 * p + h) + 2] for h in range(2)]
        weight = [weight_ref[2 * p + h] for h in range(2)]

        def solve():
            want = jnp.where(col_half == 0, sz[0], sz[1])
            pick = jnp.where(same & (away == want), 1.0, 0.0).astype(BF16)

            def load_step(t, _):
                at = pl.ds(pl.multiple_of(t * lanes, lanes), lanes)
                v = dot(stacked(a_ref[:, at], b_ref[:, at]), pick)
                base = t * (2 * ROW) + (ROW - BOX)
                held[pl.ds(pl.multiple_of(base, 8), BOX), :] = v[:, :lanes]
                held[pl.ds(pl.multiple_of(base + ROW, 8), BOX), :] = v[:, lanes:]
                return 0

            lax.fori_loop(0, BOX // 2, load_step, 0, unroll=4)

            def partner(y):
                parts = []
                for h in range(2):
                    from_y = y + sy[h]
                    block = jnp.where((from_y >= 0) & (from_y < BOX), from_y, BOX)
                    parts.append(held[pl.ds(block * ROW + (ROW - BOX) + sx[h], BOX), :])
                return jnp.where(low, parts[0], parts[1])

            def forward(i, _):
                rows = []
                for j in range(GROUP):
                    y = i * GROUP + j
                    mine = own[pl.ds(pl.multiple_of(y * BOX, BOX), BOX), :]
                    rows.append(stacked(*split(partner(y) * mine)))
                wave = dot(jnp.concatenate(rows, 0), wz[...])
                high, rest = split(wave[:, :lanes] + wave[:, lanes:])
                for j in range(0, GROUP, 2):
                    at = j * BOX
                    h = stacked(high[at : at + BOX], high[at + BOX : at + 2 * BOX])
                    l = stacked(rest[at : at + BOX], rest[at + BOX : at + 2 * BOX])
                    u = dot(rf[...], jnp.concatenate([h, l, h], 0))
                    y = i * GROUP + j
                    mid[pl.ds(y, BOX, stride=BOX), :] = u[:, :lanes]
                    mid[pl.ds(y + 1, BOX, stride=BOX), :] = u[:, lanes:]
                return 0

            lax.fori_loop(0, BOX // GROUP, forward, 0)

            def middle(i, _):
                for j in range(0, GROUP, 2):
                    k = i * GROUP + j
                    base = pl.multiple_of(k * BOX, BOX)
                    v = stacked(mid[pl.ds(base, BOX), :], mid[pl.ds(base + BOX, BOX), :])
                    h, l = split(v)
                    s = dot(rf[...], jnp.concatenate([h, l, h], 0))
                    s = s * stacked(green[(k + 1) // 2], green[(k + 2) // 2])
                    h, l = split(s)
                    v = dot(ri[...], jnp.concatenate([h, l, h], 0))
                    mid[pl.ds(base, BOX), :] = v[:, :lanes]
                    mid[pl.ds(base + BOX, BOX), :] = v[:, lanes:]
                return 0

            lax.fori_loop(0, BOX // GROUP, middle, 0)

            def backward(i, _):
                rows = []
                for j in range(0, GROUP, 2):
                    y = i * GROUP + j
                    v = stacked(mid[pl.ds(y, BOX, stride=BOX), :], mid[pl.ds(y + 1, BOX, stride=BOX), :])
                    h, l = split(v)
                    u = dot(ri[...], jnp.concatenate([h, l, h], 0))
                    h, l = split(u)
                    rows.append(stacked(h[:, :lanes], l[:, :lanes]))
                    rows.append(stacked(h[:, lanes:], l[:, lanes:]))
                wave = dot(jnp.concatenate(rows, 0), wzi[...])
                field = wave[:, :lanes] + wave[:, lanes:]
                scale = jnp.where(low, weight[0], weight[1])
                for j in range(0, GROUP, 2):
                    y = i * GROUP + j
                    parts = []
                    for k in range(2):
                        v = field[(j + k) * BOX : (j + k + 1) * BOX] * (partner(y + k) * scale)
                        parts.append(v + pltpu.roll(v, BOX, 1))
                    at = pl.ds(pl.multiple_of(y * BOX, lanes), lanes)
                    source = acc_in if p == 0 else out
                    out[:, at] = source[:, at] + jnp.where(low, parts[0], parts[1])
                return 0

            lax.fori_loop(0, BOX // GROUP, backward, 0)

        solve()


def exchange_terms(own, near, shifts, weights, acc):
    pairs = len(near) // 2
    smem = pl.BlockSpec(memory_space=pltpu.SMEM)
    vmem = pl.BlockSpec(memory_space=pltpu.VMEM)
    wz, wzi, rf, ri, green = tables()
    return pl.pallas_call(
        functools.partial(kernel, pairs),
        out_shape=jax.ShapeDtypeStruct((BOX, BOX * BOX), F32),
        in_specs=[smem, smem] + [vmem] * (len(near) + 7),
        out_specs=vmem,
        scratch_shapes=[
            pltpu.VMEM(((BOX + 1) * ROW + 32, 2 * BOX), F32),
            pltpu.VMEM((BOX * BOX, 2 * BOX), F32),
            pltpu.VMEM((BOX * BOX, 2 * BOX), F32),
        ],
        compiler_params=pltpu.CompilerParams(vmem_limit_bytes=48 * 1024 * 1024),
    )(shifts, weights, own, *near, wz, wzi, rf, ri, green, acc)


def shifted(value, axis, steps):
    count = lax.axis_size(axis)
    return lax.ppermute(value, axis, [(i, (i + steps) % count) for i in range(count)])


def body(orbitals, offsets, pair_list, pair_mask):
    count_x, count_y = lax.axis_size("dx"), lax.axis_size("dy")
    place_x, place_y = lax.axis_index("dx"), lax.axis_index("dy")
    mine = place_x * count_y + place_y
    own = orbitals[0]

    owner = pair_list[:, 1]
    rel_x = (owner // count_y - place_x + 1) % count_x
    rel_y = (owner % count_y - place_y + 1) % count_y
    target = rel_x * 3 + rel_y
    used = jnp.where(target[:, None] == jnp.arange(9)[None, :], pair_mask[:, None], 0).sum(0)
    every = lax.all_gather(used, ("dx", "dy"))

    def near(i, j):
        return (place_x + i) % count_x * count_y + (place_y + j) % count_y

    def terms(places, boxes, acc, counts):
        ids = [near(i, j) for i, j in places]
        moves = jnp.concatenate([offsets[mine] - offsets[n] for n in ids])
        return exchange_terms(own, boxes, moves, counts.astype(F32), acc)

    def counts(places):
        return jnp.stack(
            [used[(i + 1) * 3 + j + 1] + every[near(i, j), (1 - i) * 3 + 1 - j] for i, j in places]
        )

    y_up, y_down = shifted(own, "dy", -1), shifted(own, "dy", 1)
    x_up, x_down = shifted(own, "dx", -1), shifted(own, "dx", 1)
    acc = jnp.zeros(own.shape, F32)
    acc = terms([(0, 0)] * 2, [own, own], acc, jnp.stack([used[4], used[4]]))
    places = [(1, 0), (-1, 0)]
    acc = terms(places, [x_up, x_down], acc, counts(places))
    places = [(0, 1), (0, -1)]
    acc = terms(places, [y_up, y_down], acc, counts(places))
    corners = [shifted(y_up, "dx", -1), shifted(y_down, "dx", 1), shifted(y_up, "dx", 1), shifted(y_down, "dx", -1)]
    places = [(1, 1), (-1, -1), (-1, 1), (1, -1)]
    acc = terms(places, corners, acc, counts(places))
    return acc[None]


def solution(mesh):
    placed = (P(("dx", "dy"), None, None), P(), P(("dx", "dy"), None), P(("dx", "dy")))
    return jax.shard_map(
        body, mesh=mesh, in_specs=placed, out_specs=P(("dx", "dy"), None, None), check_vma=False
    )
```

time: 719 us -> 173 us (0.24)
  matrix products: 225 us -> 0 us
  loops' own time: 125 us -> 0 us
  waiting for transfers between devices: 117 us -> 0.02 us
  other arithmetic: 121 us -> 4.1 us
  local copies, waits for them, and re-layouts: 102 us -> 3.19 us
  Pallas kernels: 0 us -> 72.5 us
  blocking collectives: 0 us -> 68.8 us
  between operations: 0.31 us -> 10.1 us
    dot_general x80 -> x0, matrix products: 225 us -> none  [the longest x16 52.7 us: poisson_solve(): along = jnp.einsum('kx,xyw->kyw', cosine, wave, precision=high)]
    another operation x1 -> x0, loops' own time: 125 us -> none  [body(): lax.fori_loop(0, pair_list.shape[0], visit, (own_total, outgoing))]
    ppermute x14 -> x8, waiting for transfers between devices: 117 us -> 0.02 us  [shifted(): lax.ppermute(value, axis, [(i, (i + steps) % count) for i in range(count)])]
    pallas_call x0 -> x4, Pallas kernels: none -> 72.5 us  [exchange_terms(): pl.pallas_call(functools.partial(kernel, pairs), out_shape=jax.ShapeDtype...]
    unnamed x0 -> x1, blocking collectives: none -> 68.8 us
    scatter-add x8 -> x0, other arithmetic: 36.9 us -> none  [visit(): own_total = own_total.at[local].add(potential * partner)]
    mul x17 -> x0, other arithmetic: 28.1 us -> none  [the longest x8 19 us: visit(): density = phi_first * partner * valid]
    slice x32 -> x0, other arithmetic: 27.3 us -> none  [swap_parts(): return jnp.concatenate([block[..., box:], -block[..., :box]], axis=-1)]
  transfers between devices with their start and end apart: 14 -> 8, of which waited for: 10 -> 0; matrix products, arithmetic and copies ran while one was open for 0% -> 4% of each run, Pallas kernels for 0% -> 25%
where the time goes in v1:
time: 173 us; the launch traced here: 172 us
  Pallas kernels  72.5 us (42%)
  blocking collectives  68.8 us (40%)
  starting transfers between devices  13.6 us (8%)
  between operations  10.1 us (6%)
  other arithmetic  4.1 us (2%)
  local copies, waits for them, and re-layouts  3.19 us (2%)
    pallas_call x4, Pallas kernels, exchange_terms(): pl.pallas_call(functools.partial(kernel, pairs), out_shape=jax.ShapeDtype...  72.5 us
    unnamed x1, blocking collectives  68.8 us
    ppermute x8, starting transfers between devices, shifted(): lax.ppermute(value, axis, [(i, (i + steps) % count) for i in range(count)])  13.6 us
  transfers between devices with their start and end apart: 8, of which 0 were waited for; matrix products, arithmetic and copies ran while one was open for 4% of the time, Pallas kernels for 25%

profile of v1, /device:TPU:0, one launch (start us, length us, event | category | flops | bytes accessed | tf_op | source)
XLA Modules:
  0.0 172.4 jit_solution(10827539920844886124)
XLA Ops:
  0.0 0.0 copy-start.3
  0.0 0.0 copy-start.4
  0.0 0.0 copy-start.5
  0.0 0.0 copy-start.6
  0.0 0.0 copy-start
  0.0 3.6 %collective-permute-start.6 = (bf16[64,4096]{1,0:T(8,128)(2,1)}, bf16[64,4096]{1,0:T(8,128)(2,1)S(1)}, u32[]{:S(2)}, u32[]{:S(2)}) collective-permute-start(bf16[64,4096]{1,0:T(8,128)(2,1)} %bitcast.28), channel_id=1, source_target_pairs={{0,112},{16,0},{32,16},{48,32},{64,48},{80,64},{96,80},{112,96},{1... | collective-permute-start | bytes 1572872 | tf_op jit(solution)/shard_map/ppermute | solution.py:206
  3.6 0.0 collective-permute-start.7
  3.6 5.2 %collective-permute-start = (bf16[64,4096]{1,0:T(8,128)(2,1)}, bf16[64,4096]{1,0:T(8,128)(2,1)S(1)}, u32[]{:S(2)}, u32[]{:S(2)}) collective-permute-start(bf16[64,4096]{1,0:T(8,128)(2,1)} %bitcast.30), channel_id=1, source_target_pairs={{0,15},{1,0},{2,1},{3,2},{4,3},{5,4},{6,5},{7,6},{8,7},{9,8},{10,9... | collective-permute-start | bytes 1572872 | tf_op jit(solution)/shard_map/ppermute | solution.py:206
  8.8 0.0 collective-permute-start.2
  8.8 0.7 fusion.24
  9.5 0.7 select_reduce_fusion
  10.3 0.3 dynamic-update-slice
  10.5 68.8 %all-reduce = s32[1152]{0:T(1024)S(1)} all-reduce(s32[1152]{0:T(1024)S(1)} %dynamic-update-slice), channel_id=2, replica_groups=mesh['dx'=8,'dy'=16] {'dx','dy'}, use_global_device_ids=true, to_apply=%add | all-reduce | flops 1152 | bytes 9216
  79.3 0.2 reshape.10
  79.6 0.7 constant_dynamic-slice_fusion.17
  80.3 0.7 fusion.25
  90.9 1.4 fusion.17
  92.3 0.1 pad_add_fusion.3.shift_ref
  92.4 0.7 add_convert_fusion.3.weight_ref
  93.1 0.1 broadcast_in_dim.23.refs_7_
  93.2 0.0 copy-done.3
  93.2 0.0 copy-done.4
  93.2 0.0 copy-done.5
  93.2 0.0 copy-done.6
  93.2 0.0 copy-done
  93.2 0.0 copy-start.1
  93.3 1.2 copy-done.1
  94.5 0.0 copy-start.2
  94.5 14.5 %shard_map.226.refs_7_ = f32[64,4096]{1,0:T(8,128)S(1)} custom-call(s32[6]{0:T(128)S(1)} %pad_add_fusion.3.shift_ref, f32[2]{0:T(128)S(1)} %add_convert_fusion.3.weight_ref, bf16[64,4096]{1,0:T(8,128)(2,1)S(1)} %bitcast.32, bf16[64,4096]{1,0:T(8,128)(2,1)S(1)} %bitcast.33, bf16[64,4096]{1,0:T(8,128)(2,1)S(1)} %bitcast.34, bf16[256,256]{1,0:T(8,128)(2,1)S(1)} %copy-done.3, ...), custom_call_target="tpu_custom_call" | custom-call | tf_op jit(solution)/shard_map/pallas_call | solution.py:190
  109.0 0.1 add_convert_fusion.2.weight_ref
  109.1 0.0 collective-permute-done.refs_0_
  109.1 1.8 %collective-permute-start.1 = (bf16[64,4096]{1,0:T(8,128)(2,1)S(1)}, bf16[64,4096]{1,0:T(8,128)(2,1)S(1)}, u32[]{:S(2)}, u32[]{:S(2)}) collective-permute-start(bf16[64,4096]{1,0:T(8,128)(2,1)S(1)} %collective-permute-done.refs_0_), channel_id=1, source_target_pairs={{0,112},{16,0},{32,16},{48,32},{64,48},{80,64},{96,80},{112,96},{1... | collective-permute-start | bytes 1572872 | tf_op jit(solution)/shard_map/ppermute | solution.py:206
  111.0 0.0 collective-permute-start.4
  111.0 0.0 collective-permute-done.2.refs_1_
  111.0 0.0 collective-permute-start.3
  111.0 0.0 collective-permute-done.6.refs_0_
  111.0 3.0 %collective-permute-start.5 = (bf16[64,4096]{1,0:T(8,128)(2,1)S(1)}, bf16[64,4096]{1,0:T(8,128)(2,1)S(1)}, u32[]{:S(2)}, u32[]{:S(2)}) collective-permute-start(bf16[64,4096]{1,0:T(8,128)(2,1)S(1)} %collective-permute-done.2.refs_1_), channel_id=1, source_target_pairs={{0,112},{16,0},{32,16},{48,32},{64,48},{80,64},{96,80},{112,96},{1... | collective-permute-start | bytes 1572872 | tf_op jit(solution)/shard_map/ppermute | solution.py:206
  113.9 0.1 pad_add_fusion.2.shift_ref
  114.0 0.1 add_convert_fusion.1.weight_ref
  114.1 0.1 pad_add_fusion.1.shift_ref
  114.2 0.1 add_convert_fusion.weight_ref
  114.3 0.1 pad_add_fusion.shift_ref
  114.3 0.0 collective-permute-done.7.refs_1_
  114.3 0.0 copy-done.2
  114.3 14.6 %shard_map.227.refs_7_ = f32[64,4096]{1,0:T(8,128)S(1)} custom-call(s32[6]{0:T(128)S(1)} %pad_add_fusion.2.shift_ref, f32[2]{0:T(128)S(1)} %add_convert_fusion.2.weight_ref, bf16[64,4096]{1,0:T(8,128)(2,1)S(1)} %bitcast.35, bf16[64,4096]{1,0:T(8,128)(2,1)S(1)} %collective-permute-done.6.refs_0_, bf16[64,4096]{1,0:T(8,128)(2,1)S(1)} %collective-permute-done.7.refs_1_, ...), custom_call_target="tpu_custom_call" | custom-call | tf_op jit(solution)/shard_map/pallas_call | solution.py:190
  128.9 14.6 %shard_map.228.refs_9_ = f32[64,4096]{1,0:T(8,128)S(1)} custom-call(s32[6]{0:T(128)S(1)} %pad_add_fusion.1.shift_ref, f32[2]{0:T(128)S(1)} %add_convert_fusion.1.weight_ref, bf16[64,4096]{1,0:T(8,128)(2,1)S(1)} %bitcast.36, bf16[64,4096]{1,0:T(8,128)(2,1)S(1)} %collective-permute-done.refs_0_, bf16[64,4096]{1,0:T(8,128)(2,1)S(1)} %collective-permute-done.2.refs_1_, ...), custom_call_target="tpu_custom_call" | custom-call | tf_op jit(solution)/shard_map/pallas_call | solution.py:190
  143.5 0.0 collective-permute-done.1.refs_0_
  143.5 0.0 collective-permute-done.3.refs_1_
  143.6 0.0 collective-permute-done.4.refs_2_
  143.6 0.0 collective-permute-done.5.refs_3_
  143.6 28.8 %shard_map.229 = f32[64,4096]{1,0:T(8,128)} custom-call(s32[12]{0:T(128)S(1)} %pad_add_fusion.shift_ref, f32[4]{0:T(128)S(1)} %add_convert_fusion.weight_ref, bf16[64,4096]{1,0:T(8,128)(2,1)S(1)} %bitcast.37, bf16[64,4096]{1,0:T(8,128)(2,1)S(1)} %collective-permute-done.1.refs_0_, bf16[64,4096]{1,0:T(8,128)(2,1)S(1)} %collective-permute-done.3.refs_1_, ...), custom_call_target="tpu_custom_call" | custom-call | tf_op jit(solution)/shard_map/pallas_call | solution.py:190
  (1 shorter events, 0.0 us)
Async XLA Ops:
  0.0 93.2 %copy-start.3 = (bf16[256,256]{1,0:T(8,128)(2,1)S(1)}, bf16[256,256]{1,0:T(8,128)(2,1)}, u32[]{:S(2)}) copy-start(bf16[256,256]{1,0:T(8,128)(2,1)} %constant.167.clone.refs_2_.refs_4_) | copy-start | bytes 393220
  0.0 93.2 %copy-start.4 = (bf16[256,256]{1,0:T(8,128)(2,1)S(1)}, bf16[256,256]{1,0:T(8,128)(2,1)}, u32[]{:S(2)}) copy-start(bf16[256,256]{1,0:T(8,128)(2,1)} %constant.168.clone.refs_3_.refs_5_) | copy-start | bytes 393220
  0.0 93.2 %copy-start.5 = (bf16[64,192]{1,0:T(8,128)(2,1)S(1)}, bf16[64,192]{1,0:T(8,128)(2,1)}, u32[]{:S(2)}) copy-start(bf16[64,192]{1,0:T(8,128)(2,1)} %constant.169.clone.refs_4_.refs_6_) | copy-start | bytes 73732
  0.0 93.2 %copy-start.6 = (bf16[64,192]{1,0:T(8,128)(2,1)S(1)}, bf16[64,192]{1,0:T(8,128)(2,1)}, u32[]{:S(2)}) copy-start(bf16[64,192]{1,0:T(8,128)(2,1)} %constant.170.clone.refs_5_.refs_7_) | copy-start | bytes 73732
  0.0 93.2 %copy-start = (bf16[1,64,4096]{2,1,0:T(8,128)(2,1)S(1)}, bf16[1,64,4096]{2,1,0:T(8,128)(2,1)}, u32[]{:S(2)}) copy-start(bf16[1,64,4096]{2,1,0:T(8,128)(2,1)} %param.24) | copy-start | bytes 1572868
  0.0 111.0 %collective-permute-start.6 = (bf16[64,4096]{1,0:T(8,128)(2,1)}, bf16[64,4096]{1,0:T(8,128)(2,1)S(1)}, u32[]{:S(2)}, u32[]{:S(2)}) collective-permute-start(bf16[64,4096]{1,0:T(8,128)(2,1)} %bitcast.28), channel_id=1, source_target_pairs={{0,112},{16,0},{32,16},{48,32},{64,48},{80,64},{96,80},{112,96},{1... | collective-permute-start | bytes 1572872 | tf_op jit(solution)/shard_map/ppermute | solution.py:206
  3.6 110.7 %collective-permute-start.7 = (bf16[64,4096]{1,0:T(8,128)(2,1)}, bf16[64,4096]{1,0:T(8,128)(2,1)S(1)}, u32[]{:S(2)}, u32[]{:S(2)}) collective-permute-start(bf16[64,4096]{1,0:T(8,128)(2,1)} %bitcast.29), channel_id=1, source_target_pairs={{0,16},{16,32},{32,48},{48,64},{64,80},{80,96},{96,112},{112,0},{1... | collective-permute-start | bytes 1572872 | tf_op jit(solution)/shard_map/ppermute | solution.py:206
  3.6 105.5 %collective-permute-start = (bf16[64,4096]{1,0:T(8,128)(2,1)}, bf16[64,4096]{1,0:T(8,128)(2,1)S(1)}, u32[]{:S(2)}, u32[]{:S(2)}) collective-permute-start(bf16[64,4096]{1,0:T(8,128)(2,1)} %bitcast.30), channel_id=1, source_target_pairs={{0,15},{1,0},{2,1},{3,2},{4,3},{5,4},{6,5},{7,6},{8,7},{9,8},{10,9... | collective-permute-start | bytes 1572872 | tf_op jit(solution)/shard_map/ppermute | solution.py:206
  8.8 102.1 %collective-permute-start.2 = (bf16[64,4096]{1,0:T(8,128)(2,1)}, bf16[64,4096]{1,0:T(8,128)(2,1)S(1)}, u32[]{:S(2)}, u32[]{:S(2)}) collective-permute-start(bf16[64,4096]{1,0:T(8,128)(2,1)} %bitcast.31), channel_id=1, source_target_pairs={{0,1},{1,2},{2,3},{3,4},{4,5},{5,6},{6,7},{7,8},{8,9},{9,10},{10,1... | collective-permute-start | bytes 1572872 | tf_op jit(solution)/shard_map/ppermute | solution.py:206
  93.2 1.2 copy-start.1
  94.5 19.8 %copy-start.2 = (f32[33,64,128]{2,1,0:T(8,128)S(1)}, f32[33,64,128]{2,1,0:T(8,128)}, u32[]{:S(2)}) copy-start(f32[33,64,128]{2,1,0:T(8,128)} %constant.171.clone.refs_6_.refs_8_) | copy-start | bytes 3244036
  109.1 34.4 %collective-permute-start.1 = (bf16[64,4096]{1,0:T(8,128)(2,1)S(1)}, bf16[64,4096]{1,0:T(8,128)(2,1)S(1)}, u32[]{:S(2)}, u32[]{:S(2)}) collective-permute-start(bf16[64,4096]{1,0:T(8,128)(2,1)S(1)} %collective-permute-done.refs_0_), channel_id=1, source_target_pairs={{0,112},{16,0},{32,16},{48,32},{64,48},{80,64},{96,80},{112,96},{1... | collective-permute-start | bytes 1572872 | tf_op jit(solution)/shard_map/ppermute | solution.py:206
  111.0 32.6 %collective-permute-start.4 = (bf16[64,4096]{1,0:T(8,128)(2,1)S(1)}, bf16[64,4096]{1,0:T(8,128)(2,1)S(1)}, u32[]{:S(2)}, u32[]{:S(2)}) collective-permute-start(bf16[64,4096]{1,0:T(8,128)(2,1)S(1)} %collective-permute-done.refs_0_), channel_id=1, source_target_pairs={{0,16},{16,32},{32,48},{48,64},{64,80},{80,96},{96,112},{112,0},{1... | collective-permute-start | bytes 1572872 | tf_op jit(solution)/shard_map/ppermute | solution.py:206
  111.0 32.6 %collective-permute-start.3 = (bf16[64,4096]{1,0:T(8,128)(2,1)S(1)}, bf16[64,4096]{1,0:T(8,128)(2,1)S(1)}, u32[]{:S(2)}, u32[]{:S(2)}) collective-permute-start(bf16[64,4096]{1,0:T(8,128)(2,1)S(1)} %collective-permute-done.2.refs_1_), channel_id=1, source_target_pairs={{0,16},{16,32},{32,48},{48,64},{64,80},{80,96},{96,112},{112,0},{1... | collective-permute-start | bytes 1572872 | tf_op jit(solution)/shard_map/ppermute | solution.py:206
  111.0 32.6 %collective-permute-start.5 = (bf16[64,4096]{1,0:T(8,128)(2,1)S(1)}, bf16[64,4096]{1,0:T(8,128)(2,1)S(1)}, u32[]{:S(2)}, u32[]{:S(2)}) collective-permute-start(bf16[64,4096]{1,0:T(8,128)(2,1)S(1)} %collective-permute-done.2.refs_1_), channel_id=1, source_target_pairs={{0,112},{16,0},{32,16},{48,32},{64,48},{80,64},{96,80},{112,96},{1... | collective-permute-start | bytes 1572872 | tf_op jit(solution)/shard_map/ppermute | solution.py:206

commit v2 on v1

v2 whole, which is shorter than its diff:
```python
import functools
import math

import jax
import jax.numpy as jnp
import numpy as np
import ml_dtypes
from jax import lax
from jax.experimental import pallas as pl
from jax.experimental.pallas import tpu as pltpu
from jax.sharding import PartitionSpec as P

BOX = 64
ROW = 96
FACTS = 5
MROW = 72
CHUNK = 16
THICK = 8
F32 = jnp.float32
BF16 = jnp.bfloat16


def tables():
    n = np.arange(BOX)
    basis = np.zeros((BOX, BOX))
    basis[0] = 1.0
    for m in range(1, BOX // 2):
        basis[2 * m - 1] = math.sqrt(2.0) * np.cos(2.0 * np.pi * m * n / BOX)
        basis[2 * m] = math.sqrt(2.0) * np.sin(2.0 * np.pi * m * n / BOX)
    basis[BOX - 1] = (-1.0) ** n
    basis /= math.sqrt(BOX)

    def cut(value):
        high = value.astype(ml_dtypes.bfloat16)
        low = (value - high.astype(np.float64)).astype(ml_dtypes.bfloat16)
        return high, low

    def right(matrix):
        both = np.kron(np.eye(2), matrix)
        high, low = cut(both)
        half = np.concatenate([high, low], 1)
        return np.concatenate([half, half], 0)

    def left(matrix):
        high, low = cut(matrix)
        return np.concatenate([high, high, low], 1)

    square = (2.0 * np.pi / BOX * ((n + 1) // 2)) ** 2
    some = (2.0 * np.pi / BOX * np.arange(BOX // 2 + 1)) ** 2
    total = some[:, None, None] + square[None, :, None] + np.concatenate([square, square])[None, None, :]
    green = (1.0 / (total + (8.0 * np.pi / BOX) ** 2)).astype(np.float32)
    return right(basis.T), right(basis), left(basis), left(basis.T), green


def split(value):
    high = value.astype(BF16)
    return high, (value - high.astype(F32)).astype(BF16)


def dot(a, b):
    return jnp.dot(a, b, preferred_element_type=F32)


def stacked(first, second):
    return jnp.concatenate([first, second], axis=1)


def kernel(pairs, info_ref, own_ref, *refs):
    near = refs[: 2 * pairs]
    wz, wzi, rf, ri, green, acc_in, out, held, own, mid, mid2 = refs[2 * pairs :]
    lanes = 2 * BOX
    low = lax.broadcasted_iota(jnp.int32, (BOX, lanes), 1) < BOX

    row = lax.broadcasted_iota(jnp.int32, (4 * BOX, 4 * BOX), 0)
    col = lax.broadcasted_iota(jnp.int32, (4 * BOX, 4 * BOX), 1)
    row_half, col_half = row // lanes, (col // BOX) % 2
    same = (row_half == col_half) & ((row // BOX) % 2 == col // lanes)
    away = row % BOX - col % BOX

    for y in range(BOX + 1):
        held[pl.ds(y * ROW, ROW - BOX), :] = jnp.zeros((ROW - BOX, lanes), F32)
    held[pl.ds(BOX * ROW, ROW + 32), :] = jnp.zeros((ROW + 32, lanes), F32)

    def own_step(t, _):
        v = own_ref[:, pl.ds(pl.multiple_of(t * lanes, lanes), lanes)].astype(F32)
        r = pltpu.roll(v, BOX, 1)
        base = pl.multiple_of(t * lanes, lanes)
        own[pl.ds(base, BOX), :] = jnp.where(low, v, r)
        own[pl.ds(base + BOX, BOX), :] = jnp.where(low, r, v)
        return 0

    lax.fori_loop(0, BOX // 2, own_step, 0, unroll=4)

    for p in range(pairs):
        a_ref, b_ref = near[2 * p], near[2 * p + 1]
        sx, sy, sz, slot, count = [[info_ref[FACTS * (2 * p + h) + f] for h in range(2)] for f in range(FACTS)]

        def weight(ref, h):
            tail = ref[pl.ds(0, 16), pl.ds(BOX * BOX, lanes)].astype(F32)[:8]
            at = lax.broadcasted_iota(jnp.int32, (8, lanes), 1)
            sent = jnp.sum(jnp.where(at == slot[h], tail, 0.0), axis=1, keepdims=True)[:1]
            return sent + count[h].astype(F32)

        def solve():
            want = jnp.where(col_half == 0, sz[0], sz[1])
            pick = jnp.where(same & (away == want), 1.0, 0.0).astype(BF16)

            def load():
                for t0 in range(0, BOX // 2, THICK):
                    rows = []
                    for t in range(t0, t0 + THICK):
                        at = pl.ds(t * lanes, lanes)
                        rows.append(stacked(a_ref[:, at], b_ref[:, at]))
                    v = dot(jnp.concatenate(rows, 0), pick)
                    for t in range(t0, t0 + THICK):
                        base = t * (2 * ROW) + (ROW - BOX)
                        part = v[(t - t0) * BOX : (t - t0 + 1) * BOX]
                        held[pl.ds(base, BOX), :] = part[:, :lanes]
                        held[pl.ds(base + ROW, BOX), :] = part[:, lanes:]

            def partner(y):
                parts = []
                for h in range(2):
                    from_y = y + sy[h]
                    block = jnp.where((from_y >= 0) & (from_y < BOX), from_y, BOX)
                    parts.append(held[pl.ds(block * ROW + (ROW - BOX) + sx[h], BOX), :])
                return jnp.where(low, parts[0], parts[1])

            def skewed(count, first, second):
                before = None
                for c in range(count):
                    now = first(c)
                    if before is not None:
                        second(c - 1, before)
                    before = now
                second(count - 1, before)

            def forward():
                def first(c):
                    rows = []
                    for j in range(CHUNK):
                        y = c * CHUNK + j
                        rows.append(stacked(*split(partner(y) * own[pl.ds(y * BOX, BOX), :])))
                    return dot(jnp.concatenate(rows, 0), wz[...])

                def second(c, wave):
                    high, rest = split(wave[:, :lanes] + wave[:, lanes:])
                    for j in range(0, CHUNK, 2):
                        at = j * BOX
                        h = stacked(high[at : at + BOX], high[at + BOX : at + 2 * BOX])
                        l = stacked(rest[at : at + BOX], rest[at + BOX : at + 2 * BOX])
                        u = dot(rf[...], jnp.concatenate([h, l, h], 0))
                        y = c * CHUNK + j
                        mid[pl.ds(y, BOX, stride=MROW), :] = u[:, :lanes]
                        mid[pl.ds(y + 1, BOX, stride=MROW), :] = u[:, lanes:]

                skewed(BOX // CHUNK, first, second)

            def middle():
                def first(c):
                    waves = []
                    for j in range(0, CHUNK, 2):
                        base = (c * CHUNK + j) * MROW
                        h, l = split(stacked(mid[pl.ds(base, BOX), :], mid[pl.ds(base + MROW, BOX), :]))
                        waves.append(dot(rf[...], jnp.concatenate([h, l, h], 0)))
                    return waves

                def second(c, waves):
                    for j in range(0, CHUNK, 2):
                        k = c * CHUNK + j
                        base = k * MROW
                        h, l = split(waves[j // 2] * stacked(green[(k + 1) // 2], green[(k + 2) // 2]))
                        v = dot(ri[...], jnp.concatenate([h, l, h], 0))
                        mid2[pl.ds(base, BOX), :] = v[:, :lanes]
                        mid2[pl.ds(base + MROW, BOX), :] = v[:, lanes:]

                skewed(BOX // CHUNK, first, second)

            def backward():
                scale = jnp.where(low, weight(a_ref, 0), weight(b_ref, 1))

                def first(c):
                    waves = []
                    for j in range(0, CHUNK, 2):
                        y = c * CHUNK + j
                        v = stacked(mid2[pl.ds(y, BOX, stride=MROW), :], mid2[pl.ds(y + 1, BOX, stride=MROW), :])
                        h, l = split(v)
                        waves.append(dot(ri[...], jnp.concatenate([h, l, h], 0)))
                    return waves

                def second(c, waves):
                    rows = []
                    for u in waves:
                        h, l = split(u)
                        rows.append(stacked(h[:, :lanes], l[:, :lanes]))
                        rows.append(stacked(h[:, lanes:], l[:, lanes:]))
                    wave = dot(jnp.concatenate(rows, 0), wzi[...])
                    field = wave[:, :lanes] + wave[:, lanes:]
                    for j in range(0, CHUNK, 2):
                        y = c * CHUNK + j
                        parts = []
                        for k in range(2):
                            v = field[(j + k) * BOX : (j + k + 1) * BOX] * (partner(y + k) * scale)
                            parts.append(v + pltpu.roll(v, BOX, 1))
                        at = pl.ds(y * BOX, lanes)
                        source = acc_in if p == 0 else out
                        out[:, at] = source[:, at] + jnp.where(low, parts[0], parts[1])

                skewed(BOX // CHUNK, first, second)

            load()
            forward()
            middle()
            backward()

        solve()


def exchange_terms(own, near, info, acc):
    pairs = len(near) // 2
    smem = pl.BlockSpec(memory_space=pltpu.SMEM)
    vmem = pl.BlockSpec(memory_space=pltpu.VMEM)
    wz, wzi, rf, ri, green = tables()
    return pl.pallas_call(
        functools.partial(kernel, pairs),
        out_shape=jax.ShapeDtypeStruct((BOX, BOX * BOX), F32),
        in_specs=[smem] + [vmem] * (len(near) + 7),
        out_specs=vmem,
        scratch_shapes=[
            pltpu.VMEM(((BOX + 1) * ROW + 32, 2 * BOX), F32),
            pltpu.VMEM((BOX * BOX, 2 * BOX), F32),
            pltpu.VMEM((BOX * MROW, 2 * BOX), F32),
            pltpu.VMEM((BOX * MROW, 2 * BOX), F32),
        ],
        compiler_params=pltpu.CompilerParams(vmem_limit_bytes=48 * 1024 * 1024),
    )(info, own, *near, wz, wzi, rf, ri, green, acc)


def body(orbitals, offsets, pair_list, pair_mask):
    count_x, count_y = lax.axis_size("dx"), lax.axis_size("dy")
    place_x, place_y = lax.axis_index("dx"), lax.axis_index("dy")
    mine = place_x * count_y + place_y

    owner = pair_list[:, 1]
    rel_x = (owner // count_y - place_x + 1) % count_x
    rel_y = (owner % count_y - place_y + 1) % count_y
    target = rel_x * 3 + rel_y
    used = jnp.where(target[:, None] == jnp.arange(9)[None, :], pair_mask[:, None], 0).sum(0)
    tail = jnp.broadcast_to(jnp.pad(used, (0, 2 * BOX - 9)).astype(BF16)[None, :], (BOX, 2 * BOX))
    own = jnp.concatenate([orbitals[0], tail], axis=1)

    def facts(places):
        rows = []
        for i, j in places:
            other = (place_x + i) % count_x * count_y + (place_y + j) % count_y
            move = offsets[mine] - offsets[other]
            ends = jnp.stack([(1 - i) * 3 + 1 - j, used[(1 + i) * 3 + 1 + j]])
            rows.append(jnp.concatenate([move, ends]))
        return jnp.concatenate(rows).astype(jnp.int32)

    def along(value, axis, to):
        return lax.ppermute(value, axis, [(i, to(i)) for i in range(lax.axis_size(axis))])

    inner = lambda i: i ^ 1
    outer = lambda i: ((i + 1) ^ 1) - 1 if 0 < i < count_x - 1 else count_x - 1 - i
    near = 1 - 2 * (place_x % 2)
    far = -near

    y_next = along(own, "dy", lambda i: (i - 1) % count_y)
    y_last = along(own, "dy", lambda i: (i + 1) % count_y)
    x_near, x_far = along(own, "dx", inner), along(own, "dx", outer)
    acc = jnp.zeros((BOX, BOX * BOX), F32)
    acc = exchange_terms(own, [own, own], facts([(0, 0), (0, 0)]) * jnp.array([1, 1, 1, 1, 0] * 2), acc)
    acc = exchange_terms(own, [x_near, x_far], facts([(near, 0), (far, 0)]), acc)
    corners = [along(v, "dx", to) for to in (inner, outer) for v in (y_next, y_last)]
    acc = exchange_terms(own, [y_next, y_last], facts([(0, 1), (0, -1)]), acc)
    acc = exchange_terms(own, corners[:2], facts([(near, 1), (near, -1)]), acc)
    acc = exchange_terms(own, corners[2:], facts([(far, 1), (far, -1)]), acc)
    return acc[None]


def solution(mesh):
    placed = (P(("dx", "dy"), None, None), P(), P(("dx", "dy"), None), P(("dx", "dy")))
    return jax.shard_map(
        body, mesh=mesh, in_specs=placed, out_specs=P(("dx", "dy"), None, None), check_vma=False
    )
```

time: 173 us -> 72.7 us (0.42)
  blocking collectives: 68.8 us -> 0 us
  Pallas kernels: 72.5 us -> 34.3 us
  waiting for transfers between devices: 0.02 us -> 12.9 us
  between operations: 10.1 us -> 0.2 us
  local copies, waits for them, and re-layouts: 3.19 us -> 8.21 us
    unnamed x1 -> x0, blocking collectives: 68.8 us -> none
    pallas_call x4 -> x5, Pallas kernels: 72.5 us -> 34.3 us  [exchange_terms(): pl.pallas_call(functools.partial(kernel, pairs), out_shape=jax.ShapeDtype...]
    ppermute x8, waiting for transfers between devices: 0.02 us -> 12.9 us  [along(): lax.ppermute(value, axis, [(i, to(i)) for i in range(lax.axis_size(axis))])]
    concatenate x0 -> x5, local copies, waits for them, and re-layouts: none -> 6.58 us  [facts(): return jnp.concatenate(rows).astype(jnp.int32)]
  transfers between devices with their start and end apart: 8 -> 8, of which waited for: 0 -> 2; matrix products, arithmetic and copies ran while one was open for 4% -> 11% of each run, Pallas kernels for 25% -> 36%
where the time goes in v2:
time: 72.7 us; the launch traced here: 72.3 us
  Pallas kernels  34.3 us (47%)
  starting transfers between devices  13.7 us (19%)
  waiting for transfers between devices  12.9 us (18%)
  local copies, waits for them, and re-layouts  8.21 us (11%)
  other arithmetic  3.05 us (4%)
    pallas_call x5, Pallas kernels, exchange_terms(): pl.pallas_call(functools.partial(kernel, pairs), out_shape=jax.ShapeDtype...  34.3 us
    ppermute x8, starting transfers between devices, along(): lax.ppermute(value, axis, [(i, to(i)) for i in range(lax.axis_size(axis))])  13.7 us
    ppermute x8, waiting for transfers between devices, along(): lax.ppermute(value, axis, [(i, to(i)) for i in range(lax.axis_size(axis))])  12.9 us
    concatenate x5, local copies, waits for them, and re-layouts, facts(): return jnp.concatenate(rows).astype(jnp.int32)  6.58 us
  transfers between devices with their start and end apart: 8, of which 2 were waited for; matrix products, arithmetic and copies ran while one was open for 11% of the time, Pallas kernels for 36%

profile of v2, /device:TPU:0, one launch (start us, length us, event | category | flops | bytes accessed | tf_op | source)
XLA Modules:
  0.0 72.3 jit_solution(2126565090287906894)
XLA Ops:
  0.0 0.0 copy-start.8
  0.0 0.0 copy-start.7
  0.0 0.7 %fusion.25 = s32[8]{0:T(128)S(1)} fusion(s32[8,2]{0,1:T(2,128)} %param.32, s32[]{:T(128)S(6)} %axis_index.25, s32[]{:T(128)S(6)} %axis_index.23), kind=kLoop, calls=%fused_computation.50 | loop fusion | flops 376 | bytes 72 | tf_op jit(solution)/shard_map/eq | solution.py:248
  0.7 0.7 %select_reduce_fusion = s32[9]{0:T(128)S(1)} fusion(s32[8]{0:T(128)} %param.33, s32[8]{0:T(128)S(1)} %fusion.25), kind=kLoop, calls=%fused_computation.3 | loop fusion | flops 207 | bytes 100 | tf_op jit(solution)/shard_map/reduce_sum | solution.py:248
  1.5 0.0 copy-start
  1.5 0.0 copy-start.1
  1.5 0.0 copy-start.2
  1.5 0.0 copy-start.3
  1.5 0.0 copy-start.4
  1.5 1.2 %pad_maximum_fusion.own_ref.refs_0_.refs_1_ = bf16[64,4224]{1,0:T(8,128)(2,1)S(1)} fusion(bf16[64,4096]{1,0:T(8,128)(2,1)} %bitcast.10, bf16[4224]{0:T(1024)(128)(2,1)S(1)} %fusion), kind=kLoop, calls=%fused_computation | loop fusion | flops 1081344 | bytes 1073408 | tf_op jit(solution)/shard_map/concatenate | solution.py:250
  2.8 5.4 %collective-permute-start = (bf16[64,4224]{1,0:T(8,128)(2,1)S(1)}, bf16[64,4224]{1,0:T(8,128)(2,1)S(1)}, u32[]{:S(2)}, u32[]{:S(2)}) collective-permute-start(bf16[64,4224]{1,0:T(8,128)(2,1)S(1)} %pad_maximum_fusion.own_ref.refs_0_.refs_1_), channel_id=1, source_target_pairs={{0,15},{1,0},{2,1},{3,2},{4,3},{5,4},{6,5},{7,6},{8,7},{9,8},{10,9... | collective-permute-start | bytes 1622024 | tf_op jit(solution)/shard_map/ppermute | solution.py:262
  8.1 0.0 collective-permute-start.2
  8.1 0.0 collective-permute-start.6
  8.2 4.1 %collective-permute-start.7 = (bf16[64,4224]{1,0:T(8,128)(2,1)S(1)}, bf16[64,4224]{1,0:T(8,128)(2,1)}, u32[]{:S(2)}, u32[]{:S(2)}) collective-permute-start(bf16[64,4224]{1,0:T(8,128)(2,1)S(1)} %pad_maximum_fusion.own_ref.refs_0_.refs_1_), channel_id=1, source_target_pairs={{0,112},{16,32},{32,16},{48,64},{64,48},{80,96},{96,80},{112,0},{1... | collective-permute-start | bytes 1622024 | tf_op jit(solution)/shard_map/ppermute | solution.py:262
  12.3 7.4 %collective-permute-done.refs_0_ = bf16[64,4224]{1,0:T(8,128)(2,1)S(1)} collective-permute-done((bf16[64,4224]{1,0:T(8,128)(2,1)S(1)}, bf16[64,4224]{1,0:T(8,128)(2,1)S(1)}, u32[]{:S(2)}, u32[]{:S(2)}) %collective-permute-start) | collective-permute-done | bytes 540704 | tf_op jit(solution)/shard_map/ppermute | solution.py:262
  19.7 0.0 collective-permute-start.4
  19.7 5.5 %collective-permute-done.2.refs_1_ = bf16[64,4224]{1,0:T(8,128)(2,1)S(1)} collective-permute-done((bf16[64,4224]{1,0:T(8,128)(2,1)S(1)}, bf16[64,4224]{1,0:T(8,128)(2,1)S(1)}, u32[]{:S(2)}, u32[]{:S(2)}) %collective-permute-start.2) | collective-permute-done | bytes 540704 | tf_op jit(solution)/shard_map/ppermute | solution.py:262
  25.2 0.0 collective-permute-start.5
  25.2 4.1 %collective-permute-start.1 = (bf16[64,4224]{1,0:T(8,128)(2,1)S(1)}, bf16[64,4224]{1,0:T(8,128)(2,1)}, u32[]{:S(2)}, u32[]{:S(2)}) collective-permute-start(bf16[64,4224]{1,0:T(8,128)(2,1)S(1)} %collective-permute-done.refs_0_), channel_id=1, source_target_pairs={{0,112},{16,32},{32,16},{48,64},{64,48},{80,96},{96,80},{112,0},{1... | collective-permute-start | bytes 1622024 | tf_op jit(solution)/shard_map/ppermute | solution.py:262
  29.4 0.0 collective-permute-done.6.refs_0_
  29.4 0.0 copy-start.5
  29.4 0.8 %copy-done.5 = bf16[64,4224]{1,0:T(8,128)(2,1)} copy-done((bf16[64,4224]{1,0:T(8,128)(2,1)}, bf16[64,4224]{1,0:T(8,128)(2,1)S(1)}, u32[]{:S(2)}) %copy-start.5) | copy-done | bytes 540696
  30.2 0.0 collective-permute-start.3
  30.2 0.0 copy-done.7
  30.2 0.3 fusion.18
  30.5 0.7 fusion.26
  31.2 1.3 %concatenate.23 = s32[10]{0:T(128)S(1)} concatenate(s32[3]{0:T(128)S(1)} %get-tuple-element.5, s32[1]{0:T(128)} %constant.168.clone.1, s32[1]{0:T(128)} %get-tuple-element.14, s32[3]{0:T(128)S(1)} %get-tuple-element.5, s32[1]{0:T(128)} %constant.168.clone.1, s32[1]{0:T(128)} %get-tuple-element.14), dimensions={0} | concatenate | bytes 80 | tf_op jit(solution)/shard_map/concatenate | solution.py:259
  32.5 0.0 copy-done.8
  32.6 1.4 %concatenate.22.info_ref = s32[10]{0:T(128)S(1)} concatenate(s32[3]{0:T(128)S(1)} %get-tuple-element.12, s32[1]{0:T(128)} %bitcast.6, s32[1]{0:T(128)} %get-tuple-element.16, s32[3]{0:T(128)S(1)} %get-tuple-element.13, s32[1]{0:T(128)} %bitcast.7, s32[1]{0:T(128)} %get-tuple-element.15), dimensions={0} | concatenate | bytes 80 | tf_op jit(solution)/shard_map/concatenate | solution.py:259
  33.9 1.3 %concatenate.21.info_ref = s32[10]{0:T(128)S(1)} concatenate(s32[3]{0:T(128)S(1)} %get-tuple-element.7, s32[1]{0:T(128)} %constant.165.clone.1, s32[1]{0:T(128)} %get-tuple-element.18, s32[3]{0:T(128)S(1)} %get-tuple-element.6, s32[1]{0:T(128)} %constant.166.clone.1, s32[1]{0:T(128)} %get-tuple-element.17), dimensions={0} | concatenate | bytes 80 | tf_op jit(solution)/shard_map/concatenate | solution.py:259
  35.2 1.3 %concatenate.20.info_ref = s32[10]{0:T(128)S(1)} concatenate(s32[3]{0:T(128)S(1)} %get-tuple-element.9, s32[1]{0:T(128)} %bitcast.4, s32[1]{0:T(128)} %get-tuple-element.20, s32[3]{0:T(128)S(1)} %get-tuple-element.8, s32[1]{0:T(128)} %bitcast.5, s32[1]{0:T(128)} %get-tuple-element.19), dimensions={0} | concatenate | bytes 80 | tf_op jit(solution)/shard_map/concatenate | solution.py:259
  36.5 1.3 %concatenate.18.info_ref = s32[10]{0:T(128)S(1)} concatenate(s32[3]{0:T(128)S(1)} %get-tuple-element.11, s32[1]{0:T(128)} %bitcast, s32[1]{0:T(128)} %get-tuple-element.22, s32[3]{0:T(128)S(1)} %get-tuple-element.10, s32[1]{0:T(128)} %bitcast.2, s32[1]{0:T(128)} %get-tuple-element.21), dimensions={0} | concatenate | bytes 80 | tf_op jit(solution)/shard_map/concatenate | solution.py:259
  37.8 0.1 broadcast_in_dim.30.refs_7_
  37.9 0.0 copy-done
  37.9 0.0 copy-done.1
  37.9 0.0 copy-done.2
  37.9 0.0 copy-done.3
  37.9 0.0 copy-done.4
  37.9 0.0 copy-start.6
  37.9 6.2 %shard_map.280.refs_7_ = f32[64,4096]{1,0:T(8,128)S(1)} custom-call(s32[10]{0:T(128)S(1)} %mul.59.info_ref, bf16[64,4224]{1,0:T(8,128)(2,1)S(1)} %pad_maximum_fusion.own_ref.refs_0_.refs_1_, bf16[64,4224]{1,0:T(8,128)(2,1)S(1)} %pad_maximum_fusion.own_ref.refs_0_.refs_1_, bf16[64,4224]{1,0:T(8,128)(2,1)S(1)} %pad_maximum_fusion.own_ref.refs_0_.refs_1_, ...), custom_call_target="tpu_custom_call" | custom-call | tf_op jit(solution)/shard_map/pallas_call | solution.py:224
  44.1 0.0 collective-permute-done.7.refs_1_
  44.1 0.0 copy-done.6
  44.1 6.7 %shard_map.281.refs_7_ = f32[64,4096]{1,0:T(8,128)S(1)} custom-call(s32[10]{0:T(128)S(1)} %concatenate.22.info_ref, bf16[64,4224]{1,0:T(8,128)(2,1)S(1)} %pad_maximum_fusion.own_ref.refs_0_.refs_1_, bf16[64,4224]{1,0:T(8,128)(2,1)S(1)} %copy-done.6, bf16[64,4224]{1,0:T(8,128)(2,1)} %collective-permute-done.7.refs_1_, bf16[256,256]{1,0:T(8,128)(2,1)S(1)} %copy-done.1, ...), custom_call_target="tpu_custom_call" | custom-call | tf_op jit(solution)/shard_map/pallas_call | solution.py:224
  50.9 6.3 %shard_map.282.refs_7_ = f32[64,4096]{1,0:T(8,128)S(1)} custom-call(s32[10]{0:T(128)S(1)} %concatenate.21.info_ref, bf16[64,4224]{1,0:T(8,128)(2,1)S(1)} %pad_maximum_fusion.own_ref.refs_0_.refs_1_, bf16[64,4224]{1,0:T(8,128)(2,1)S(1)} %collective-permute-done.refs_0_, bf16[64,4224]{1,0:T(8,128)(2,1)S(1)} %collective-permute-done.2.refs_1_, ...), custom_call_target="tpu_custom_call" | custom-call | tf_op jit(solution)/shard_map/pallas_call | solution.py:224
  57.2 0.0 collective-permute-done.4.refs_0_
  57.2 0.0 collective-permute-done.5.refs_1_
  57.2 7.2 %shard_map.283.refs_7_ = f32[64,4096]{1,0:T(8,128)S(1)} custom-call(s32[10]{0:T(128)S(1)} %concatenate.20.info_ref, bf16[64,4224]{1,0:T(8,128)(2,1)S(1)} %pad_maximum_fusion.own_ref.refs_0_.refs_1_, bf16[64,4224]{1,0:T(8,128)(2,1)} %collective-permute-done.4.refs_0_, bf16[64,4224]{1,0:T(8,128)(2,1)} %collective-permute-done.5.refs_1_, ...), custom_call_target="tpu_custom_call" | custom-call | tf_op jit(solution)/shard_map/pallas_call | solution.py:224
  64.4 0.0 collective-permute-done.1.refs_0_
  64.4 0.0 collective-permute-done.3.refs_1_
  64.4 7.9 %shard_map.284 = f32[64,4096]{1,0:T(8,128)} custom-call(s32[10]{0:T(128)S(1)} %concatenate.18.info_ref, bf16[64,4224]{1,0:T(8,128)(2,1)S(1)} %pad_maximum_fusion.own_ref.refs_0_.refs_1_, bf16[64,4224]{1,0:T(8,128)(2,1)} %collective-permute-done.1.refs_0_, bf16[64,4224]{1,0:T(8,128)(2,1)} %collective-permute-done.3.refs_1_, bf16[256,256]{1,0:T(8,128)(2,1)S(1)} %copy-done.1, ...), custom_call_target="tpu_custom_call" | custom-call | tf_op jit(solution)/shard_map/pallas_call | solution.py:224
  (3 shorter events, 0.0 us)
Async XLA Ops:
  0.0 32.5 %copy-start.8 = (s32[10]{0:T(128)S(1)}, s32[10]{0:T(128)}, u32[]{:S(2)}) copy-start(s32[10]{0:T(128)} %constant.170.clone) | copy-start | bytes 124
  0.0 30.2 %copy-start.7 = (s32[128,3]{0,1:T(4,128)S(1)}, s32[128,3]{0,1:T(4,128)}, u32[]{:S(2)}) copy-start(s32[128,3]{0,1:T(4,128)} %param.31) | copy-start | bytes 4612
  1.5 36.4 %copy-start = (f32[33,64,128]{2,1,0:T(8,128)S(1)}, f32[33,64,128]{2,1,0:T(8,128)}, u32[]{:S(2)}) copy-start(f32[33,64,128]{2,1,0:T(8,128)} %constant.175.clone.refs_6_) | copy-start | bytes 3244036
  1.5 36.4 %copy-start.1 = (bf16[256,256]{1,0:T(8,128)(2,1)S(1)}, bf16[256,256]{1,0:T(8,128)(2,1)}, u32[]{:S(2)}) copy-start(bf16[256,256]{1,0:T(8,128)(2,1)} %constant.171.clone.refs_2_) | copy-start | bytes 393220
  1.5 36.4 %copy-start.2 = (bf16[256,256]{1,0:T(8,128)(2,1)S(1)}, bf16[256,256]{1,0:T(8,128)(2,1)}, u32[]{:S(2)}) copy-start(bf16[256,256]{1,0:T(8,128)(2,1)} %constant.172.clone.refs_3_) | copy-start | bytes 393220
  1.5 36.4 %copy-start.3 = (bf16[64,192]{1,0:T(8,128)(2,1)S(1)}, bf16[64,192]{1,0:T(8,128)(2,1)}, u32[]{:S(2)}) copy-start(bf16[64,192]{1,0:T(8,128)(2,1)} %constant.173.clone.refs_4_) | copy-start | bytes 73732
  1.5 36.4 %copy-start.4 = (bf16[64,192]{1,0:T(8,128)(2,1)S(1)}, bf16[64,192]{1,0:T(8,128)(2,1)}, u32[]{:S(2)}) copy-start(bf16[64,192]{1,0:T(8,128)(2,1)} %constant.174.clone.refs_5_) | copy-start | bytes 73732
  2.8 16.9 %collective-permute-start = (bf16[64,4224]{1,0:T(8,128)(2,1)S(1)}, bf16[64,4224]{1,0:T(8,128)(2,1)S(1)}, u32[]{:S(2)}, u32[]{:S(2)}) collective-permute-start(bf16[64,4224]{1,0:T(8,128)(2,1)S(1)} %pad_maximum_fusion.own_ref.refs_0_.refs_1_), channel_id=1, source_target_pairs={{0,15},{1,0},{2,1},{3,2},{4,3},{5,4},{6,5},{7,6},{8,7},{9,8},{10,9... | collective-permute-start | bytes 1622024 | tf_op jit(solution)/shard_map/ppermute | solution.py:262
  8.1 17.1 %collective-permute-start.2 = (bf16[64,4224]{1,0:T(8,128)(2,1)S(1)}, bf16[64,4224]{1,0:T(8,128)(2,1)S(1)}, u32[]{:S(2)}, u32[]{:S(2)}) collective-permute-start(bf16[64,4224]{1,0:T(8,128)(2,1)S(1)} %pad_maximum_fusion.own_ref.refs_0_.refs_1_), channel_id=1, source_target_pairs={{0,1},{1,2},{2,3},{3,4},{4,5},{5,6},{6,7},{7,8},{8,9},{9,10},{10,1... | collective-permute-start | bytes 1622024 | tf_op jit(solution)/shard_map/ppermute | solution.py:262
  8.1 21.2 %collective-permute-start.6 = (bf16[64,4224]{1,0:T(8,128)(2,1)S(1)}, bf16[64,4224]{1,0:T(8,128)(2,1)S(1)}, u32[]{:S(2)}, u32[]{:S(2)}) collective-permute-start(bf16[64,4224]{1,0:T(8,128)(2,1)S(1)} %pad_maximum_fusion.own_ref.refs_0_.refs_1_), channel_id=1, source_target_pairs={{0,16},{16,0},{32,48},{48,32},{64,80},{80,64},{96,112},{112,96},{1... | collective-permute-start | bytes 1622024 | tf_op jit(solution)/shard_map/ppermute | solution.py:262
  8.2 36.0 %collective-permute-start.7 = (bf16[64,4224]{1,0:T(8,128)(2,1)S(1)}, bf16[64,4224]{1,0:T(8,128)(2,1)}, u32[]{:S(2)}, u32[]{:S(2)}) collective-permute-start(bf16[64,4224]{1,0:T(8,128)(2,1)S(1)} %pad_maximum_fusion.own_ref.refs_0_.refs_1_), channel_id=1, source_target_pairs={{0,112},{16,32},{32,16},{48,64},{64,48},{80,96},{96,80},{112,0},{1... | collective-permute-start | bytes 1622024 | tf_op jit(solution)/shard_map/ppermute | solution.py:262
  19.7 37.5 %collective-permute-start.4 = (bf16[64,4224]{1,0:T(8,128)(2,1)S(1)}, bf16[64,4224]{1,0:T(8,128)(2,1)}, u32[]{:S(2)}, u32[]{:S(2)}) collective-permute-start(bf16[64,4224]{1,0:T(8,128)(2,1)S(1)} %collective-permute-done.refs_0_), channel_id=1, source_target_pairs={{0,16},{16,0},{32,48},{48,32},{64,80},{80,64},{96,112},{112,96},{1... | collective-permute-start | bytes 1622024 | tf_op jit(solution)/shard_map/ppermute | solution.py:262
  25.2 32.0 %collective-permute-start.5 = (bf16[64,4224]{1,0:T(8,128)(2,1)S(1)}, bf16[64,4224]{1,0:T(8,128)(2,1)}, u32[]{:S(2)}, u32[]{:S(2)}) collective-permute-start(bf16[64,4224]{1,0:T(8,128)(2,1)S(1)} %collective-permute-done.2.refs_1_), channel_id=1, source_target_pairs={{0,16},{16,0},{32,48},{48,32},{64,80},{80,64},{96,112},{112,96},{1... | collective-permute-start | bytes 1622024 | tf_op jit(solution)/shard_map/ppermute | solution.py:262
  25.2 39.2 %collective-permute-start.1 = (bf16[64,4224]{1,0:T(8,128)(2,1)S(1)}, bf16[64,4224]{1,0:T(8,128)(2,1)}, u32[]{:S(2)}, u32[]{:S(2)}) collective-permute-start(bf16[64,4224]{1,0:T(8,128)(2,1)S(1)} %collective-permute-done.refs_0_), channel_id=1, source_target_pairs={{0,112},{16,32},{32,16},{48,64},{64,48},{80,96},{96,80},{112,0},{1... | collective-permute-start | bytes 1622024 | tf_op jit(solution)/shard_map/ppermute | solution.py:262
  29.4 0.8 %copy-start.5 = (bf16[64,4224]{1,0:T(8,128)(2,1)}, bf16[64,4224]{1,0:T(8,128)(2,1)S(1)}, u32[]{:S(2)}) copy-start(bf16[64,4224]{1,0:T(8,128)(2,1)S(1)} %collective-permute-done.6.refs_0_) | copy-start | bytes 1622020
  30.2 34.2 %collective-permute-start.3 = (bf16[64,4224]{1,0:T(8,128)(2,1)S(1)}, bf16[64,4224]{1,0:T(8,128)(2,1)}, u32[]{:S(2)}, u32[]{:S(2)}) collective-permute-start(bf16[64,4224]{1,0:T(8,128)(2,1)S(1)} %collective-permute-done.2.refs_1_), channel_id=1, source_target_pairs={{0,112},{16,32},{32,16},{48,64},{64,48},{80,96},{96,80},{112,0},{1... | collective-permute-start | bytes 1622024 | tf_op jit(solution)/shard_map/ppermute | solution.py:262
  37.9 6.2 %copy-start.6 = (bf16[64,4224]{1,0:T(8,128)(2,1)S(1)}, bf16[64,4224]{1,0:T(8,128)(2,1)}, u32[]{:S(2)}) copy-start(bf16[64,4224]{1,0:T(8,128)(2,1)} %copy-done.5) | copy-start | bytes 1622020

commit v3 on v2

--- a/solution.py
+++ b/solution.py
@@ -12,7 +12,7 @@
 
 BOX = 64
 ROW = 96
-FACTS = 5
+HOME = (0, 0)
 MROW = 72
 CHUNK = 16
 THICK = 8
@@ -65,9 +65,47 @@
     return jnp.concatenate([first, second], axis=1)
 
 
-def kernel(pairs, info_ref, own_ref, *refs):
+def target(pair_list, slot):
+    size_x, size_y = lax.axis_size("dx"), lax.axis_size("dy")
+    owner = pair_list[slot, 1]
+    rel_x = (owner // size_y - lax.axis_index("dx") + 1 + size_x) % size_x
+    rel_y = (owner % size_y - lax.axis_index("dy") + 1 + size_y) % size_y
+    return rel_x * 3 + rel_y
+
+
+def known(i, j, offsets, pair_list, pair_mask):
+    size_x, size_y = lax.axis_size("dx"), lax.axis_size("dy")
+    here_x, here_y = lax.axis_index("dx"), lax.axis_index("dy")
+    if (i, j) == HOME:
+        return tuple(0 * offsets[0, c] for c in range(3)) + (4 + 0 * offsets[0, 0], 0 * offsets[0, 0])
+    step = i * (1 - 2 * (here_x % 2))
+    other = (here_x + step + size_x) % size_x * size_y + (here_y + j + size_y) % size_y
+    mine = here_x * size_y + here_y
+    move = tuple(offsets[mine, c] - offsets[other, c] for c in range(3))
+    index = (1 + step) * 3 + 1 + j
+    count = sum(jnp.where(target(pair_list, n) == index, pair_mask[n], 0) for n in range(pair_list.shape[0]))
+    return move + (8 - index, count)
+
+
+def tail_kernel(pair_list, pair_mask, box, out):
+    lane = lax.broadcasted_iota(jnp.int32, (BOX, 2 * BOX), 1)
+    counts = jnp.zeros((BOX, 2 * BOX), jnp.int32)
+    for n in range(pair_list.shape[0]):
+        counts += jnp.where(lane == target(pair_list, n), pair_mask[n], 0)
+    out[:, pl.ds(BOX * BOX, 2 * BOX)] = counts.astype(F32).astype(BF16)
+    out[:, pl.ds(0, BOX * BOX)] = box[...]
+
+
+def kernel(places, offsets, pair_list, pair_mask, own_ref, *refs):
+    pairs = len(places) // 2
     near = refs[: 2 * pairs]
-    wz, wzi, rf, ri, green, acc_in, out, held, own, mid, mid2 = refs[2 * pairs :]
+    if places[0] == HOME:
+        wz, wzi, rf, ri, green, out, own, held, mid, mid2 = refs[2 * pairs :]
+        acc_in = None
+    else:
+        wz, wzi, rf, ri, green, acc_in, out, held, mid, mid2 = refs[2 * pairs :]
+        own = own_ref
+    facts = [known(i, j, offsets, pair_list, pair_mask) for i, j in places]
     lanes = 2 * BOX
     low = lax.broadcasted_iota(jnp.int32, (BOX, lanes), 1) < BOX
 
@@ -89,11 +127,12 @@
         own[pl.ds(base + BOX, BOX), :] = jnp.where(low, r, v)
         return 0
 
-    lax.fori_loop(0, BOX // 2, own_step, 0, unroll=4)
+    if places[0] == HOME:
+        lax.fori_loop(0, BOX // 2, own_step, 0, unroll=4)
 
     for p in range(pairs):
         a_ref, b_ref = near[2 * p], near[2 * p + 1]
-        sx, sy, sz, slot, count = [[info_ref[FACTS * (2 * p + h) + f] for h in range(2)] for f in range(FACTS)]
+        sx, sy, sz, slot, count = zip(*facts[2 * p : 2 * p + 2])
 
         def weight(ref, h):
             tail = ref[pl.ds(0, 16), pl.ds(BOX * BOX, lanes)].astype(F32)[:8]
@@ -203,8 +242,12 @@
                             v = field[(j + k) * BOX : (j + k + 1) * BOX] * (partner(y + k) * scale)
                             parts.append(v + pltpu.roll(v, BOX, 1))
                         at = pl.ds(y * BOX, lanes)
-                        source = acc_in if p == 0 else out
-                        out[:, at] = source[:, at] + jnp.where(low, parts[0], parts[1])
+                        both = jnp.where(low, parts[0], parts[1])
+                        if p > 0:
+                            both = out[:, at] + both
+                        elif acc_in is not None:
+                            both = acc_in[:, at] + both
+                        out[:, at] = both
 
                 skewed(BOX // CHUNK, first, second)
 
@@ -216,66 +259,61 @@
         solve()
 
 
-def exchange_terms(own, near, info, acc):
-    pairs = len(near) // 2
-    smem = pl.BlockSpec(memory_space=pltpu.SMEM)
-    vmem = pl.BlockSpec(memory_space=pltpu.VMEM)
-    wz, wzi, rf, ri, green = tables()
+SMEM = pl.BlockSpec(memory_space=pltpu.SMEM)
+VMEM = pl.BlockSpec(memory_space=pltpu.VMEM)
+PARAMS = pltpu.CompilerParams(vmem_limit_bytes=48 * 1024 * 1024)
+
+
+def exchange_terms(places, ints, own, boxes, *acc):
+    first = places[0] == HOME
+    shape = [jax.ShapeDtypeStruct((BOX, BOX * BOX), F32)]
+    if first:
+        shape.append(jax.ShapeDtypeStruct((BOX * BOX, 2 * BOX), F32))
     return pl.pallas_call(
-        functools.partial(kernel, pairs),
-        out_shape=jax.ShapeDtypeStruct((BOX, BOX * BOX), F32),
-        in_specs=[smem] + [vmem] * (len(near) + 7),
-        out_specs=vmem,
+        functools.partial(kernel, places),
+        out_shape=shape,
+        in_specs=[SMEM] * 3 + [VMEM] * (len(boxes) + 6 + len(acc)),
+        out_specs=[VMEM] * len(shape),
         scratch_shapes=[
             pltpu.VMEM(((BOX + 1) * ROW + 32, 2 * BOX), F32),
-            pltpu.VMEM((BOX * BOX, 2 * BOX), F32),
             pltpu.VMEM((BOX * MROW, 2 * BOX), F32),
             pltpu.VMEM((BOX * MROW, 2 * BOX), F32),
         ],
-        compiler_params=pltpu.CompilerParams(vmem_limit_bytes=48 * 1024 * 1024),
-    )(info, own, *near, wz, wzi, rf, ri, green, acc)
+        compiler_params=PARAMS,
+    )(*ints, own, *boxes, *tables(), *acc)
+
+
+def along(value, axis, to):
+    return lax.ppermute(value, axis, [(i, to(i)) for i in range(lax.axis_size(axis))])
 
 
 def body(orbitals, offsets, pair_list, pair_mask):
-    count_x, count_y = lax.axis_size("dx"), lax.axis_size("dy")
-    place_x, place_y = lax.axis_index("dx"), lax.axis_index("dy")
-    mine = place_x * count_y + place_y
-
-    owner = pair_list[:, 1]
-    rel_x = (owner // count_y - place_x + 1) % count_x
-    rel_y = (owner % count_y - place_y + 1) % count_y
-    target = rel_x * 3 + rel_y
-    used = jnp.where(target[:, None] == jnp.arange(9)[None, :], pair_mask[:, None], 0).sum(0)
-    tail = jnp.broadcast_to(jnp.pad(used, (0, 2 * BOX - 9)).astype(BF16)[None, :], (BOX, 2 * BOX))
-    own = jnp.concatenate([orbitals[0], tail], axis=1)
-
-    def facts(places):
-        rows = []
-        for i, j in places:
-            other = (place_x + i) % count_x * count_y + (place_y + j) % count_y
-            move = offsets[mine] - offsets[other]
-            ends = jnp.stack([(1 - i) * 3 + 1 - j, used[(1 + i) * 3 + 1 + j]])
-            rows.append(jnp.concatenate([move, ends]))
-        return jnp.concatenate(rows).astype(jnp.int32)
-
-    def along(value, axis, to):
-        return lax.ppermute(value, axis, [(i, to(i)) for i in range(lax.axis_size(axis))])
-
-    inner = lambda i: i ^ 1
-    outer = lambda i: ((i + 1) ^ 1) - 1 if 0 < i < count_x - 1 else count_x - 1 - i
-    near = 1 - 2 * (place_x % 2)
-    far = -near
-
-    y_next = along(own, "dy", lambda i: (i - 1) % count_y)
-    y_last = along(own, "dy", lambda i: (i + 1) % count_y)
+    size_x, size_y = lax.axis_size("dx"), lax.axis_size("dy")
+    ints = (offsets, pair_list, pair_mask)
+    own = pl.pallas_call(
+        tail_kernel,
+        out_shape=jax.ShapeDtypeStruct((BOX, BOX * BOX + 2 * BOX), BF16),
+        in_specs=[SMEM, SMEM, VMEM],
+        out_specs=VMEM,
+        compiler_params=PARAMS,
+    )(pair_list, pair_mask, orbitals[0])
+
+    def inner(i):
+        return i ^ 1
+
+    def outer(i):
+        return (i - 1 + 2 * (i % 2)) % size_x
+
+    y_next = along(own, "dy", lambda i: (i - 1) % size_y)
+    y_last = along(own, "dy", lambda i: (i + 1) % size_y)
     x_near, x_far = along(own, "dx", inner), along(own, "dx", outer)
-    acc = jnp.zeros((BOX, BOX * BOX), F32)
-    acc = exchange_terms(own, [own, own], facts([(0, 0), (0, 0)]) * jnp.array([1, 1, 1, 1, 0] * 2), acc)
-    acc = exchange_terms(own, [x_near, x_far], facts([(near, 0), (far, 0)]), acc)
+    acc, wide = exchange_terms((HOME, HOME), ints, own, (own, own))
+    (acc,) = exchange_terms(((1, 0), (-1, 0)), ints, wide, (x_near, x_far), acc)
+    y_next, y_last, acc = lax.optimization_barrier((y_next, y_last, acc))
     corners = [along(v, "dx", to) for to in (inner, outer) for v in (y_next, y_last)]
-    acc = exchange_terms(own, [y_next, y_last], facts([(0, 1), (0, -1)]), acc)
-    acc = exchange_terms(own, corners[:2], facts([(near, 1), (near, -1)]), acc)
-    acc = exchange_terms(own, corners[2:], facts([(far, 1), (far, -1)]), acc)
+    (acc,) = exchange_terms(((0, 1), (0, -1)), ints, wide, (y_next, y_last), acc)
+    (acc,) = exchange_terms(((1, 1), (1, -1)), ints, wide, corners[:2], acc)
+    (acc,) = exchange_terms(((-1, 1), (-1, -1)), ints, wide, corners[2:], acc)
     return acc[None]
 
 

time: 72.7 us -> 58.1 us (0.80)
  waiting for transfers between devices: 12.9 us -> 0.02 us
  other arithmetic: 3.05 us -> 0 us
  local copies, waits for them, and re-layouts: 8.21 us -> 9.78 us
  starting transfers between devices: 13.7 us -> 12.5 us
    ppermute x8, waiting for transfers between devices: 12.9 us -> 0.02 us  [along(): lax.ppermute(value, axis, [(i, to(i)) for i in range(lax.axis_size(axis))])]
    unnamed x18 -> x32, local copies, waits for them, and re-layouts: 0.84 us -> 9.78 us
    concatenate x5 -> x0, local copies, waits for them, and re-layouts: 6.58 us -> none  [facts(): return jnp.concatenate(rows).astype(jnp.int32)]
    concatenate x2 -> x0, other arithmetic: 1.24 us -> none  [body(): own = jnp.concatenate([orbitals[0], tail], axis=1)]
    ppermute x8, starting transfers between devices: 13.7 us -> 12.5 us  [along(): lax.ppermute(value, axis, [(i, to(i)) for i in range(lax.axis_size(axis))])]
    reduce_sum x1 -> x0, other arithmetic: 0.74 us -> none  [body(): jnp.where(target[:, None] == jnp.arange(9)[None, :], pair_mask[:, None], 0)]
    eq x1 -> x0, other arithmetic: 0.73 us -> none  [body(): target[:, None] == jnp.arange(9)[None, :]]
    pallas_call x5 -> x6, Pallas kernels: 34.3 us -> 35 us  [the longest x5 34.3 us: exchange_terms(): pl.pallas_call(functools.partial(kernel, places), out_shape=shape, in_spe...]
  transfers between devices with their start and end apart: 8 -> 8, of which waited for: 2 -> 0; matrix products, arithmetic and copies ran while one was open for 11% -> 1% of each run, Pallas kernels for 36% -> 46%
where the time goes in v3:
time: 58.1 us; the launch traced here: 57.5 us
  Pallas kernels  35 us (60%)
  starting transfers between devices  12.5 us (22%)
  local copies, waits for them, and re-layouts  9.78 us (17%)
    pallas_call x5, Pallas kernels, exchange_terms(): pl.pallas_call(functools.partial(kernel, places), out_shape=shape, in_spe...  34.3 us
    ppermute x8, starting transfers between devices, along(): lax.ppermute(value, axis, [(i, to(i)) for i in range(lax.axis_size(axis))])  12.5 us
    unnamed x32, local copies, waits for them, and re-layouts  9.78 us
  transfers between devices with their start and end apart: 8, of which 0 were waited for; matrix products, arithmetic and copies ran while one was open for 1% of the time, Pallas kernels for 46%

profile of v3, /device:TPU:0, one launch (start us, length us, event | category | flops | bytes accessed | tf_op | source)
XLA Modules:
  0.0 57.5 jit_solution(5565938636077724981)
XLA Ops:
  0.0 0.8 %copy.40.pair_list = s32[8,2]{1,0:T(8,128)S(1)} copy(s32[8,2]{0,1:T(2,128)} %param.31) | data formatting | bytes 128 | tf_op args[2]
  0.8 0.0 copy-start.12
  0.8 1.0 %copy-done.12 = bf16[1,64,4096]{2,1,0:T(8,128)(2,1)S(1)} copy-done((bf16[1,64,4096]{2,1,0:T(8,128)(2,1)S(1)}, bf16[1,64,4096]{2,1,0:T(8,128)(2,1)}, u32[]{:S(2)}) %copy-start.12) | copy-done | bytes 524312
  1.8 0.0 copy-start.13
  1.8 0.7 %copy-done.13 = s32[8]{0:T(128)S(1)} copy-done((s32[8]{0:T(128)S(1)}, s32[8]{0:T(128)}, u32[]{:S(2)}) %copy-start.13) | copy-done | bytes 56
  2.5 0.0 copy-start.3
  2.5 0.0 copy-start.9
  2.5 0.7 %shard_map.271.own_ref.refs_0_.refs_1_ = bf16[64,4224]{1,0:T(8,128)(2,1)S(1)} custom-call(s32[8,2]{1,0:T(8,128)S(1)} %copy.40.pair_list, s32[8]{0:T(128)S(1)} %copy-done.13, bf16[64,4096]{1,0:T(8,128)(2,1)S(1)} %bitcast.2), custom_call_target="tpu_custom_call" | custom-call | tf_op jit(solution)/shard_map/pallas_call | solution.py:293
  3.2 3.6 %collective-permute-start.3 = (bf16[64,4224]{1,0:T(8,128)(2,1)S(1)}, bf16[64,4224]{1,0:T(8,128)(2,1)S(1)}, u32[]{:S(2)}, u32[]{:S(2)}) collective-permute-start(bf16[64,4224]{1,0:T(8,128)(2,1)S(1)} %shard_map.271.own_ref.refs_0_.refs_1_), channel_id=1, source_target_pairs={{0,112},{16,32},{32,16},{48,64},{64,48},{80,96},{96,80},{112,0},{1... | collective-permute-start | bytes 1622024 | tf_op jit(solution)/shard_map/ppermute | solution.py:287
  6.8 0.0 collective-permute-start.2
  6.8 1.5 %collective-permute-start.1 = (bf16[64,4224]{1,0:T(8,128)(2,1)S(1)}, bf16[64,4224]{1,0:T(8,128)(2,1)S(1)}, u32[]{:S(2)}, u32[]{:S(2)}) collective-permute-start(bf16[64,4224]{1,0:T(8,128)(2,1)S(1)} %shard_map.271.own_ref.refs_0_.refs_1_), channel_id=1, source_target_pairs={{0,1},{1,2},{2,3},{3,4},{4,5},{5,6},{6,7},{7,8},{8,9},{9,10},{10,1... | collective-permute-start | bytes 1622024 | tf_op jit(solution)/shard_map/ppermute | solution.py:287
  8.3 3.9 %collective-permute-start = (bf16[64,4224]{1,0:T(8,128)(2,1)S(1)}, bf16[64,4224]{1,0:T(8,128)(2,1)S(1)}, u32[]{:S(2)}, u32[]{:S(2)}) collective-permute-start(bf16[64,4224]{1,0:T(8,128)(2,1)S(1)} %shard_map.271.own_ref.refs_0_.refs_1_), channel_id=1, source_target_pairs={{0,15},{1,0},{2,1},{3,2},{4,3},{5,4},{6,5},{7,6},{8,7},{9,8},{10,9... | collective-permute-start | bytes 1622024 | tf_op jit(solution)/shard_map/ppermute | solution.py:287
  12.2 0.8 %copy.39.offsets = s32[128,3]{1,0:T(8,128)S(1)} copy(s32[128,3]{0,1:T(4,128)} %param.30) | data formatting | bytes 3072 | tf_op args[1]
  13.0 0.0 copy-start.2
  13.0 1.2 %copy-done.2 = f32[33,64,128]{2,1,0:T(8,128)S(1)} copy-done((f32[33,64,128]{2,1,0:T(8,128)S(1)}, f32[33,64,128]{2,1,0:T(8,128)}, u32[]{:S(2)}) %copy-start.2) | copy-done | bytes 1081368
  14.2 0.0 copy-start.4
  14.2 0.9 %copy-done.4 = bf16[256,256]{1,0:T(8,128)(2,1)S(1)} copy-done((bf16[256,256]{1,0:T(8,128)(2,1)S(1)}, bf16[256,256]{1,0:T(8,128)(2,1)}, u32[]{:S(2)}) %copy-start.4) | copy-done | bytes 131096
  15.1 0.0 copy-start.6
  15.1 0.9 %copy-done.6 = bf16[256,256]{1,0:T(8,128)(2,1)S(1)} copy-done((bf16[256,256]{1,0:T(8,128)(2,1)S(1)}, bf16[256,256]{1,0:T(8,128)(2,1)}, u32[]{:S(2)}) %copy-start.6) | copy-done | bytes 131096
  16.0 0.0 copy-start.8
  16.0 0.8 %copy-done.8 = bf16[64,192]{1,0:T(8,128)(2,1)S(1)} copy-done((bf16[64,192]{1,0:T(8,128)(2,1)S(1)}, bf16[64,192]{1,0:T(8,128)(2,1)}, u32[]{:S(2)}) %copy-start.8) | copy-done | bytes 24600
  16.8 0.0 copy-start.10
  16.8 0.8 %copy-done.10 = bf16[64,192]{1,0:T(8,128)(2,1)S(1)} copy-done((bf16[64,192]{1,0:T(8,128)(2,1)S(1)}, bf16[64,192]{1,0:T(8,128)(2,1)}, u32[]{:S(2)}) %copy-start.10) | copy-done | bytes 24600
  17.5 0.0 copy-start.14
  17.5 0.7 %copy-done.14 = s32[8]{0:T(128)S(1)} copy-done((s32[8]{0:T(128)S(1)}, s32[8]{0:T(128)}, u32[]{:S(2)}) %copy-start.14) | copy-done | bytes 56
  18.2 0.0 copy-start.5
  18.2 0.0 copy-start.7
  18.2 0.0 copy-start.11
  18.2 6.9 %shard_map.272 = (f32[64,4096]{1,0:T(8,128)S(1)}, f32[4096,128]{1,0:T(8,128)S(1)}) custom-call(s32[128,3]{1,0:T(8,128)S(1)} %copy.39.offsets, s32[8,2]{1,0:T(8,128)S(1)} %copy.40.pair_list, s32[8]{0:T(128)S(1)} %copy-done.14, bf16[64,4224]{1,0:T(8,128)(2,1)S(1)} %shard_map.271.own_ref.refs_0_.refs_1_, ...), custom_call_target="tpu_custom_call" | custom-call | tf_op jit(solution)/shard_map/pallas_call | solution.py:272
  25.1 0.0 copy-start
  25.1 1.3 %copy-done = f32[4096,128]{1,0:T(8,128)} copy-done((f32[4096,128]{1,0:T(8,128)}, f32[4096,128]{1,0:T(8,128)S(1)}, u32[]{:S(2)}) %copy-start) | copy-done | bytes 2097176
  26.4 0.0 collective-permute-done.3.refs_1_
  26.4 0.0 collective-permute-done.2.refs_0_
  26.4 0.0 copy-done.3
  26.4 0.0 copy-done.9
  26.4 0.0 copy-done.5
  26.5 0.0 copy-done.7
  26.5 0.0 copy-done.11
  26.5 6.5 %shard_map.273.refs_7_ = f32[64,4096]{1,0:T(8,128)S(1)} custom-call(s32[128,3]{1,0:T(8,128)S(1)} %copy.39.offsets, s32[8,2]{1,0:T(8,128)S(1)} %copy.40.pair_list, s32[8]{0:T(128)S(1)} %copy-done.14, f32[4096,128]{1,0:T(8,128)} %copy-done, bf16[64,4224]{1,0:T(8,128)(2,1)} %collective-permute-done.2.refs_0_, ...), custom_call_target="tpu_custom_call" | custom-call | tf_op jit(solution)/shard_map/pallas_call | solution.py:272
  33.0 0.0 collective-permute-done.1.refs_1_
  33.0 0.0 collective-permute-done.refs_0_
  33.0 0.2 collective-permute-start.6
  33.3 0.4 collective-permute-start.7
  33.6 0.5 collective-permute-start.4
  34.1 2.5 %collective-permute-start.5 = (bf16[64,4224]{1,0:T(8,128)(2,1)S(1)}, bf16[64,4224]{1,0:T(8,128)(2,1)S(1)}, u32[]{:S(2)}, u32[]{:S(2)}) collective-permute-start(bf16[64,4224]{1,0:T(8,128)(2,1)S(1)} %collective-permute-done.1.refs_1_), channel_id=1, source_target_pairs={{0,112},{16,32},{32,16},{48,64},{64,48},{80,96},{96,80},{112,0},{1... | collective-permute-start | bytes 1622024 | tf_op jit(solution)/shard_map/ppermute | solution.py:287
  36.6 6.5 %shard_map.274.refs_7_ = f32[64,4096]{1,0:T(8,128)S(1)} custom-call(s32[128,3]{1,0:T(8,128)S(1)} %copy.39.offsets, s32[8,2]{1,0:T(8,128)S(1)} %copy.40.pair_list, s32[8]{0:T(128)S(1)} %copy-done.14, f32[4096,128]{1,0:T(8,128)} %copy-done, bf16[64,4224]{1,0:T(8,128)(2,1)S(1)} %collective-permute-done.refs_0_, ...), custom_call_target="tpu_custom_call" | custom-call | tf_op jit(solution)/shard_map/pallas_call | solution.py:272
  43.1 0.0 copy-start.1
  43.1 0.0 collective-permute-done.6.refs_0_
  43.1 0.0 collective-permute-done.7.refs_1_
  43.2 6.7 %shard_map.275.refs_7_ = f32[64,4096]{1,0:T(8,128)S(1)} custom-call(s32[128,3]{1,0:T(8,128)S(1)} %copy.39.offsets, s32[8,2]{1,0:T(8,128)S(1)} %copy.40.pair_list, s32[8]{0:T(128)S(1)} %copy-done.14, f32[4096,128]{1,0:T(8,128)} %copy-done, bf16[64,4224]{1,0:T(8,128)(2,1)S(1)} %collective-permute-done.6.refs_0_, ...), custom_call_target="tpu_custom_call" | custom-call | tf_op jit(solution)/shard_map/pallas_call | solution.py:272
  49.9 0.0 collective-permute-done.4.refs_0_
  49.9 0.0 collective-permute-done.5.refs_1_
  49.9 0.0 copy-done.1
  49.9 7.6 %shard_map.276 = f32[64,4096]{1,0:T(8,128)} custom-call(s32[128,3]{1,0:T(8,128)S(1)} %copy.39.offsets, s32[8,2]{1,0:T(8,128)S(1)} %copy.40.pair_list, s32[8]{0:T(128)S(1)} %copy-done.14, f32[4096,128]{1,0:T(8,128)S(1)} %copy-done.1, bf16[64,4224]{1,0:T(8,128)(2,1)S(1)} %collective-permute-done.4.refs_0_, ...), custom_call_target="tpu_custom_call" | custom-call | tf_op jit(solution)/shard_map/pallas_call | solution.py:272
Async XLA Ops:
  0.8 1.0 %copy-start.12 = (bf16[1,64,4096]{2,1,0:T(8,128)(2,1)S(1)}, bf16[1,64,4096]{2,1,0:T(8,128)(2,1)}, u32[]{:S(2)}) copy-start(bf16[1,64,4096]{2,1,0:T(8,128)(2,1)} %param.29) | copy-start | bytes 1572868
  1.8 0.7 %copy-start.13 = (s32[8]{0:T(128)S(1)}, s32[8]{0:T(128)}, u32[]{:S(2)}) copy-start(s32[8]{0:T(128)} %pair_mask.11) | copy-start | bytes 100
  2.5 24.0 %copy-start.3 = (f32[33,64,128]{2,1,0:T(8,128)S(1)}, f32[33,64,128]{2,1,0:T(8,128)}, u32[]{:S(2)}) copy-start(f32[33,64,128]{2,1,0:T(8,128)} %constant.14.clone.refs_6_) | copy-start | bytes 3244036
  2.5 24.0 %copy-start.9 = (bf16[64,192]{1,0:T(8,128)(2,1)S(1)}, bf16[64,192]{1,0:T(8,128)(2,1)}, u32[]{:S(2)}) copy-start(bf16[64,192]{1,0:T(8,128)(2,1)} %constant.13.clone.refs_5_) | copy-start | bytes 73732
  3.2 23.3 %collective-permute-start.3 = (bf16[64,4224]{1,0:T(8,128)(2,1)S(1)}, bf16[64,4224]{1,0:T(8,128)(2,1)S(1)}, u32[]{:S(2)}, u32[]{:S(2)}) collective-permute-start(bf16[64,4224]{1,0:T(8,128)(2,1)S(1)} %shard_map.271.own_ref.refs_0_.refs_1_), channel_id=1, source_target_pairs={{0,112},{16,32},{32,16},{48,64},{64,48},{80,96},{96,80},{112,0},{1... | collective-permute-start | bytes 1622024 | tf_op jit(solution)/shard_map/ppermute | solution.py:287
  6.8 19.6 %collective-permute-start.2 = (bf16[64,4224]{1,0:T(8,128)(2,1)S(1)}, bf16[64,4224]{1,0:T(8,128)(2,1)}, u32[]{:S(2)}, u32[]{:S(2)}) collective-permute-start(bf16[64,4224]{1,0:T(8,128)(2,1)S(1)} %shard_map.271.own_ref.refs_0_.refs_1_), channel_id=1, source_target_pairs={{0,16},{16,0},{32,48},{48,32},{64,80},{80,64},{96,112},{112,96},{1... | collective-permute-start | bytes 1622024 | tf_op jit(solution)/shard_map/ppermute | solution.py:287
  6.8 26.2 %collective-permute-start.1 = (bf16[64,4224]{1,0:T(8,128)(2,1)S(1)}, bf16[64,4224]{1,0:T(8,128)(2,1)S(1)}, u32[]{:S(2)}, u32[]{:S(2)}) collective-permute-start(bf16[64,4224]{1,0:T(8,128)(2,1)S(1)} %shard_map.271.own_ref.refs_0_.refs_1_), channel_id=1, source_target_pairs={{0,1},{1,2},{2,3},{3,4},{4,5},{5,6},{6,7},{7,8},{8,9},{9,10},{10,1... | collective-permute-start | bytes 1622024 | tf_op jit(solution)/shard_map/ppermute | solution.py:287
  8.3 24.7 %collective-permute-start = (bf16[64,4224]{1,0:T(8,128)(2,1)S(1)}, bf16[64,4224]{1,0:T(8,128)(2,1)S(1)}, u32[]{:S(2)}, u32[]{:S(2)}) collective-permute-start(bf16[64,4224]{1,0:T(8,128)(2,1)S(1)} %shard_map.271.own_ref.refs_0_.refs_1_), channel_id=1, source_target_pairs={{0,15},{1,0},{2,1},{3,2},{4,3},{5,4},{6,5},{7,6},{8,7},{9,8},{10,9... | collective-permute-start | bytes 1622024 | tf_op jit(solution)/shard_map/ppermute | solution.py:287
  13.0 1.2 %copy-start.2 = (f32[33,64,128]{2,1,0:T(8,128)S(1)}, f32[33,64,128]{2,1,0:T(8,128)}, u32[]{:S(2)}) copy-start(f32[33,64,128]{2,1,0:T(8,128)} %constant.14.clone.refs_6_) | copy-start | bytes 3244036
  14.2 0.9 %copy-start.4 = (bf16[256,256]{1,0:T(8,128)(2,1)S(1)}, bf16[256,256]{1,0:T(8,128)(2,1)}, u32[]{:S(2)}) copy-start(bf16[256,256]{1,0:T(8,128)(2,1)} %constant.11.clone.refs_3_) | copy-start | bytes 393220
  15.1 0.9 %copy-start.6 = (bf16[256,256]{1,0:T(8,128)(2,1)S(1)}, bf16[256,256]{1,0:T(8,128)(2,1)}, u32[]{:S(2)}) copy-start(bf16[256,256]{1,0:T(8,128)(2,1)} %constant.10.clone.refs_2_) | copy-start | bytes 393220
  16.0 0.8 %copy-start.8 = (bf16[64,192]{1,0:T(8,128)(2,1)S(1)}, bf16[64,192]{1,0:T(8,128)(2,1)}, u32[]{:S(2)}) copy-start(bf16[64,192]{1,0:T(8,128)(2,1)} %constant.13.clone.refs_5_) | copy-start | bytes 73732
  16.8 0.8 %copy-start.10 = (bf16[64,192]{1,0:T(8,128)(2,1)S(1)}, bf16[64,192]{1,0:T(8,128)(2,1)}, u32[]{:S(2)}) copy-start(bf16[64,192]{1,0:T(8,128)(2,1)} %constant.12.clone.refs_4_) | copy-start | bytes 73732
  17.5 0.7 %copy-start.14 = (s32[8]{0:T(128)S(1)}, s32[8]{0:T(128)}, u32[]{:S(2)}) copy-start(s32[8]{0:T(128)} %pair_mask.11) | copy-start | bytes 100
  18.2 8.3 %copy-start.5 = (bf16[256,256]{1,0:T(8,128)(2,1)S(1)}, bf16[256,256]{1,0:T(8,128)(2,1)}, u32[]{:S(2)}) copy-start(bf16[256,256]{1,0:T(8,128)(2,1)} %constant.11.clone.refs_3_) | copy-start | bytes 393220
  18.2 8.3 %copy-start.7 = (bf16[256,256]{1,0:T(8,128)(2,1)S(1)}, bf16[256,256]{1,0:T(8,128)(2,1)}, u32[]{:S(2)}) copy-start(bf16[256,256]{1,0:T(8,128)(2,1)} %constant.10.clone.refs_2_) | copy-start | bytes 393220
  18.2 8.3 %copy-start.11 = (bf16[64,192]{1,0:T(8,128)(2,1)S(1)}, bf16[64,192]{1,0:T(8,128)(2,1)}, u32[]{:S(2)}) copy-start(bf16[64,192]{1,0:T(8,128)(2,1)} %constant.12.clone.refs_4_) | copy-start | bytes 73732
  25.1 1.3 %copy-start = (f32[4096,128]{1,0:T(8,128)}, f32[4096,128]{1,0:T(8,128)S(1)}, u32[]{:S(2)}) copy-start(f32[4096,128]{1,0:T(8,128)S(1)} %get-tuple-element.10.own_ref) | copy-start | bytes 6291460
  33.0 10.1 %collective-permute-start.6 = (bf16[64,4224]{1,0:T(8,128)(2,1)S(1)}, bf16[64,4224]{1,0:T(8,128)(2,1)S(1)}, u32[]{:S(2)}, u32[]{:S(2)}) collective-permute-start(bf16[64,4224]{1,0:T(8,128)(2,1)S(1)} %collective-permute-done.refs_0_), channel_id=1, source_target_pairs={{0,16},{16,0},{32,48},{48,32},{64,80},{80,64},{96,112},{112,96},{1... | collective-permute-start | bytes 1622024 | tf_op jit(solution)/shard_map/ppermute | solution.py:287
  33.3 9.9 %collective-permute-start.7 = (bf16[64,4224]{1,0:T(8,128)(2,1)S(1)}, bf16[64,4224]{1,0:T(8,128)(2,1)S(1)}, u32[]{:S(2)}, u32[]{:S(2)}) collective-permute-start(bf16[64,4224]{1,0:T(8,128)(2,1)S(1)} %collective-permute-done.1.refs_1_), channel_id=1, source_target_pairs={{0,16},{16,0},{32,48},{48,32},{64,80},{80,64},{96,112},{112,96},{1... | collective-permute-start | bytes 1622024 | tf_op jit(solution)/shard_map/ppermute | solution.py:287
  33.6 16.2 %collective-permute-start.4 = (bf16[64,4224]{1,0:T(8,128)(2,1)S(1)}, bf16[64,4224]{1,0:T(8,128)(2,1)S(1)}, u32[]{:S(2)}, u32[]{:S(2)}) collective-permute-start(bf16[64,4224]{1,0:T(8,128)(2,1)S(1)} %collective-permute-done.refs_0_), channel_id=1, source_target_pairs={{0,112},{16,32},{32,16},{48,64},{64,48},{80,96},{96,80},{112,0},{1... | collective-permute-start | bytes 1622024 | tf_op jit(solution)/shard_map/ppermute | solution.py:287
  34.1 15.8 %collective-permute-start.5 = (bf16[64,4224]{1,0:T(8,128)(2,1)S(1)}, bf16[64,4224]{1,0:T(8,128)(2,1)S(1)}, u32[]{:S(2)}, u32[]{:S(2)}) collective-permute-start(bf16[64,4224]{1,0:T(8,128)(2,1)S(1)} %collective-permute-done.1.refs_1_), channel_id=1, source_target_pairs={{0,112},{16,32},{32,16},{48,64},{64,48},{80,96},{96,80},{112,0},{1... | collective-permute-start | bytes 1622024 | tf_op jit(solution)/shard_map/ppermute | solution.py:287
  43.1 6.8 %copy-start.1 = (f32[4096,128]{1,0:T(8,128)S(1)}, f32[4096,128]{1,0:T(8,128)}, u32[]{:S(2)}) copy-start(f32[4096,128]{1,0:T(8,128)} %copy-done) | copy-start | bytes 6291460

commit v4 on v3

--- a/solution.py
+++ b/solution.py
@@ -13,6 +13,7 @@
 BOX = 64
 ROW = 96
 HOME = (0, 0)
+GREEN = (BOX // 2 + 1) * BOX
 MROW = 72
 CHUNK = 16
 THICK = 8
@@ -49,7 +50,11 @@
     some = (2.0 * np.pi / BOX * np.arange(BOX // 2 + 1)) ** 2
     total = some[:, None, None] + square[None, :, None] + np.concatenate([square, square])[None, None, :]
     green = (1.0 / (total + (8.0 * np.pi / BOX) ** 2)).astype(np.float32)
-    return right(basis.T), right(basis), left(basis), left(basis.T), green
+    blocks = [green.reshape(-1, 2 * BOX)]
+    for wide in (right(basis.T), right(basis), left(basis), left(basis.T)):
+        wide = np.pad(wide.astype(np.float32), ((0, 0), (0, 4 * BOX - wide.shape[1])))
+        blocks += [wide[:, : 2 * BOX], wide[:, 2 * BOX :]]
+    return np.concatenate(blocks, 0)
 
 
 def split(value):
@@ -67,7 +72,7 @@
 
 def target(pair_list, slot):
     size_x, size_y = lax.axis_size("dx"), lax.axis_size("dy")
-    owner = pair_list[slot, 1]
+    owner = pair_list[1, slot]
     rel_x = (owner // size_y - lax.axis_index("dx") + 1 + size_x) % size_x
     rel_y = (owner % size_y - lax.axis_index("dy") + 1 + size_y) % size_y
     return rel_x * 3 + rel_y
@@ -77,34 +82,48 @@
     size_x, size_y = lax.axis_size("dx"), lax.axis_size("dy")
     here_x, here_y = lax.axis_index("dx"), lax.axis_index("dy")
     if (i, j) == HOME:
-        return tuple(0 * offsets[0, c] for c in range(3)) + (4 + 0 * offsets[0, 0], 0 * offsets[0, 0])
+        return tuple(0 * offsets[c, 0] for c in range(3)) + (4 + 0 * offsets[0, 0], 0 * offsets[0, 0])
     step = i * (1 - 2 * (here_x % 2))
     other = (here_x + step + size_x) % size_x * size_y + (here_y + j + size_y) % size_y
     mine = here_x * size_y + here_y
-    move = tuple(offsets[mine, c] - offsets[other, c] for c in range(3))
+    move = tuple(offsets[c, mine] - offsets[c, other] for c in range(3))
     index = (1 + step) * 3 + 1 + j
-    count = sum(jnp.where(target(pair_list, n) == index, pair_mask[n], 0) for n in range(pair_list.shape[0]))
+    count = sum(jnp.where(target(pair_list, n) == index, pair_mask[n], 0) for n in range(pair_list.shape[1]))
     return move + (8 - index, count)
 
 
-def tail_kernel(pair_list, pair_mask, box, out):
+def tail_kernel(list_hbm, mask_hbm, box_hbm, out, pair_list, pair_mask, sems):
+    copies = [
+        pltpu.make_async_copy(box_hbm, out.at[:, pl.ds(0, BOX * BOX)], sems.at[0]),
+        pltpu.make_async_copy(list_hbm, pair_list, sems.at[1]),
+        pltpu.make_async_copy(mask_hbm, pair_mask, sems.at[2]),
+    ]
+    for copy in copies:
+        copy.start()
+    copies[1].wait()
+    copies[2].wait()
     lane = lax.broadcasted_iota(jnp.int32, (BOX, 2 * BOX), 1)
     counts = jnp.zeros((BOX, 2 * BOX), jnp.int32)
-    for n in range(pair_list.shape[0]):
+    for n in range(pair_list.shape[1]):
         counts += jnp.where(lane == target(pair_list, n), pair_mask[n], 0)
     out[:, pl.ds(BOX * BOX, 2 * BOX)] = counts.astype(F32).astype(BF16)
-    out[:, pl.ds(0, BOX * BOX)] = box[...]
-
-
-def kernel(places, offsets, pair_list, pair_mask, own_ref, *refs):
+    copies[0].wait()
+
+
+def kernel(places, last, offsets, pair_list, pair_mask, own_ref, *refs):
     pairs = len(places) // 2
-    near = refs[: 2 * pairs]
+    near, (tab_hbm, *refs) = refs[: 2 * pairs], refs[2 * pairs :]
+    acc_in = None
     if places[0] == HOME:
-        wz, wzi, rf, ri, green, out, own, held, mid, mid2 = refs[2 * pairs :]
-        acc_in = None
+        out, own, *refs = refs
     else:
-        wz, wzi, rf, ri, green, acc_in, out, held, mid, mid2 = refs[2 * pairs :]
+        acc_in, out, *refs = refs
         own = own_ref
+    if last:
+        out_hbm, (out, out_sem, *refs) = out, refs
+    held, mid, mid2, tab, wz, wzi, rf, ri, tab_sem = refs
+    tab_copy = pltpu.make_async_copy(tab_hbm, tab, tab_sem)
+    tab_copy.start()
     facts = [known(i, j, offsets, pair_list, pair_mask) for i, j in places]
     lanes = 2 * BOX
     low = lax.broadcasted_iota(jnp.int32, (BOX, lanes), 1) < BOX
@@ -129,6 +148,19 @@
 
     if places[0] == HOME:
         lax.fori_loop(0, BOX // 2, own_step, 0, unroll=4)
+
+    def out_copy(c):
+        at = pl.ds(c * CHUNK * BOX, CHUNK * BOX)
+        return pltpu.make_async_copy(out.at[:, at], out_hbm.at[:, at], out_sem.at[c])
+
+    def ready():
+        tab_copy.wait()
+        at = GREEN
+        for ref in (wz, wzi, rf, ri):
+            size, width = ref.shape
+            ref[:, pl.ds(0, lanes)] = tab[pl.ds(at, size), :].astype(BF16)
+            ref[:, pl.ds(lanes, width - lanes)] = tab[pl.ds(at + size, size), :][:, : width - lanes].astype(BF16)
+            at += 2 * size
 
     for p in range(pairs):
         a_ref, b_ref = near[2 * p], near[2 * p + 1]
@@ -195,6 +227,9 @@
 
                 skewed(BOX // CHUNK, first, second)
 
+            def green(k):
+                return tab[pl.ds(k * BOX, BOX), :]
+
             def middle():
                 def first(c):
                     waves = []
@@ -208,7 +243,7 @@
                     for j in range(0, CHUNK, 2):
                         k = c * CHUNK + j
                         base = k * MROW
-                        h, l = split(waves[j // 2] * stacked(green[(k + 1) // 2], green[(k + 2) // 2]))
+                        h, l = split(waves[j // 2] * stacked(green((k + 1) // 2), green((k + 2) // 2)))
                         v = dot(ri[...], jnp.concatenate([h, l, h], 0))
                         mid2[pl.ds(base, BOX), :] = v[:, :lanes]
                         mid2[pl.ds(base + MROW, BOX), :] = v[:, lanes:]
@@ -248,39 +283,57 @@
                         elif acc_in is not None:
                             both = acc_in[:, at] + both
                         out[:, at] = both
+                    if last and p == pairs - 1:
+                        out_copy(c).start()
 
                 skewed(BOX // CHUNK, first, second)
 
             load()
+            if p == 0:
+                ready()
             forward()
             middle()
             backward()
 
         solve()
 
+    if last:
+        for c in range(BOX // CHUNK):
+            out_copy(c).wait()
+
 
 SMEM = pl.BlockSpec(memory_space=pltpu.SMEM)
+HBM = pl.BlockSpec(memory_space=pltpu.HBM)
 VMEM = pl.BlockSpec(memory_space=pltpu.VMEM)
-PARAMS = pltpu.CompilerParams(vmem_limit_bytes=48 * 1024 * 1024)
-
-
-def exchange_terms(places, ints, own, boxes, *acc):
-    first = places[0] == HOME
+PARAMS = pltpu.CompilerParams(vmem_limit_bytes=28 * 1024 * 1024)
+
+
+def exchange_terms(places, ints, own, boxes, *acc, last=False):
+    lanes = 2 * BOX
     shape = [jax.ShapeDtypeStruct((BOX, BOX * BOX), F32)]
-    if first:
-        shape.append(jax.ShapeDtypeStruct((BOX * BOX, 2 * BOX), F32))
+    if places[0] == HOME:
+        shape.append(jax.ShapeDtypeStruct((BOX * BOX, lanes), F32))
+    sink = [pltpu.VMEM((BOX, BOX * BOX), F32), pltpu.SemaphoreType.DMA((BOX // CHUNK,))] if last else []
+    table = tables()
     return pl.pallas_call(
-        functools.partial(kernel, places),
+        functools.partial(kernel, places, last),
         out_shape=shape,
-        in_specs=[SMEM] * 3 + [VMEM] * (len(boxes) + 6 + len(acc)),
-        out_specs=[VMEM] * len(shape),
-        scratch_shapes=[
-            pltpu.VMEM(((BOX + 1) * ROW + 32, 2 * BOX), F32),
-            pltpu.VMEM((BOX * MROW, 2 * BOX), F32),
-            pltpu.VMEM((BOX * MROW, 2 * BOX), F32),
+        in_specs=[SMEM] * 3 + [VMEM] * (1 + len(boxes)) + [HBM] + [VMEM] * len(acc),
+        out_specs=[HBM if last else VMEM] * len(shape),
+        scratch_shapes=sink
+        + [
+            pltpu.VMEM(((BOX + 1) * ROW + 32, lanes), F32),
+            pltpu.VMEM((BOX * MROW, lanes), F32),
+            pltpu.VMEM((BOX * MROW, lanes), F32),
+            pltpu.VMEM(table.shape, F32),
+            pltpu.VMEM((2 * lanes, 2 * lanes), BF16),
+            pltpu.VMEM((2 * lanes, 2 * lanes), BF16),
+            pltpu.VMEM((BOX, 3 * BOX), BF16),
+            pltpu.VMEM((BOX, 3 * BOX), BF16),
+            pltpu.SemaphoreType.DMA,
         ],
         compiler_params=PARAMS,
-    )(*ints, own, *boxes, *tables(), *acc)
+    )(*ints, own, *boxes, table, *acc)
 
 
 def along(value, axis, to):
@@ -289,14 +342,19 @@
 
 def body(orbitals, offsets, pair_list, pair_mask):
     size_x, size_y = lax.axis_size("dx"), lax.axis_size("dy")
-    ints = (offsets, pair_list, pair_mask)
+    ints = (offsets.T, pair_list.T, pair_mask)
     own = pl.pallas_call(
         tail_kernel,
         out_shape=jax.ShapeDtypeStruct((BOX, BOX * BOX + 2 * BOX), BF16),
-        in_specs=[SMEM, SMEM, VMEM],
+        in_specs=[HBM] * 3,
         out_specs=VMEM,
+        scratch_shapes=[
+            pltpu.SMEM(ints[1].shape, jnp.int32),
+            pltpu.SMEM(pair_mask.shape, jnp.int32),
+            pltpu.SemaphoreType.DMA((3,)),
+        ],
         compiler_params=PARAMS,
-    )(pair_list, pair_mask, orbitals[0])
+    )(ints[1], pair_mask, orbitals[0])
 
     def inner(i):
         return i ^ 1
@@ -313,7 +371,7 @@
     corners = [along(v, "dx", to) for to in (inner, outer) for v in (y_next, y_last)]
     (acc,) = exchange_terms(((0, 1), (0, -1)), ints, wide, (y_next, y_last), acc)
     (acc,) = exchange_terms(((1, 1), (1, -1)), ints, wide, corners[:2], acc)
-    (acc,) = exchange_terms(((-1, 1), (-1, -1)), ints, wide, corners[2:], acc)
+    (acc,) = exchange_terms(((-1, 1), (-1, -1)), ints, wide, corners[2:], acc, last=True)
     return acc[None]
 
 

time: 58.1 us -> 50.4 us (0.87)
  local copies, waits for them, and re-layouts: 9.78 us -> 4.53 us
  Pallas kernels: 35 us -> 32 us
  waiting for transfers between devices: 0.02 us -> 0.84 us
    unnamed x32 -> x14, local copies, waits for them, and re-layouts: 9.78 us -> 4.53 us
    pallas_call x5, Pallas kernels: 34.3 us -> 31.2 us  [exchange_terms(): pl.pallas_call(functools.partial(kernel, places, last), out_shape=shape,...]
    ppermute x8, waiting for transfers between devices: 0.02 us -> 0.84 us  [along(): lax.ppermute(value, axis, [(i, to(i)) for i in range(lax.axis_size(axis))])]
  transfers between devices with their start and end apart: 8 -> 8, of which waited for: 0 -> 1; matrix products, arithmetic and copies ran while one was open for 1% -> 0% of each run, Pallas kernels for 46% -> 48%
where the time goes in v4:
time: 50.4 us; the launch traced here: 50.2 us
  Pallas kernels  32 us (63%)
  starting transfers between devices  12.5 us (25%)
  local copies, waits for them, and re-layouts  4.53 us (9%)
  waiting for transfers between devices  0.84 us (2%)
    pallas_call x5, Pallas kernels, exchange_terms(): pl.pallas_call(functools.partial(kernel, places, last), out_shape=shape,...  31.2 us
    ppermute x8, starting transfers between devices, along(): lax.ppermute(value, axis, [(i, to(i)) for i in range(lax.axis_size(axis))])  12.5 us
    unnamed x14, local copies, waits for them, and re-layouts  4.53 us
  transfers between devices with their start and end apart: 8, of which 1 were waited for; matrix products, arithmetic and copies ran while one was open for 0% of the time, Pallas kernels for 48%

profile of v4, /device:TPU:0, one launch (start us, length us, event | category | flops | bytes accessed | tf_op | source)
XLA Modules:
  0.0 50.2 jit_solution(13218700741930199839)
XLA Ops:
  0.0 0.0 copy-start.2
  0.0 1.0 %copy-done.2 = bf16[1,64,4096]{2,1,0:T(8,128)(2,1)S(1)} copy-done((bf16[1,64,4096]{2,1,0:T(8,128)(2,1)S(1)}, bf16[1,64,4096]{2,1,0:T(8,128)(2,1)}, u32[]{:S(2)}) %copy-start.2) | copy-done | bytes 524312
  1.0 0.0 copy-start.5
  1.0 0.7 %copy-done.5 = s32[8,2]{0,1:T(2,128)S(1)} copy-done((s32[8,2]{0,1:T(2,128)S(1)}, s32[8,2]{0,1:T(2,128)}, u32[]{:S(2)}) %copy-start.5) | copy-done | bytes 88
  1.7 0.0 copy-start.6
  1.7 0.7 %copy-done.6 = s32[8]{0:T(128)S(1)} copy-done((s32[8]{0:T(128)S(1)}, s32[8]{0:T(128)}, u32[]{:S(2)}) %copy-start.6) | copy-done | bytes 56
  2.4 0.7 %shard_map.91.own_ref.refs_0_.refs_1_ = bf16[64,4224]{1,0:T(8,128)(2,1)S(1)} custom-call(s32[2,8]{1,0:T(2,128)S(1)} %bitcast.10, s32[8]{0:T(128)S(1)} %copy-done.6, bf16[64,4096]{1,0:T(8,128)(2,1)S(1)} %bitcast.4), custom_call_target="tpu_custom_call" | custom-call | tf_op jit(solution)/shard_map/pallas_call | solution.py:346
  3.1 3.6 %collective-permute-start.3 = (bf16[64,4224]{1,0:T(8,128)(2,1)S(1)}, bf16[64,4224]{1,0:T(8,128)(2,1)S(1)}, u32[]{:S(2)}, u32[]{:S(2)}) collective-permute-start(bf16[64,4224]{1,0:T(8,128)(2,1)S(1)} %shard_map.91.own_ref.refs_0_.refs_1_), channel_id=1, source_target_pairs={{0,112},{16,32},{32,16},{48,64},{64,48},{80,96},{96,80},{112,0},{1... | collective-permute-start | bytes 1622024 | tf_op jit(solution)/shard_map/ppermute | solution.py:340
  6.8 0.0 collective-permute-start.2
  6.8 1.5 %collective-permute-start.1 = (bf16[64,4224]{1,0:T(8,128)(2,1)S(1)}, bf16[64,4224]{1,0:T(8,128)(2,1)S(1)}, u32[]{:S(2)}, u32[]{:S(2)}) collective-permute-start(bf16[64,4224]{1,0:T(8,128)(2,1)S(1)} %shard_map.91.own_ref.refs_0_.refs_1_), channel_id=1, source_target_pairs={{0,1},{1,2},{2,3},{3,4},{4,5},{5,6},{6,7},{7,8},{8,9},{9,10},{10,1... | collective-permute-start | bytes 1622024 | tf_op jit(solution)/shard_map/ppermute | solution.py:340
  8.2 3.9 %collective-permute-start = (bf16[64,4224]{1,0:T(8,128)(2,1)S(1)}, bf16[64,4224]{1,0:T(8,128)(2,1)S(1)}, u32[]{:S(2)}, u32[]{:S(2)}) collective-permute-start(bf16[64,4224]{1,0:T(8,128)(2,1)S(1)} %shard_map.91.own_ref.refs_0_.refs_1_), channel_id=1, source_target_pairs={{0,15},{1,0},{2,1},{3,2},{4,3},{5,4},{6,5},{7,6},{8,7},{9,8},{10,9... | collective-permute-start | bytes 1622024 | tf_op jit(solution)/shard_map/ppermute | solution.py:340
  12.1 0.0 copy-start
  12.1 1.5 %copy-done = f32[3392,128]{1,0:T(8,128)S(1)} copy-done((f32[3392,128]{1,0:T(8,128)S(1)}, f32[3392,128]{1,0:T(8,128)}, u32[]{:S(2)}) %copy-start) | copy-done | bytes 1736728
  13.6 0.0 copy-start.3
  13.6 0.7 %copy-done.3 = s32[128,3]{0,1:T(4,128)S(1)} copy-done((s32[128,3]{0,1:T(4,128)S(1)}, s32[128,3]{0,1:T(4,128)}, u32[]{:S(2)}) %copy-start.3) | copy-done | bytes 1560
  14.3 0.0 copy-start.1
  14.3 6.2 %shard_map.92 = (f32[64,4096]{1,0:T(8,128)S(1)}, f32[4096,128]{1,0:T(8,128)S(1)}) custom-call(s32[3,128]{1,0:T(4,128)S(1)} %bitcast.5, s32[2,8]{1,0:T(2,128)S(1)} %bitcast.11, s32[8]{0:T(128)S(1)} %copy-done.6, bf16[64,4224]{1,0:T(8,128)(2,1)S(1)} %shard_map.91.own_ref.refs_0_.refs_1_, bf16[64,4224]{1,0:T(8,128)(2,1)S(1)} %shard_map.91.own_ref.refs_0_.refs_1_, ...), custom_call_target="tpu_custom_call" | custom-call | tf_op jit(solution)/shard_map/pallas_call | solution.py:318
  20.5 0.0 collective-permute-done.3.refs_1_
  20.5 0.0 collective-permute-done.2.refs_0_
  20.5 0.0 copy-done.1
  20.5 6.0 %shard_map.93.refs_3_ = f32[64,4096]{1,0:T(8,128)S(1)} custom-call(s32[3,128]{1,0:T(4,128)S(1)} %bitcast.6, s32[2,8]{1,0:T(2,128)S(1)} %bitcast.12, s32[8]{0:T(128)S(1)} %copy-done.6, f32[4096,128]{1,0:T(8,128)S(1)} %get-tuple-element.10.own_ref, bf16[64,4224]{1,0:T(8,128)(2,1)S(1)} %collective-permute-done.2.refs_0_, ...), custom_call_target="tpu_custom_call" | custom-call | tf_op jit(solution)/shard_map/pallas_call | solution.py:318
  26.6 0.0 copy-start.4
  26.6 0.0 collective-permute-done.1.refs_1_
  26.6 0.0 collective-permute-done.refs_0_
  26.6 0.1 collective-permute-start.6
  26.8 0.4 collective-permute-start.7
  27.2 0.4 collective-permute-start.4
  27.6 2.6 %collective-permute-start.5 = (bf16[64,4224]{1,0:T(8,128)(2,1)S(1)}, bf16[64,4224]{1,0:T(8,128)(2,1)S(1)}, u32[]{:S(2)}, u32[]{:S(2)}) collective-permute-start(bf16[64,4224]{1,0:T(8,128)(2,1)S(1)} %collective-permute-done.1.refs_1_), channel_id=1, source_target_pairs={{0,112},{16,32},{32,16},{48,64},{64,48},{80,96},{96,80},{112,0},{1... | collective-permute-start | bytes 1622024 | tf_op jit(solution)/shard_map/ppermute | solution.py:340
  30.2 6.0 %shard_map.94.refs_3_ = f32[64,4096]{1,0:T(8,128)S(1)} custom-call(s32[3,128]{1,0:T(4,128)S(1)} %bitcast.7, s32[2,8]{1,0:T(2,128)S(1)} %bitcast.13, s32[8]{0:T(128)S(1)} %copy-done.6, f32[4096,128]{1,0:T(8,128)S(1)} %get-tuple-element.10.own_ref, bf16[64,4224]{1,0:T(8,128)(2,1)S(1)} %collective-permute-done.refs_0_, ...), custom_call_target="tpu_custom_call" | custom-call | tf_op jit(solution)/shard_map/pallas_call | solution.py:318
  36.2 0.0 collective-permute-done.6.refs_0_
  36.2 0.0 collective-permute-done.7.refs_1_
  36.2 0.0 copy-done.4
  36.2 6.0 %shard_map.95.refs_3_ = f32[64,4096]{1,0:T(8,128)S(1)} custom-call(s32[3,128]{1,0:T(4,128)S(1)} %bitcast.8, s32[2,8]{1,0:T(2,128)S(1)} %bitcast.14, s32[8]{0:T(128)S(1)} %copy-done.6, f32[4096,128]{1,0:T(8,128)S(1)} %get-tuple-element.10.own_ref, bf16[64,4224]{1,0:T(8,128)(2,1)S(1)} %collective-permute-done.6.refs_0_, ...), custom_call_target="tpu_custom_call" | custom-call | tf_op jit(solution)/shard_map/pallas_call | solution.py:318
  42.2 0.0 collective-permute-done.4.refs_0_
  42.2 0.8 %collective-permute-done.5.refs_1_ = bf16[64,4224]{1,0:T(8,128)(2,1)S(1)} collective-permute-done((bf16[64,4224]{1,0:T(8,128)(2,1)S(1)}, bf16[64,4224]{1,0:T(8,128)(2,1)S(1)}, u32[]{:S(2)}, u32[]{:S(2)}) %collective-permute-start.5) | collective-permute-done | bytes 540704 | tf_op jit(solution)/shard_map/ppermute | solution.py:340
  43.0 7.0 %shard_map.96 = f32[64,4096]{1,0:T(8,128)} custom-call(s32[3,128]{1,0:T(4,128)S(1)} %bitcast.9, s32[2,8]{1,0:T(2,128)S(1)} %bitcast.15, s32[8]{0:T(128)S(1)} %copy-done.6, f32[4096,128]{1,0:T(8,128)S(1)} %get-tuple-element.10.own_ref, bf16[64,4224]{1,0:T(8,128)(2,1)S(1)} %collective-permute-done.4.refs_0_, ...), custom_call_target="tpu_custom_call" | custom-call | tf_op jit(solution)/shard_map/pallas_call | solution.py:318
Async XLA Ops:
  0.0 1.0 %copy-start.2 = (bf16[1,64,4096]{2,1,0:T(8,128)(2,1)S(1)}, bf16[1,64,4096]{2,1,0:T(8,128)(2,1)}, u32[]{:S(2)}) copy-start(bf16[1,64,4096]{2,1,0:T(8,128)(2,1)} %param.9) | copy-start | bytes 1572868
  1.0 0.7 %copy-start.5 = (s32[8,2]{0,1:T(2,128)S(1)}, s32[8,2]{0,1:T(2,128)}, u32[]{:S(2)}) copy-start(s32[8,2]{0,1:T(2,128)} %param.11) | copy-start | bytes 196
  1.7 0.7 %copy-start.6 = (s32[8]{0:T(128)S(1)}, s32[8]{0:T(128)}, u32[]{:S(2)}) copy-start(s32[8]{0:T(128)} %pair_mask.9) | copy-start | bytes 100
  3.1 17.4 %collective-permute-start.3 = (bf16[64,4224]{1,0:T(8,128)(2,1)S(1)}, bf16[64,4224]{1,0:T(8,128)(2,1)S(1)}, u32[]{:S(2)}, u32[]{:S(2)}) collective-permute-start(bf16[64,4224]{1,0:T(8,128)(2,1)S(1)} %shard_map.91.own_ref.refs_0_.refs_1_), channel_id=1, source_target_pairs={{0,112},{16,32},{32,16},{48,64},{64,48},{80,96},{96,80},{112,0},{1... | collective-permute-start | bytes 1622024 | tf_op jit(solution)/shard_map/ppermute | solution.py:340
  6.8 13.8 %collective-permute-start.2 = (bf16[64,4224]{1,0:T(8,128)(2,1)S(1)}, bf16[64,4224]{1,0:T(8,128)(2,1)S(1)}, u32[]{:S(2)}, u32[]{:S(2)}) collective-permute-start(bf16[64,4224]{1,0:T(8,128)(2,1)S(1)} %shard_map.91.own_ref.refs_0_.refs_1_), channel_id=1, source_target_pairs={{0,16},{16,0},{32,48},{48,32},{64,80},{80,64},{96,112},{112,96},{1... | collective-permute-start | bytes 1622024 | tf_op jit(solution)/shard_map/ppermute | solution.py:340
  6.8 19.8 %collective-permute-start.1 = (bf16[64,4224]{1,0:T(8,128)(2,1)S(1)}, bf16[64,4224]{1,0:T(8,128)(2,1)S(1)}, u32[]{:S(2)}, u32[]{:S(2)}) collective-permute-start(bf16[64,4224]{1,0:T(8,128)(2,1)S(1)} %shard_map.91.own_ref.refs_0_.refs_1_), channel_id=1, source_target_pairs={{0,1},{1,2},{2,3},{3,4},{4,5},{5,6},{6,7},{7,8},{8,9},{9,10},{10,1... | collective-permute-start | bytes 1622024 | tf_op jit(solution)/shard_map/ppermute | solution.py:340
  8.2 18.4 %collective-permute-start = (bf16[64,4224]{1,0:T(8,128)(2,1)S(1)}, bf16[64,4224]{1,0:T(8,128)(2,1)S(1)}, u32[]{:S(2)}, u32[]{:S(2)}) collective-permute-start(bf16[64,4224]{1,0:T(8,128)(2,1)S(1)} %shard_map.91.own_ref.refs_0_.refs_1_), channel_id=1, source_target_pairs={{0,15},{1,0},{2,1},{3,2},{4,3},{5,4},{6,5},{7,6},{8,7},{9,8},{10,9... | collective-permute-start | bytes 1622024 | tf_op jit(solution)/shard_map/ppermute | solution.py:340
  12.1 1.5 %copy-start = (f32[3392,128]{1,0:T(8,128)S(1)}, f32[3392,128]{1,0:T(8,128)}, u32[]{:S(2)}) copy-start(f32[3392,128]{1,0:T(8,128)} %constant.2.clone.refs_2_) | copy-start | bytes 5210116
  13.6 0.7 %copy-start.3 = (s32[128,3]{0,1:T(4,128)S(1)}, s32[128,3]{0,1:T(4,128)}, u32[]{:S(2)}) copy-start(s32[128,3]{0,1:T(4,128)} %param.10) | copy-start | bytes 4612
  14.3 6.3 %copy-start.1 = (f32[3392,128]{1,0:T(8,128)S(1)}, f32[3392,128]{1,0:T(8,128)}, u32[]{:S(2)}) copy-start(f32[3392,128]{1,0:T(8,128)} %constant.2.clone.refs_2_) | copy-start | bytes 5210116
  26.6 9.6 %copy-start.4 = (s32[128,3]{0,1:T(4,128)S(1)}, s32[128,3]{0,1:T(4,128)}, u32[]{:S(2)}) copy-start(s32[128,3]{0,1:T(4,128)} %param.10) | copy-start | bytes 4612
  26.6 9.5 %collective-permute-start.6 = (bf16[64,4224]{1,0:T(8,128)(2,1)S(1)}, bf16[64,4224]{1,0:T(8,128)(2,1)S(1)}, u32[]{:S(2)}, u32[]{:S(2)}) collective-permute-start(bf16[64,4224]{1,0:T(8,128)(2,1)S(1)} %collective-permute-done.refs_0_), channel_id=1, source_target_pairs={{0,16},{16,0},{32,48},{48,32},{64,80},{80,64},{96,112},{112,96},{1... | collective-permute-start | bytes 1622024 | tf_op jit(solution)/shard_map/ppermute | solution.py:340
  26.8 9.4 %collective-permute-start.7 = (bf16[64,4224]{1,0:T(8,128)(2,1)S(1)}, bf16[64,4224]{1,0:T(8,128)(2,1)S(1)}, u32[]{:S(2)}, u32[]{:S(2)}) collective-permute-start(bf16[64,4224]{1,0:T(8,128)(2,1)S(1)} %collective-permute-done.1.refs_1_), channel_id=1, source_target_pairs={{0,16},{16,0},{32,48},{48,32},{64,80},{80,64},{96,112},{112,96},{1... | collective-permute-start | bytes 1622024 | tf_op jit(solution)/shard_map/ppermute | solution.py:340
  27.2 15.0 %collective-permute-start.4 = (bf16[64,4224]{1,0:T(8,128)(2,1)S(1)}, bf16[64,4224]{1,0:T(8,128)(2,1)S(1)}, u32[]{:S(2)}, u32[]{:S(2)}) collective-permute-start(bf16[64,4224]{1,0:T(8,128)(2,1)S(1)} %collective-permute-done.refs_0_), channel_id=1, source_target_pairs={{0,112},{16,32},{32,16},{48,64},{64,48},{80,96},{96,80},{112,0},{1... | collective-permute-start | bytes 1622024 | tf_op jit(solution)/shard_map/ppermute | solution.py:340
  27.6 15.4 %collective-permute-start.5 = (bf16[64,4224]{1,0:T(8,128)(2,1)S(1)}, bf16[64,4224]{1,0:T(8,128)(2,1)S(1)}, u32[]{:S(2)}, u32[]{:S(2)}) collective-permute-start(bf16[64,4224]{1,0:T(8,128)(2,1)S(1)} %collective-permute-done.1.refs_1_), channel_id=1, source_target_pairs={{0,112},{16,32},{32,16},{48,64},{64,48},{80,96},{96,80},{112,0},{1... | collective-permute-start | bytes 1622024 | tf_op jit(solution)/shard_map/ppermute | solution.py:340

commit v5 on v4

--- a/solution.py
+++ b/solution.py
@@ -12,9 +12,9 @@
 
 BOX = 64
 ROW = 96
-HOME = (0, 0)
 GREEN = (BOX // 2 + 1) * BOX
 MROW = 72
+HROW = 40
 CHUNK = 16
 THICK = 8
 F32 = jnp.float32
@@ -50,11 +50,21 @@
     some = (2.0 * np.pi / BOX * np.arange(BOX // 2 + 1)) ** 2
     total = some[:, None, None] + square[None, :, None] + np.concatenate([square, square])[None, None, :]
     green = (1.0 / (total + (8.0 * np.pi / BOX) ** 2)).astype(np.float32)
-    blocks = [green.reshape(-1, 2 * BOX)]
-    for wide in (right(basis.T), right(basis), left(basis), left(basis.T)):
-        wide = np.pad(wide.astype(np.float32), ((0, 0), (0, 4 * BOX - wide.shape[1])))
-        blocks += [wide[:, : 2 * BOX], wide[:, 2 * BOX :]]
-    return np.concatenate(blocks, 0)
+    def packed(first, *tables):
+        blocks = [first.reshape(-1, 2 * BOX)]
+        for wide in tables:
+            wide = np.pad(wide.astype(np.float32), ((0, 0), (0, 4 * BOX - wide.shape[1])))
+            blocks += [wide[:, : 2 * BOX], wide[:, 2 * BOX :]]
+        return np.concatenate(blocks, 0)
+
+    four = (right(basis.T), right(basis), left(basis), left(basis.T))
+    even = [m for m in range(BOX) if (m + 1) // 2 % 2 == 0]
+    odd = [m for m in range(BOX) if (m + 1) // 2 % 2 == 1]
+    half = BOX // 2
+    there = np.concatenate([basis[even, :half], basis[odd, :half]], 0)
+    back = np.concatenate([basis[even, :half].T, basis[odd, :half].T], 0)
+    halved = np.concatenate([green[:, even, :BOX], green[:, odd, :BOX]], 2)
+    return green.reshape(-1, 2 * BOX), packed(halved, *four, left(there), left(back))
 
 
 def split(value):
@@ -81,8 +91,6 @@
 def known(i, j, offsets, pair_list, pair_mask):
     size_x, size_y = lax.axis_size("dx"), lax.axis_size("dy")
     here_x, here_y = lax.axis_index("dx"), lax.axis_index("dy")
-    if (i, j) == HOME:
-        return tuple(0 * offsets[c, 0] for c in range(3)) + (4 + 0 * offsets[0, 0], 0 * offsets[0, 0])
     step = i * (1 - 2 * (here_x % 2))
     other = (here_x + step + size_x) % size_x * size_y + (here_y + j + size_y) % size_y
     mine = here_x * size_y + here_y
@@ -90,6 +98,131 @@
     index = (1 + step) * 3 + 1 + j
     count = sum(jnp.where(target(pair_list, n) == index, pair_mask[n], 0) for n in range(pair_list.shape[1]))
     return move + (8 - index, count)
+
+
+def unpack(tab, at, refs):
+    lanes = 2 * BOX
+    for ref in refs:
+        size, width = ref.shape
+        first = min(width, lanes)
+        ref[:, pl.ds(0, first)] = tab[pl.ds(at, size), :][:, :first].astype(BF16)
+        if width > lanes:
+            ref[:, pl.ds(lanes, width - lanes)] = tab[pl.ds(at + size, size), :][:, : width - lanes].astype(BF16)
+        at += 2 * size
+
+
+def skewed(count, first, second):
+    before = None
+    for c in range(count):
+        now = first(c)
+        if before is not None:
+            second(c - 1, before)
+        before = now
+    second(count - 1, before)
+
+
+def three(value):
+    high, rest = split(value)
+    return jnp.concatenate([high, rest, high], 0)
+
+
+def alone_kernel(own_ref, tab_hbm, green_hbm, out, own, green, wz, wzi, rf, ri, held, mid, mid2, tab, there, back, sems):
+    tab_copy = pltpu.make_async_copy(tab_hbm, tab, sems.at[0])
+    tab_copy.start()
+    green_copy = pltpu.make_async_copy(green_hbm, green, sems.at[1])
+    green_copy.start()
+    lanes, half = 2 * BOX, BOX // 2
+    low = lax.broadcasted_iota(jnp.int32, (BOX, lanes), 1) < BOX
+    few = low[:half]
+    sign = jnp.where(few, 1.0, -1.0)
+
+    def turned(value):
+        return pltpu.roll(value, BOX, 1)
+
+    for t in range(half // 2):
+        v = own_ref[:, pl.ds(t * lanes, lanes)].astype(F32)
+        w = own_ref[:, pl.ds((t + half // 2) * lanes, lanes)].astype(F32)
+        tv, tw = turned(v), turned(w)
+        for y, value in ((2 * t, jnp.where(low, v, tv)), (2 * t + 1, jnp.where(low, tv, v))):
+            own[pl.ds(y * BOX, BOX), :] = value
+        for y, value in ((2 * t, jnp.where(low, w, tw)), (2 * t + 1, jnp.where(low, tw, w))):
+            own[pl.ds((y + half) * BOX, BOX), :] = value
+        held[pl.ds(2 * t * BOX, BOX), :] = jnp.where(low, v, tw)
+        held[pl.ds((2 * t + 1) * BOX, BOX), :] = jnp.where(low, tv, w)
+
+    tab_copy.wait()
+    unpack(tab, GREEN // 2, (wz, wzi, rf, ri, there, back))
+
+    def forward_first(c):
+        rows = []
+        for y in range(c * CHUNK, (c + 1) * CHUNK):
+            v = held[pl.ds(y * BOX, BOX), :]
+            rows.append(stacked(*split(v * v)))
+        return dot(jnp.concatenate(rows, 0), wz[...])
+
+    def forward_second(c, wave):
+        wave = wave[:, :lanes] + wave[:, lanes:]
+        for j in range(0, CHUNK, 2):
+            y, at = c * CHUNK + j, j * BOX
+            u = dot(rf[...], three(stacked(wave[at : at + BOX], wave[at + BOX : at + 2 * BOX])))
+            mid[pl.ds(y, BOX, stride=HROW), :] = u[:, :lanes]
+            mid[pl.ds(y + 1, BOX, stride=HROW), :] = u[:, lanes:]
+
+    skewed(half // CHUNK, forward_first, forward_second)
+
+    def crossed(value):
+        return value * sign + turned(value)
+
+    def chosen(value):
+        return [jnp.where(few, value[:half, at : at + lanes], value[half:, at : at + lanes]) for at in (0, lanes)]
+
+    def middle_first(c):
+        waves = []
+        for k in range(c * CHUNK, (c + 1) * CHUNK, 2):
+            parts = [crossed(mid[pl.ds((k + q) * HROW, half), :]) for q in range(2)]
+            waves.append(dot(there[...], three(stacked(*parts))))
+        return waves
+
+    def middle_second(c, waves):
+        for j, wave in enumerate(waves):
+            k = c * CHUNK + 2 * j
+            parts = [v * tab[pl.ds((k + q + 1) // 2 * half, half), :] for q, v in enumerate(chosen(wave))]
+            wave = dot(back[...], three(stacked(*parts)))
+            for q, v in enumerate(chosen(wave)):
+                mid2[pl.ds((k + q) * HROW, half), :] = crossed(v)
+
+    skewed(BOX // CHUNK, middle_first, middle_second)
+
+    tail = own_ref[pl.ds(0, 16), pl.ds(BOX * BOX, lanes)].astype(F32)[:8]
+    at_lane = lax.broadcasted_iota(jnp.int32, (8, lanes), 1)
+    weight = 2.0 * jnp.sum(jnp.where(at_lane == 4, tail, 0.0), axis=1, keepdims=True)[:1]
+
+    def backward_first(c):
+        waves = []
+        for y in range(c * CHUNK, (c + 1) * CHUNK, 2):
+            v = stacked(mid2[pl.ds(y, BOX, stride=HROW), :], mid2[pl.ds(y + 1, BOX, stride=HROW), :])
+            waves.append(dot(ri[...], three(v)))
+        return waves
+
+    def backward_second(c, waves):
+        rows = []
+        for u in waves:
+            high, rest = split(u)
+            rows.append(stacked(high[:, :lanes], rest[:, :lanes]))
+            rows.append(stacked(high[:, lanes:], rest[:, lanes:]))
+        wave = dot(jnp.concatenate(rows, 0), wzi[...])
+        field = wave[:, :lanes] + wave[:, lanes:]
+        for j in range(0, CHUNK, 2):
+            y = c * CHUNK + j
+            v, w = [
+                field[(j + q) * BOX : (j + q + 1) * BOX] * (held[pl.ds((y + q) * BOX, BOX), :] * weight)
+                for q in range(2)
+            ]
+            out[:, pl.ds(y * BOX, lanes)] = jnp.where(low, v, turned(w))
+            out[:, pl.ds((y + half) * BOX, lanes)] = jnp.where(low, turned(v), w)
+
+    skewed(half // CHUNK, backward_first, backward_second)
+    green_copy.wait()
 
 
 def tail_kernel(list_hbm, mask_hbm, box_hbm, out, pair_list, pair_mask, sems):
@@ -112,18 +245,12 @@
 
 def kernel(places, last, offsets, pair_list, pair_mask, own_ref, *refs):
     pairs = len(places) // 2
-    near, (tab_hbm, *refs) = refs[: 2 * pairs], refs[2 * pairs :]
-    acc_in = None
-    if places[0] == HOME:
-        out, own, *refs = refs
-    else:
-        acc_in, out, *refs = refs
-        own = own_ref
+    near, refs = refs[: 2 * pairs], refs[2 * pairs :]
+    own = own_ref
+    tab, wz, wzi, rf, ri, acc_in, out, *refs = refs
     if last:
         out_hbm, (out, out_sem, *refs) = out, refs
-    held, mid, mid2, tab, wz, wzi, rf, ri, tab_sem = refs
-    tab_copy = pltpu.make_async_copy(tab_hbm, tab, tab_sem)
-    tab_copy.start()
+    held, mid, mid2 = refs
     facts = [known(i, j, offsets, pair_list, pair_mask) for i, j in places]
     lanes = 2 * BOX
     low = lax.broadcasted_iota(jnp.int32, (BOX, lanes), 1) < BOX
@@ -138,29 +265,9 @@
         held[pl.ds(y * ROW, ROW - BOX), :] = jnp.zeros((ROW - BOX, lanes), F32)
     held[pl.ds(BOX * ROW, ROW + 32), :] = jnp.zeros((ROW + 32, lanes), F32)
 
-    def own_step(t, _):
-        v = own_ref[:, pl.ds(pl.multiple_of(t * lanes, lanes), lanes)].astype(F32)
-        r = pltpu.roll(v, BOX, 1)
-        base = pl.multiple_of(t * lanes, lanes)
-        own[pl.ds(base, BOX), :] = jnp.where(low, v, r)
-        own[pl.ds(base + BOX, BOX), :] = jnp.where(low, r, v)
-        return 0
-
-    if places[0] == HOME:
-        lax.fori_loop(0, BOX // 2, own_step, 0, unroll=4)
-
     def out_copy(c):
         at = pl.ds(c * CHUNK * BOX, CHUNK * BOX)
         return pltpu.make_async_copy(out.at[:, at], out_hbm.at[:, at], out_sem.at[c])
-
-    def ready():
-        tab_copy.wait()
-        at = GREEN
-        for ref in (wz, wzi, rf, ri):
-            size, width = ref.shape
-            ref[:, pl.ds(0, lanes)] = tab[pl.ds(at, size), :].astype(BF16)
-            ref[:, pl.ds(lanes, width - lanes)] = tab[pl.ds(at + size, size), :][:, : width - lanes].astype(BF16)
-            at += 2 * size
 
     for p in range(pairs):
         a_ref, b_ref = near[2 * p], near[2 * p + 1]
@@ -196,15 +303,6 @@
                     block = jnp.where((from_y >= 0) & (from_y < BOX), from_y, BOX)
                     parts.append(held[pl.ds(block * ROW + (ROW - BOX) + sx[h], BOX), :])
                 return jnp.where(low, parts[0], parts[1])
-
-            def skewed(count, first, second):
-                before = None
-                for c in range(count):
-                    now = first(c)
-                    if before is not None:
-                        second(c - 1, before)
-                    before = now
-                second(count - 1, before)
 
             def forward():
                 def first(c):
@@ -280,7 +378,7 @@
                         both = jnp.where(low, parts[0], parts[1])
                         if p > 0:
                             both = out[:, at] + both
-                        elif acc_in is not None:
+                        else:
                             both = acc_in[:, at] + both
                         out[:, at] = both
                     if last and p == pairs - 1:
@@ -289,8 +387,6 @@
                 skewed(BOX // CHUNK, first, second)
 
             load()
-            if p == 0:
-                ready()
             forward()
             middle()
             backward()
@@ -308,32 +404,42 @@
 PARAMS = pltpu.CompilerParams(vmem_limit_bytes=28 * 1024 * 1024)
 
 
-def exchange_terms(places, ints, own, boxes, *acc, last=False):
+def in_hbm(value):
+    return pltpu.with_memory_space_constraint(jnp.asarray(value), pltpu.HBM)
+
+
+def own_term(own):
     lanes = 2 * BOX
-    shape = [jax.ShapeDtypeStruct((BOX, BOX * BOX), F32)]
-    if places[0] == HOME:
-        shape.append(jax.ShapeDtypeStruct((BOX * BOX, lanes), F32))
+    green, table = tables()
+    rows = pltpu.VMEM((BOX * HROW, lanes), F32)
+    shapes = [((BOX, BOX * BOX), F32), ((BOX * BOX, lanes), F32), (green.shape, F32)]
+    shapes += [((2 * lanes, 2 * lanes), BF16)] * 2 + [((BOX, 3 * BOX), BF16)] * 2
+    acc, *shared = pl.pallas_call(
+        alone_kernel,
+        out_shape=[jax.ShapeDtypeStruct(*shape) for shape in shapes],
+        in_specs=[VMEM, HBM, HBM],
+        out_specs=[VMEM] * len(shapes),
+        scratch_shapes=[pltpu.VMEM((BOX * BOX // 2, lanes), F32), rows, rows, pltpu.VMEM(table.shape, F32)]
+        + [pltpu.VMEM((BOX, 3 * BOX // 2), BF16)] * 2
+        + [pltpu.SemaphoreType.DMA((2,))],
+        compiler_params=PARAMS,
+    )(own, in_hbm(table), in_hbm(green))
+    return acc, shared
+
+
+def exchange_terms(places, ints, shared, boxes, acc, last=False):
+    lanes = 2 * BOX
     sink = [pltpu.VMEM((BOX, BOX * BOX), F32), pltpu.SemaphoreType.DMA((BOX // CHUNK,))] if last else []
-    table = tables()
+    rows = pltpu.VMEM((BOX * MROW, lanes), F32)
+    own, *tabs = shared
     return pl.pallas_call(
         functools.partial(kernel, places, last),
-        out_shape=shape,
-        in_specs=[SMEM] * 3 + [VMEM] * (1 + len(boxes)) + [HBM] + [VMEM] * len(acc),
-        out_specs=[HBM if last else VMEM] * len(shape),
-        scratch_shapes=sink
-        + [
-            pltpu.VMEM(((BOX + 1) * ROW + 32, lanes), F32),
-            pltpu.VMEM((BOX * MROW, lanes), F32),
-            pltpu.VMEM((BOX * MROW, lanes), F32),
-            pltpu.VMEM(table.shape, F32),
-            pltpu.VMEM((2 * lanes, 2 * lanes), BF16),
-            pltpu.VMEM((2 * lanes, 2 * lanes), BF16),
-            pltpu.VMEM((BOX, 3 * BOX), BF16),
-            pltpu.VMEM((BOX, 3 * BOX), BF16),
-            pltpu.SemaphoreType.DMA,
-        ],
+        out_shape=jax.ShapeDtypeStruct((BOX, BOX * BOX), F32),
+        in_specs=[SMEM] * 3 + [VMEM] * (2 + len(boxes) + len(tabs)),
+        out_specs=HBM if last else VMEM,
+        scratch_shapes=sink + [pltpu.VMEM(((BOX + 1) * ROW + 32, lanes), F32), rows, rows],
         compiler_params=PARAMS,
-    )(*ints, own, *boxes, table, *acc)
+    )(*ints, own, *boxes, *tabs, acc)
 
 
 def along(value, axis, to):
@@ -354,7 +460,7 @@
             pltpu.SemaphoreType.DMA((3,)),
         ],
         compiler_params=PARAMS,
-    )(ints[1], pair_mask, orbitals[0])
+    )(in_hbm(ints[1]), in_hbm(pair_mask), in_hbm(orbitals[0]))
 
     def inner(i):
         return i ^ 1
@@ -362,16 +468,16 @@
     def outer(i):
         return (i - 1 + 2 * (i % 2)) % size_x
 
+    x_far, x_near = along(own, "dx", outer), along(own, "dx", inner)
+    y_last = along(own, "dy", lambda i: (i + 1) % size_y)
     y_next = along(own, "dy", lambda i: (i - 1) % size_y)
-    y_last = along(own, "dy", lambda i: (i + 1) % size_y)
-    x_near, x_far = along(own, "dx", inner), along(own, "dx", outer)
-    acc, wide = exchange_terms((HOME, HOME), ints, own, (own, own))
-    (acc,) = exchange_terms(((1, 0), (-1, 0)), ints, wide, (x_near, x_far), acc)
+    acc, shared = own_term(own)
+    acc = exchange_terms(((1, 0), (-1, 0)), ints, shared, (x_near, x_far), acc)
     y_next, y_last, acc = lax.optimization_barrier((y_next, y_last, acc))
     corners = [along(v, "dx", to) for to in (inner, outer) for v in (y_next, y_last)]
-    (acc,) = exchange_terms(((0, 1), (0, -1)), ints, wide, (y_next, y_last), acc)
-    (acc,) = exchange_terms(((1, 1), (1, -1)), ints, wide, corners[:2], acc)
-    (acc,) = exchange_terms(((-1, 1), (-1, -1)), ints, wide, corners[2:], acc, last=True)
+    acc = exchange_terms(((0, 1), (0, -1)), ints, shared, (y_next, y_last), acc)
+    acc = exchange_terms(((1, 1), (1, -1)), ints, shared, corners[:2], acc)
+    acc = exchange_terms(((-1, 1), (-1, -1)), ints, shared, corners[2:], acc, last=True)
     return acc[None]
 
 

time: 50.4 us -> 45.9 us (0.911)
  local copies, waits for them, and re-layouts: 4.53 us -> 0.02 us
  waiting for transfers between devices: 0.84 us -> 5.12 us
  Pallas kernels: 32 us -> 27.9 us
    unnamed x14 -> x6, local copies, waits for them, and re-layouts: 4.53 us -> 0.02 us
    pallas_call x5, Pallas kernels: 31.2 us -> 26.8 us  [the longest x4 22.9 us: exchange_terms(): pl.pallas_call(functools.partial(kernel, places, last), out_shape=jax.Sha...]
    ppermute x8, waiting for transfers between devices: 0.84 us -> 5.12 us  [along(): lax.ppermute(value, axis, [(i, to(i)) for i in range(lax.axis_size(axis))])]
  transfers between devices with their start and end apart: 8 -> 8, of which waited for: 1 -> 2; matrix products, arithmetic and copies ran while one was open for 0% -> 0% of each run, Pallas kernels for 48% -> 45%
where the time goes in v5:
time: 45.9 us; the launch traced here: 45.8 us
  Pallas kernels  27.9 us (61%)
  starting transfers between devices  12.5 us (27%)
  waiting for transfers between devices  5.12 us (11%)
    pallas_call x4, Pallas kernels, exchange_terms(): pl.pallas_call(functools.partial(kernel, places, last), out_shape=jax.Sha...  22.9 us
    ppermute x8, starting transfers between devices, along(): lax.ppermute(value, axis, [(i, to(i)) for i in range(lax.axis_size(axis))])  12.5 us
    ppermute x8, waiting for transfers between devices, along(): lax.ppermute(value, axis, [(i, to(i)) for i in range(lax.axis_size(axis))])  5.12 us
    pallas_call x1, Pallas kernels, own_term(): pl.pallas_call(alone_kernel, out_shape=[jax.ShapeDtypeStruct(*shape) for...  3.9 us
    pallas_call x1, Pallas kernels, body(): pl.pallas_call(tail_kernel, out_shape=jax.ShapeDtypeStruct((BOX, BOX * BO...  1.07 us
  transfers between devices with their start and end apart: 8, of which 2 were waited for; matrix products, arithmetic and copies ran while one was open for 0% of the time, Pallas kernels for 45%

profile of v5, /device:TPU:0, one launch (start us, length us, event | category | flops | bytes accessed | tf_op | source)
XLA Modules:
  0.0 45.8 jit_solution(7082516633418722939)
XLA Ops:
  0.0 1.1 %shard_map.64.own_ref = bf16[64,4224]{1,0:T(8,128)(2,1)S(1)} custom-call(s32[2,8]{1,0:T(2,128)} %bitcast.8, s32[8]{0:T(128)} %pair_mask.7, bf16[64,4096]{1,0:T(8,128)(2,1)} %bitcast.13), custom_call_target="tpu_custom_call" | custom-call | tf_op jit(solution)/shard_map/pallas_call | solution.py:452
  1.1 0.0 copy-start
  1.1 0.0 copy-start.1
  1.1 0.0 copy-start.2
  1.1 3.6 %collective-permute-start.3 = (bf16[64,4224]{1,0:T(8,128)(2,1)S(1)}, bf16[64,4224]{1,0:T(8,128)(2,1)S(1)}, u32[]{:S(2)}, u32[]{:S(2)}) collective-permute-start(bf16[64,4224]{1,0:T(8,128)(2,1)S(1)} %shard_map.64.own_ref), channel_id=1, source_target_pairs={{0,112},{16,32},{32,16},{48,64},{64,48},{80,96},{96,80},{112,0},{1... | collective-permute-start | bytes 1622024 | tf_op jit(solution)/shard_map/ppermute | solution.py:446
  4.8 0.0 collective-permute-start.2
  4.8 1.5 %collective-permute-start.1 = (bf16[64,4224]{1,0:T(8,128)(2,1)S(1)}, bf16[64,4224]{1,0:T(8,128)(2,1)S(1)}, u32[]{:S(2)}, u32[]{:S(2)}) collective-permute-start(bf16[64,4224]{1,0:T(8,128)(2,1)S(1)} %shard_map.64.own_ref), channel_id=1, source_target_pairs={{0,1},{1,2},{2,3},{3,4},{4,5},{5,6},{6,7},{7,8},{8,9},{9,10},{10,1... | collective-permute-start | bytes 1622024 | tf_op jit(solution)/shard_map/ppermute | solution.py:446
  6.2 3.9 %collective-permute-start = (bf16[64,4224]{1,0:T(8,128)(2,1)S(1)}, bf16[64,4224]{1,0:T(8,128)(2,1)S(1)}, u32[]{:S(2)}, u32[]{:S(2)}) collective-permute-start(bf16[64,4224]{1,0:T(8,128)(2,1)S(1)} %shard_map.64.own_ref), channel_id=1, source_target_pairs={{0,15},{1,0},{2,1},{3,2},{4,3},{5,4},{6,5},{7,6},{8,7},{9,8},{10,9... | collective-permute-start | bytes 1622024 | tf_op jit(solution)/shard_map/ppermute | solution.py:446
  10.1 3.9 %shard_map.65 = (f32[64,4096]{1,0:T(8,128)S(1)}, f32[4096,128]{1,0:T(8,128)S(1)}, f32[2112,128]{1,0:T(8,128)S(1)}, bf16[256,256]{1,0:T(8,128)(2,1)S(1)}, bf16[25...) custom-call(bf16[64,4224]{1,0:T(8,128)(2,1)S(1)} %shard_map.64.own_ref, ...), custom_call_target="tpu_custom_call" | custom-call | tf_op jit(solution)/shard_map/pallas_call | solution.py:417
  14.0 0.0 collective-permute-done.3.refs_1_
  14.0 0.0 collective-permute-done.2.refs_0_
  14.0 0.0 copy-done
  14.1 0.0 copy-done.1
  14.1 0.0 copy-done.2
  14.1 5.5 %shard_map.66.refs_7_ = f32[64,4096]{1,0:T(8,128)S(1)} custom-call(s32[3,128]{1,0:T(4,128)S(1)} %bitcast.4, s32[2,8]{1,0:T(2,128)S(1)} %bitcast.9, s32[8]{0:T(128)S(1)} %copy-done.2, f32[4096,128]{1,0:T(8,128)S(1)} %get-tuple-element.15.own_ref, bf16[64,4224]{1,0:T(8,128)(2,1)S(1)} %collective-permute-done.2.refs_0_, ...), custom_call_target="tpu_custom_call" | custom-call | tf_op jit(solution)/shard_map/pallas_call | solution.py:435
  19.6 3.3 %collective-permute-done.1.refs_1_ = bf16[64,4224]{1,0:T(8,128)(2,1)S(1)} collective-permute-done((bf16[64,4224]{1,0:T(8,128)(2,1)S(1)}, bf16[64,4224]{1,0:T(8,128)(2,1)S(1)}, u32[]{:S(2)}, u32[]{:S(2)}) %collective-permute-start.1) | collective-permute-done | bytes 540704 | tf_op jit(solution)/shard_map/ppermute | solution.py:446
  22.9 0.0 collective-permute-done.refs_0_
  22.9 0.0 collective-permute-start.6
  22.9 0.5 %collective-permute-start.7 = (bf16[64,4224]{1,0:T(8,128)(2,1)S(1)}, bf16[64,4224]{1,0:T(8,128)(2,1)S(1)}, u32[]{:S(2)}, u32[]{:S(2)}) collective-permute-start(bf16[64,4224]{1,0:T(8,128)(2,1)S(1)} %collective-permute-done.1.refs_1_), channel_id=1, source_target_pairs={{0,16},{16,0},{32,48},{48,32},{64,80},{80,64},{96,112},{112,96},{1... | collective-permute-start | bytes 1622024 | tf_op jit(solution)/shard_map/ppermute | solution.py:446
  23.4 0.3 collective-permute-start.4
  23.7 2.7 %collective-permute-start.5 = (bf16[64,4224]{1,0:T(8,128)(2,1)S(1)}, bf16[64,4224]{1,0:T(8,128)(2,1)S(1)}, u32[]{:S(2)}, u32[]{:S(2)}) collective-permute-start(bf16[64,4224]{1,0:T(8,128)(2,1)S(1)} %collective-permute-done.1.refs_1_), channel_id=1, source_target_pairs={{0,112},{16,32},{32,16},{48,64},{64,48},{80,96},{96,80},{112,0},{1... | collective-permute-start | bytes 1622024 | tf_op jit(solution)/shard_map/ppermute | solution.py:446
  26.4 5.5 %shard_map.67.refs_7_ = f32[64,4096]{1,0:T(8,128)S(1)} custom-call(s32[3,128]{1,0:T(4,128)S(1)} %bitcast.5, s32[2,8]{1,0:T(2,128)S(1)} %bitcast.10, s32[8]{0:T(128)S(1)} %copy-done.2, f32[4096,128]{1,0:T(8,128)S(1)} %get-tuple-element.15.own_ref, bf16[64,4224]{1,0:T(8,128)(2,1)S(1)} %collective-permute-done.refs_0_, ...), custom_call_target="tpu_custom_call" | custom-call | tf_op jit(solution)/shard_map/pallas_call | solution.py:435
  31.9 0.0 collective-permute-done.6.refs_0_
  31.9 0.0 collective-permute-done.7.refs_1_
  31.9 5.5 %shard_map.68.refs_7_ = f32[64,4096]{1,0:T(8,128)S(1)} custom-call(s32[3,128]{1,0:T(4,128)S(1)} %bitcast.6, s32[2,8]{1,0:T(2,128)S(1)} %bitcast.11, s32[8]{0:T(128)S(1)} %copy-done.2, f32[4096,128]{1,0:T(8,128)S(1)} %get-tuple-element.15.own_ref, bf16[64,4224]{1,0:T(8,128)(2,1)S(1)} %collective-permute-done.6.refs_0_, ...), custom_call_target="tpu_custom_call" | custom-call | tf_op jit(solution)/shard_map/pallas_call | solution.py:435
  37.4 0.0 collective-permute-done.4.refs_0_
  37.4 1.8 %collective-permute-done.5.refs_1_ = bf16[64,4224]{1,0:T(8,128)(2,1)S(1)} collective-permute-done((bf16[64,4224]{1,0:T(8,128)(2,1)S(1)}, bf16[64,4224]{1,0:T(8,128)(2,1)S(1)}, u32[]{:S(2)}, u32[]{:S(2)}) %collective-permute-start.5) | collective-permute-done | bytes 540704 | tf_op jit(solution)/shard_map/ppermute | solution.py:446
  39.2 6.4 %shard_map.69 = f32[64,4096]{1,0:T(8,128)} custom-call(s32[3,128]{1,0:T(4,128)S(1)} %bitcast.7, s32[2,8]{1,0:T(2,128)S(1)} %bitcast.12, s32[8]{0:T(128)S(1)} %copy-done.2, f32[4096,128]{1,0:T(8,128)S(1)} %get-tuple-element.15.own_ref, bf16[64,4224]{1,0:T(8,128)(2,1)S(1)} %collective-permute-done.4.refs_0_, ...), custom_call_target="tpu_custom_call" | custom-call | tf_op jit(solution)/shard_map/pallas_call | solution.py:435
Async XLA Ops:
  1.1 13.0 %copy-start = (s32[128,3]{0,1:T(4,128)S(1)}, s32[128,3]{0,1:T(4,128)}, u32[]{:S(2)}) copy-start(s32[128,3]{0,1:T(4,128)} %param.7) | copy-start | bytes 4612
  1.1 13.0 %copy-start.1 = (s32[8,2]{0,1:T(2,128)S(1)}, s32[8,2]{0,1:T(2,128)}, u32[]{:S(2)}) copy-start(s32[8,2]{0,1:T(2,128)} %param.8) | copy-start | bytes 196
  1.1 13.0 %copy-start.2 = (s32[8]{0:T(128)S(1)}, s32[8]{0:T(128)}, u32[]{:S(2)}) copy-start(s32[8]{0:T(128)} %pair_mask.7) | copy-start | bytes 100
  1.1 12.9 %collective-permute-start.3 = (bf16[64,4224]{1,0:T(8,128)(2,1)S(1)}, bf16[64,4224]{1,0:T(8,128)(2,1)S(1)}, u32[]{:S(2)}, u32[]{:S(2)}) collective-permute-start(bf16[64,4224]{1,0:T(8,128)(2,1)S(1)} %shard_map.64.own_ref), channel_id=1, source_target_pairs={{0,112},{16,32},{32,16},{48,64},{64,48},{80,96},{96,80},{112,0},{1... | collective-permute-start | bytes 1622024 | tf_op jit(solution)/shard_map/ppermute | solution.py:446
  4.8 9.3 %collective-permute-start.2 = (bf16[64,4224]{1,0:T(8,128)(2,1)S(1)}, bf16[64,4224]{1,0:T(8,128)(2,1)S(1)}, u32[]{:S(2)}, u32[]{:S(2)}) collective-permute-start(bf16[64,4224]{1,0:T(8,128)(2,1)S(1)} %shard_map.64.own_ref), channel_id=1, source_target_pairs={{0,16},{16,0},{32,48},{48,32},{64,80},{80,64},{96,112},{112,96},{1... | collective-permute-start | bytes 1622024 | tf_op jit(solution)/shard_map/ppermute | solution.py:446
  4.8 18.2 %collective-permute-start.1 = (bf16[64,4224]{1,0:T(8,128)(2,1)S(1)}, bf16[64,4224]{1,0:T(8,128)(2,1)S(1)}, u32[]{:S(2)}, u32[]{:S(2)}) collective-permute-start(bf16[64,4224]{1,0:T(8,128)(2,1)S(1)} %shard_map.64.own_ref), channel_id=1, source_target_pairs={{0,1},{1,2},{2,3},{3,4},{4,5},{5,6},{6,7},{7,8},{8,9},{9,10},{10,1... | collective-permute-start | bytes 1622024 | tf_op jit(solution)/shard_map/ppermute | solution.py:446
  6.2 16.7 %collective-permute-start = (bf16[64,4224]{1,0:T(8,128)(2,1)S(1)}, bf16[64,4224]{1,0:T(8,128)(2,1)S(1)}, u32[]{:S(2)}, u32[]{:S(2)}) collective-permute-start(bf16[64,4224]{1,0:T(8,128)(2,1)S(1)} %shard_map.64.own_ref), channel_id=1, source_target_pairs={{0,15},{1,0},{2,1},{3,2},{4,3},{5,4},{6,5},{7,6},{8,7},{9,8},{10,9... | collective-permute-start | bytes 1622024 | tf_op jit(solution)/shard_map/ppermute | solution.py:446
  22.9 9.0 %collective-permute-start.6 = (bf16[64,4224]{1,0:T(8,128)(2,1)S(1)}, bf16[64,4224]{1,0:T(8,128)(2,1)S(1)}, u32[]{:S(2)}, u32[]{:S(2)}) collective-permute-start(bf16[64,4224]{1,0:T(8,128)(2,1)S(1)} %collective-permute-done.refs_0_), channel_id=1, source_target_pairs={{0,16},{16,0},{32,48},{48,32},{64,80},{80,64},{96,112},{112,96},{1... | collective-permute-start | bytes 1622024 | tf_op jit(solution)/shard_map/ppermute | solution.py:446
  22.9 9.0 %collective-permute-start.7 = (bf16[64,4224]{1,0:T(8,128)(2,1)S(1)}, bf16[64,4224]{1,0:T(8,128)(2,1)S(1)}, u32[]{:S(2)}, u32[]{:S(2)}) collective-permute-start(bf16[64,4224]{1,0:T(8,128)(2,1)S(1)} %collective-permute-done.1.refs_1_), channel_id=1, source_target_pairs={{0,16},{16,0},{32,48},{48,32},{64,80},{80,64},{96,112},{112,96},{1... | collective-permute-start | bytes 1622024 | tf_op jit(solution)/shard_map/ppermute | solution.py:446
  23.4 14.0 %collective-permute-start.4 = (bf16[64,4224]{1,0:T(8,128)(2,1)S(1)}, bf16[64,4224]{1,0:T(8,128)(2,1)S(1)}, u32[]{:S(2)}, u32[]{:S(2)}) collective-permute-start(bf16[64,4224]{1,0:T(8,128)(2,1)S(1)} %collective-permute-done.refs_0_), channel_id=1, source_target_pairs={{0,112},{16,32},{32,16},{48,64},{64,48},{80,96},{96,80},{112,0},{1... | collective-permute-start | bytes 1622024 | tf_op jit(solution)/shard_map/ppermute | solution.py:446
  23.7 15.5 %collective-permute-start.5 = (bf16[64,4224]{1,0:T(8,128)(2,1)S(1)}, bf16[64,4224]{1,0:T(8,128)(2,1)S(1)}, u32[]{:S(2)}, u32[]{:S(2)}) collective-permute-start(bf16[64,4224]{1,0:T(8,128)(2,1)S(1)} %collective-permute-done.1.refs_1_), channel_id=1, source_target_pairs={{0,112},{16,32},{32,16},{48,64},{64,48},{80,96},{96,80},{112,0},{1... | collective-permute-start | bytes 1622024 | tf_op jit(solution)/shard_map/ppermute | solution.py:446

commit v6 on v5

--- a/solution.py
+++ b/solution.py
@@ -16,6 +16,8 @@
 MROW = 72
 HROW = 40
 CHUNK = 16
+WIDE = 32
+SMALL = 8
 THICK = 8
 F32 = jnp.float32
 BF16 = jnp.bfloat16
@@ -307,23 +309,23 @@
             def forward():
                 def first(c):
                     rows = []
-                    for j in range(CHUNK):
-                        y = c * CHUNK + j
+                    for j in range(WIDE):
+                        y = c * WIDE + j
                         rows.append(stacked(*split(partner(y) * own[pl.ds(y * BOX, BOX), :])))
                     return dot(jnp.concatenate(rows, 0), wz[...])
 
                 def second(c, wave):
                     high, rest = split(wave[:, :lanes] + wave[:, lanes:])
-                    for j in range(0, CHUNK, 2):
+                    for j in range(0, WIDE, 2):
                         at = j * BOX
                         h = stacked(high[at : at + BOX], high[at + BOX : at + 2 * BOX])
                         l = stacked(rest[at : at + BOX], rest[at + BOX : at + 2 * BOX])
                         u = dot(rf[...], jnp.concatenate([h, l, h], 0))
-                        y = c * CHUNK + j
+                        y = c * WIDE + j
                         mid[pl.ds(y, BOX, stride=MROW), :] = u[:, :lanes]
                         mid[pl.ds(y + 1, BOX, stride=MROW), :] = u[:, lanes:]
 
-                skewed(BOX // CHUNK, first, second)
+                skewed(BOX // WIDE, first, second)
 
             def green(k):
                 return tab[pl.ds(k * BOX, BOX), :]
@@ -331,22 +333,22 @@
             def middle():
                 def first(c):
                     waves = []
-                    for j in range(0, CHUNK, 2):
-                        base = (c * CHUNK + j) * MROW
+                    for j in range(0, SMALL, 2):
+                        base = (c * SMALL + j) * MROW
                         h, l = split(stacked(mid[pl.ds(base, BOX), :], mid[pl.ds(base + MROW, BOX), :]))
                         waves.append(dot(rf[...], jnp.concatenate([h, l, h], 0)))
                     return waves
 
                 def second(c, waves):
-                    for j in range(0, CHUNK, 2):
-                        k = c * CHUNK + j
+                    for j in range(0, SMALL, 2):
+                        k = c * SMALL + j
                         base = k * MROW
                         h, l = split(waves[j // 2] * stacked(green((k + 1) // 2), green((k + 2) // 2)))
                         v = dot(ri[...], jnp.concatenate([h, l, h], 0))
                         mid2[pl.ds(base, BOX), :] = v[:, :lanes]
                         mid2[pl.ds(base + MROW, BOX), :] = v[:, lanes:]
 
-                skewed(BOX // CHUNK, first, second)
+                skewed(BOX // SMALL, first, second)
 
             def backward():
                 scale = jnp.where(low, weight(a_ref, 0), weight(b_ref, 1))

time: 45.9 us -> 45.8 us (level)
  no operation moved by 1% of the time
where the time goes in v6:
time: 45.8 us; the launch traced here: 45.7 us
  Pallas kernels  27.9 us (61%)
  starting transfers between devices  12.5 us (27%)
  waiting for transfers between devices  5.03 us (11%)
    pallas_call x4, Pallas kernels, exchange_terms(): pl.pallas_call(functools.partial(kernel, places, last), out_shape=jax.Sha...  22.9 us
    ppermute x8, starting transfers between devices, along(): lax.ppermute(value, axis, [(i, to(i)) for i in range(lax.axis_size(axis))])  12.5 us
    ppermute x8, waiting for transfers between devices, along(): lax.ppermute(value, axis, [(i, to(i)) for i in range(lax.axis_size(axis))])  5.03 us
    pallas_call x1, Pallas kernels, own_term(): pl.pallas_call(alone_kernel, out_shape=[jax.ShapeDtypeStruct(*shape) for...  3.9 us
    pallas_call x1, Pallas kernels, body(): pl.pallas_call(tail_kernel, out_shape=jax.ShapeDtypeStruct((BOX, BOX * BO...  1.07 us
  transfers between devices with their start and end apart: 8, of which 2 were waited for; matrix products, arithmetic and copies ran while one was open for 0% of the time, Pallas kernels for 45%

profile of v6, /device:TPU:0, one launch (start us, length us, event | category | flops | bytes accessed | tf_op | source)
XLA Modules:
  0.0 45.7 jit_solution(4210622668350696602)
XLA Ops:
  0.0 1.1 %shard_map.64.own_ref = bf16[64,4224]{1,0:T(8,128)(2,1)S(1)} custom-call(s32[2,8]{1,0:T(2,128)} %bitcast.8, s32[8]{0:T(128)} %pair_mask.7, bf16[64,4096]{1,0:T(8,128)(2,1)} %bitcast.13), custom_call_target="tpu_custom_call" | custom-call | tf_op jit(solution)/shard_map/pallas_call | solution.py:454
  1.1 0.0 copy-start
  1.1 0.0 copy-start.1
  1.1 0.0 copy-start.2
  1.1 3.6 %collective-permute-start.3 = (bf16[64,4224]{1,0:T(8,128)(2,1)S(1)}, bf16[64,4224]{1,0:T(8,128)(2,1)S(1)}, u32[]{:S(2)}, u32[]{:S(2)}) collective-permute-start(bf16[64,4224]{1,0:T(8,128)(2,1)S(1)} %shard_map.64.own_ref), channel_id=1, source_target_pairs={{0,112},{16,32},{32,16},{48,64},{64,48},{80,96},{96,80},{112,0},{1... | collective-permute-start | bytes 1622024 | tf_op jit(solution)/shard_map/ppermute | solution.py:448
  4.8 0.0 collective-permute-start.2
  4.8 1.5 %collective-permute-start.1 = (bf16[64,4224]{1,0:T(8,128)(2,1)S(1)}, bf16[64,4224]{1,0:T(8,128)(2,1)S(1)}, u32[]{:S(2)}, u32[]{:S(2)}) collective-permute-start(bf16[64,4224]{1,0:T(8,128)(2,1)S(1)} %shard_map.64.own_ref), channel_id=1, source_target_pairs={{0,1},{1,2},{2,3},{3,4},{4,5},{5,6},{6,7},{7,8},{8,9},{9,10},{10,1... | collective-permute-start | bytes 1622024 | tf_op jit(solution)/shard_map/ppermute | solution.py:448
  6.2 3.9 %collective-permute-start = (bf16[64,4224]{1,0:T(8,128)(2,1)S(1)}, bf16[64,4224]{1,0:T(8,128)(2,1)S(1)}, u32[]{:S(2)}, u32[]{:S(2)}) collective-permute-start(bf16[64,4224]{1,0:T(8,128)(2,1)S(1)} %shard_map.64.own_ref), channel_id=1, source_target_pairs={{0,15},{1,0},{2,1},{3,2},{4,3},{5,4},{6,5},{7,6},{8,7},{9,8},{10,9... | collective-permute-start | bytes 1622024 | tf_op jit(solution)/shard_map/ppermute | solution.py:448
  10.1 3.9 %shard_map.65 = (f32[64,4096]{1,0:T(8,128)S(1)}, f32[4096,128]{1,0:T(8,128)S(1)}, f32[2112,128]{1,0:T(8,128)S(1)}, bf16[256,256]{1,0:T(8,128)(2,1)S(1)}, bf16[25...) custom-call(bf16[64,4224]{1,0:T(8,128)(2,1)S(1)} %shard_map.64.own_ref, ...), custom_call_target="tpu_custom_call" | custom-call | tf_op jit(solution)/shard_map/pallas_call | solution.py:419
  14.0 0.0 collective-permute-done.3.refs_1_
  14.0 0.0 collective-permute-done.2.refs_0_
  14.0 0.0 copy-done
  14.1 0.0 copy-done.1
  14.1 0.0 copy-done.2
  14.1 5.6 %shard_map.66.refs_7_ = f32[64,4096]{1,0:T(8,128)S(1)} custom-call(s32[3,128]{1,0:T(4,128)S(1)} %bitcast.4, s32[2,8]{1,0:T(2,128)S(1)} %bitcast.9, s32[8]{0:T(128)S(1)} %copy-done.2, f32[4096,128]{1,0:T(8,128)S(1)} %get-tuple-element.15.own_ref, bf16[64,4224]{1,0:T(8,128)(2,1)S(1)} %collective-permute-done.2.refs_0_, ...), custom_call_target="tpu_custom_call" | custom-call | tf_op jit(solution)/shard_map/pallas_call | solution.py:437
  19.7 3.2 %collective-permute-done.1.refs_1_ = bf16[64,4224]{1,0:T(8,128)(2,1)S(1)} collective-permute-done((bf16[64,4224]{1,0:T(8,128)(2,1)S(1)}, bf16[64,4224]{1,0:T(8,128)(2,1)S(1)}, u32[]{:S(2)}, u32[]{:S(2)}) %collective-permute-start.1) | collective-permute-done | bytes 540704 | tf_op jit(solution)/shard_map/ppermute | solution.py:448
  22.9 0.0 collective-permute-done.refs_0_
  22.9 0.0 collective-permute-start.6
  22.9 0.5 %collective-permute-start.7 = (bf16[64,4224]{1,0:T(8,128)(2,1)S(1)}, bf16[64,4224]{1,0:T(8,128)(2,1)S(1)}, u32[]{:S(2)}, u32[]{:S(2)}) collective-permute-start(bf16[64,4224]{1,0:T(8,128)(2,1)S(1)} %collective-permute-done.1.refs_1_), channel_id=1, source_target_pairs={{0,16},{16,0},{32,48},{48,32},{64,80},{80,64},{96,112},{112,96},{1... | collective-permute-start | bytes 1622024 | tf_op jit(solution)/shard_map/ppermute | solution.py:448
  23.4 0.3 collective-permute-start.4
  23.7 2.7 %collective-permute-start.5 = (bf16[64,4224]{1,0:T(8,128)(2,1)S(1)}, bf16[64,4224]{1,0:T(8,128)(2,1)S(1)}, u32[]{:S(2)}, u32[]{:S(2)}) collective-permute-start(bf16[64,4224]{1,0:T(8,128)(2,1)S(1)} %collective-permute-done.1.refs_1_), channel_id=1, source_target_pairs={{0,112},{16,32},{32,16},{48,64},{64,48},{80,96},{96,80},{112,0},{1... | collective-permute-start | bytes 1622024 | tf_op jit(solution)/shard_map/ppermute | solution.py:448
  26.4 5.5 %shard_map.67.refs_7_ = f32[64,4096]{1,0:T(8,128)S(1)} custom-call(s32[3,128]{1,0:T(4,128)S(1)} %bitcast.5, s32[2,8]{1,0:T(2,128)S(1)} %bitcast.10, s32[8]{0:T(128)S(1)} %copy-done.2, f32[4096,128]{1,0:T(8,128)S(1)} %get-tuple-element.15.own_ref, bf16[64,4224]{1,0:T(8,128)(2,1)S(1)} %collective-permute-done.refs_0_, ...), custom_call_target="tpu_custom_call" | custom-call | tf_op jit(solution)/shard_map/pallas_call | solution.py:437
  31.9 0.0 collective-permute-done.6.refs_0_
  31.9 0.0 collective-permute-done.7.refs_1_
  31.9 5.5 %shard_map.68.refs_7_ = f32[64,4096]{1,0:T(8,128)S(1)} custom-call(s32[3,128]{1,0:T(4,128)S(1)} %bitcast.6, s32[2,8]{1,0:T(2,128)S(1)} %bitcast.11, s32[8]{0:T(128)S(1)} %copy-done.2, f32[4096,128]{1,0:T(8,128)S(1)} %get-tuple-element.15.own_ref, bf16[64,4224]{1,0:T(8,128)(2,1)S(1)} %collective-permute-done.6.refs_0_, ...), custom_call_target="tpu_custom_call" | custom-call | tf_op jit(solution)/shard_map/pallas_call | solution.py:437
  37.4 0.0 collective-permute-done.4.refs_0_
  37.4 1.8 %collective-permute-done.5.refs_1_ = bf16[64,4224]{1,0:T(8,128)(2,1)S(1)} collective-permute-done((bf16[64,4224]{1,0:T(8,128)(2,1)S(1)}, bf16[64,4224]{1,0:T(8,128)(2,1)S(1)}, u32[]{:S(2)}, u32[]{:S(2)}) %collective-permute-start.5) | collective-permute-done | bytes 540704 | tf_op jit(solution)/shard_map/ppermute | solution.py:448
  39.2 6.3 %shard_map.69 = f32[64,4096]{1,0:T(8,128)} custom-call(s32[3,128]{1,0:T(4,128)S(1)} %bitcast.7, s32[2,8]{1,0:T(2,128)S(1)} %bitcast.12, s32[8]{0:T(128)S(1)} %copy-done.2, f32[4096,128]{1,0:T(8,128)S(1)} %get-tuple-element.15.own_ref, bf16[64,4224]{1,0:T(8,128)(2,1)S(1)} %collective-permute-done.4.refs_0_, ...), custom_call_target="tpu_custom_call" | custom-call | tf_op jit(solution)/shard_map/pallas_call | solution.py:437
Async XLA Ops:
  1.1 13.0 %copy-start = (s32[128,3]{0,1:T(4,128)S(1)}, s32[128,3]{0,1:T(4,128)}, u32[]{:S(2)}) copy-start(s32[128,3]{0,1:T(4,128)} %param.7) | copy-start | bytes 4612
  1.1 13.0 %copy-start.1 = (s32[8,2]{0,1:T(2,128)S(1)}, s32[8,2]{0,1:T(2,128)}, u32[]{:S(2)}) copy-start(s32[8,2]{0,1:T(2,128)} %param.8) | copy-start | bytes 196
  1.1 13.0 %copy-start.2 = (s32[8]{0:T(128)S(1)}, s32[8]{0:T(128)}, u32[]{:S(2)}) copy-start(s32[8]{0:T(128)} %pair_mask.7) | copy-start | bytes 100
  1.1 12.9 %collective-permute-start.3 = (bf16[64,4224]{1,0:T(8,128)(2,1)S(1)}, bf16[64,4224]{1,0:T(8,128)(2,1)S(1)}, u32[]{:S(2)}, u32[]{:S(2)}) collective-permute-start(bf16[64,4224]{1,0:T(8,128)(2,1)S(1)} %shard_map.64.own_ref), channel_id=1, source_target_pairs={{0,112},{16,32},{32,16},{48,64},{64,48},{80,96},{96,80},{112,0},{1... | collective-permute-start | bytes 1622024 | tf_op jit(solution)/shard_map/ppermute | solution.py:448
  4.8 9.3 %collective-permute-start.2 = (bf16[64,4224]{1,0:T(8,128)(2,1)S(1)}, bf16[64,4224]{1,0:T(8,128)(2,1)S(1)}, u32[]{:S(2)}, u32[]{:S(2)}) collective-permute-start(bf16[64,4224]{1,0:T(8,128)(2,1)S(1)} %shard_map.64.own_ref), channel_id=1, source_target_pairs={{0,16},{16,0},{32,48},{48,32},{64,80},{80,64},{96,112},{112,96},{1... | collective-permute-start | bytes 1622024 | tf_op jit(solution)/shard_map/ppermute | solution.py:448
  4.8 18.2 %collective-permute-start.1 = (bf16[64,4224]{1,0:T(8,128)(2,1)S(1)}, bf16[64,4224]{1,0:T(8,128)(2,1)S(1)}, u32[]{:S(2)}, u32[]{:S(2)}) collective-permute-start(bf16[64,4224]{1,0:T(8,128)(2,1)S(1)} %shard_map.64.own_ref), channel_id=1, source_target_pairs={{0,1},{1,2},{2,3},{3,4},{4,5},{5,6},{6,7},{7,8},{8,9},{9,10},{10,1... | collective-permute-start | bytes 1622024 | tf_op jit(solution)/shard_map/ppermute | solution.py:448
  6.2 16.7 %collective-permute-start = (bf16[64,4224]{1,0:T(8,128)(2,1)S(1)}, bf16[64,4224]{1,0:T(8,128)(2,1)S(1)}, u32[]{:S(2)}, u32[]{:S(2)}) collective-permute-start(bf16[64,4224]{1,0:T(8,128)(2,1)S(1)} %shard_map.64.own_ref), channel_id=1, source_target_pairs={{0,15},{1,0},{2,1},{3,2},{4,3},{5,4},{6,5},{7,6},{8,7},{9,8},{10,9... | collective-permute-start | bytes 1622024 | tf_op jit(solution)/shard_map/ppermute | solution.py:448
  22.9 9.0 %collective-permute-start.6 = (bf16[64,4224]{1,0:T(8,128)(2,1)S(1)}, bf16[64,4224]{1,0:T(8,128)(2,1)S(1)}, u32[]{:S(2)}, u32[]{:S(2)}) collective-permute-start(bf16[64,4224]{1,0:T(8,128)(2,1)S(1)} %collective-permute-done.refs_0_), channel_id=1, source_target_pairs={{0,16},{16,0},{32,48},{48,32},{64,80},{80,64},{96,112},{112,96},{1... | collective-permute-start | bytes 1622024 | tf_op jit(solution)/shard_map/ppermute | solution.py:448
  22.9 9.0 %collective-permute-start.7 = (bf16[64,4224]{1,0:T(8,128)(2,1)S(1)}, bf16[64,4224]{1,0:T(8,128)(2,1)S(1)}, u32[]{:S(2)}, u32[]{:S(2)}) collective-permute-start(bf16[64,4224]{1,0:T(8,128)(2,1)S(1)} %collective-permute-done.1.refs_1_), channel_id=1, source_target_pairs={{0,16},{16,0},{32,48},{48,32},{64,80},{80,64},{96,112},{112,96},{1... | collective-permute-start | bytes 1622024 | tf_op jit(solution)/shard_map/ppermute | solution.py:448
  23.4 14.0 %collective-permute-start.4 = (bf16[64,4224]{1,0:T(8,128)(2,1)S(1)}, bf16[64,4224]{1,0:T(8,128)(2,1)S(1)}, u32[]{:S(2)}, u32[]{:S(2)}) collective-permute-start(bf16[64,4224]{1,0:T(8,128)(2,1)S(1)} %collective-permute-done.refs_0_), channel_id=1, source_target_pairs={{0,112},{16,32},{32,16},{48,64},{64,48},{80,96},{96,80},{112,0},{1... | collective-permute-start | bytes 1622024 | tf_op jit(solution)/shard_map/ppermute | solution.py:448
  23.7 15.5 %collective-permute-start.5 = (bf16[64,4224]{1,0:T(8,128)(2,1)S(1)}, bf16[64,4224]{1,0:T(8,128)(2,1)S(1)}, u32[]{:S(2)}, u32[]{:S(2)}) collective-permute-start(bf16[64,4224]{1,0:T(8,128)(2,1)S(1)} %collective-permute-done.1.refs_1_), channel_id=1, source_target_pairs={{0,112},{16,32},{32,16},{48,64},{64,48},{80,96},{96,80},{112,0},{1... | collective-permute-start | bytes 1622024 | tf_op jit(solution)/shard_map/ppermute | solution.py:448
